TPU v7x, 256 devices: a whole 4x4x8 slice. The times are simulated.
256 devices in a mesh: blk: 8 (over x_hi, y), dp: 32 (over x_lo, z, core).
Axes of the slice: x: 4 (x_hi: 2, x_lo: 2; x = x_hi * 2 + x_lo), y: 4, z: 8, core: 2. Of those that a mesh axis runs over, the one named last changes fastest.
Arguments:
- image_feats: bfloat16 [32, 1024, 1152], P('dp', 'blk'), may hold values from -6 to 6
- text_feats: bfloat16 [32, 1024, 1152], P('dp', 'blk'), may hold values from -6 to 6
- image_proj: bfloat16 [1152, 1152], replicated, may hold values from -0.1875 to 0.1875
- text_proj: bfloat16 [1152, 1152], replicated, may hold values from -0.1875 to 0.1875
- logit_scale: float32 [1], replicated, may hold values from 4 to 16
- logit_bias: float32 [1], replicated, may hold values from -6 to -2
Outputs:
- group_loss: float32 [32], P('dp')
- grad_image_proj: float32 [1152, 1152], P('dp')
- grad_text_proj: float32 [1152, 1152], P('dp')
- image_emb_grad: bfloat16 [32, 1024, 1152], P('dp', 'blk')
- text_emb_grad: bfloat16 [32, 1024, 1152], P('dp', 'blk')
All inputs are finite; a program needn't handle non-finite values.
Results may differ from a plain program's by a relative error of at most 0.022.
Values may be sent and summed in bfloat16 or wider, within the bound.
No kernel may reach another device: no remote copies, remote signals or barrier semaphores. Data moves between devices by JAX's collectives and lax.ppermute only.
A program may use at most 128 MiB of HBM per device.

v0:
```python
import jax
import jax.numpy as jnp
from jax import lax
from jax.sharding import PartitionSpec as P

epsilon = 1e-06
contract_rows = (((0,), (0,)), ((), ()))
contract_cols = (((1,), (1,)), ((), ()))


def unit_rows(features, weight):
    projected = jnp.dot(features, weight, preferred_element_type=jnp.float32)
    inverse = lax.rsqrt(jnp.sum(projected * projected, axis=-1, keepdims=True) + epsilon)
    return (projected * inverse, inverse)


def back_unit(gradient, unit_vec, inverse):
    radial = jnp.sum(unit_vec * gradient, axis=-1, keepdims=True)
    return ((gradient - unit_vec * radial) * inverse).astype(jnp.bfloat16)


def on_device(image_feats, text_feats, image_proj, text_proj, logit_scale, logit_bias):
    image_rows = image_feats[0]
    text_rows = text_feats[0]
    row_count = image_rows.shape[0]
    embed_width = image_proj.shape[1]
    cycle_size = lax.axis_size("blk")
    group_rows = row_count * cycle_size
    logit_mult = logit_scale[0]
    offset = logit_bias[0]
    image_unit, image_inv = unit_rows(image_rows, image_proj)
    text_unit, text_inv = unit_rows(text_rows, text_proj)
    image_emb = image_unit.astype(jnp.bfloat16)
    text_emb = text_unit.astype(jnp.bfloat16)
    own_anchor = lax.axis_index("blk") * row_count
    text_block = lax.all_gather(text_emb, "blk", axis=0, tiled=True)
    logits = (
        logit_mult
        * lax.dot_general(image_emb, text_block, contract_cols, preferred_element_type=jnp.float32)
        + offset
    )
    image_ids = own_anchor + lax.broadcasted_iota(jnp.int32, logits.shape, 0)
    text_ids = lax.broadcasted_iota(jnp.int32, logits.shape, 1)
    target = jnp.where(image_ids == text_ids, 1.0, -1.0).astype(jnp.float32)
    loss_term = -jnp.sum(jax.nn.log_sigmoid(target * logits)) / group_rows
    slopes = (-target * jax.nn.sigmoid(-target * logits)).astype(jnp.bfloat16)
    image_part = jnp.dot(slopes, text_block, preferred_element_type=jnp.float32)
    text_part = lax.dot_general(
        slopes, image_emb, contract_rows, preferred_element_type=jnp.float32
    )
    loss_term, image_part, text_part = (loss_term, image_part, text_part)
    text_sum = lax.psum_scatter(text_part, "blk", scatter_dimension=0, tiled=True)
    image_grad = logit_mult * image_part
    text_grad = logit_mult * text_sum
    image_back = back_unit(image_grad, image_unit, image_inv)
    text_back = back_unit(text_grad, text_unit, text_inv)
    image_term = lax.dot_general(
        image_rows, image_back, contract_rows, preferred_element_type=jnp.float32
    )
    text_term = lax.dot_general(
        text_rows, text_back, contract_rows, preferred_element_type=jnp.float32
    )
    summed = lax.psum_scatter(
        jnp.concatenate([image_term, text_term], axis=1).astype(jnp.bfloat16),
        "dp",
        scatter_dimension=0,
        tiled=True,
    ).astype(jnp.float32)
    weight_grads, loss_total = lax.psum((summed, loss_term), "blk")
    return (
        loss_total.reshape(1),
        weight_grads[:, :embed_width],
        weight_grads[:, embed_width:],
        image_grad.astype(jnp.bfloat16)[None],
        text_grad.astype(jnp.bfloat16)[None],
    )


def solution(mesh):
    in_specs = (P("dp", "blk", None), P("dp", "blk", None), P(), P(), P(), P())
    out_specs = (P("dp"), P("dp", None), P("dp", None), P("dp", "blk", None), P("dp", "blk", None))
    return jax.shard_map(
        on_device, mesh=mesh, in_specs=in_specs, out_specs=out_specs, check_vma=False
    )
```

profile of v0, /device:TPU:32, one launch (start us, length us, event | category | flops | bytes accessed | tf_op | source)
XLA Modules:
  0.0 524.7 jit_solution(15600574963741895512)
XLA Ops:
  7.2 0.0 all-gather.2.cloned.1.call-start
  7.2 1.7 copy-done
  8.9 1.6 multiply_reduce_fusion.2
  10.6 0.8 copy-done.2
  11.4 0.8 multiply_convert_fusion.3
  12.2 0.0 all-gather.2.cloned.1.call-update
  12.2 0.0 reduce-scatter.3.cloned.1.call-start
  13.6 2.4 multiply_reduce_fusion.3
  16.0 60.0 %all-gather.2.cloned.1.call-done = bf16[1024,1152]{1,0:T(8,128)(2,1)} async-done(((bf16[128,1152]{1,0:T(8,128)(2,1)}), bf16[1024,1152]{1,0:T(8,128)(2,1)}) %all-gather.2.cloned.1.call-update) | async-done | bytes 2359312 | tf_op jit(solution)/shard_map/all_gather | solution.py:36
  76.1 3.4 fusion.10
  79.5 0.8 copy-done.4
  80.3 3.1 fusion.24
  83.4 0.0 reduce-scatter.3.cloned.1.call-update
  83.5 0.0 all-reduce.6.cloned.1.call-start
  83.5 2.5 convolution_multiply_fusion
  86.0 0.9 convert_bitcast_fusion
  86.9 2.5 fusion
  89.4 85.0 %reduce-scatter.3.cloned.1.call-done = f32[128,1152]{1,0:T(8,128)} async-done(((f32[1024,1152]{1,0:T(8,128)}), f32[128,1152]{1,0:T(8,128)}) %reduce-scatter.3.cloned.1.call-update) | async-done | bytes 589840 | tf_op jit(solution)/shard_map/reduce_scatter | solution.py:52
  174.4 2.2 fusion.12
  176.6 2.3 fusion.1
  178.9 2.8 pad_maximum_fusion
  181.7 0.0 all-reduce.6.cloned.1.call-update
  181.7 0.0 all-reduce.4.cloned.1.call-start
  181.7 0.6 copy-done.5
  182.3 0.6 dynamic-slice
  183.6 232.1 %all-reduce.6.cloned.1.call-done = bf16[1152,2304]{0,1:T(8,128)(2,1)} async-done(((bf16[1152,2304]{0,1:T(8,128)(2,1)}), bf16[1152,2304]{0,1:T(8,128)(2,1)}) %all-reduce.6.cloned.1.call-update) | async-done | bytes 5308432
  415.7 2.5 dynamic-slice_convert_fusion
  418.9 24.9 %psum.14 = f32[1]{0:T(128)} all-reduce(f32[1]{0:T(128)} %bitcast.4), channel_id=1, replica_groups=mesh['blk'=8,'dp'=32] {'blk'}, use_global_device_ids=true, to_apply=%region_3.4 | all-reduce | flops 1 | bytes 8 | tf_op jit(solution)/shard_map/psum | solution.py:69
  443.8 69.3 %all-reduce.4.cloned.1.call-done = f32[36,2304]{0,1:T(8,128)} async-done(((f32[36,2304]{0,1:T(8,128)}), f32[36,2304]{0,1:T(8,128)}) %all-reduce.4.cloned.1.call-update) | async-done | bytes 331792 | tf_op jit(solution)/shard_map/psum | solution.py:69
  513.1 2.2 fusion.27
  515.3 2.0 copy.13
  517.3 0.9 copy.14
  (12 shorter events, 0.1 us)
Async XLA Ops:
  7.2 1.8 copy-start
  7.2 6.4 %copy-start.3 = (bf16[1,128,1152]{2,1,0:T(8,128)(2,1)S(1)}, bf16[1,128,1152]{2,1,0:T(8,128)(2,1)}, u32[]{:S(2)}) copy-start(bf16[1,128,1152]{2,1,0:T(8,128)(2,1)} %param.6) | copy-start | bytes 884740
  7.2 68.9 %all-gather.2.cloned.1.call-start = ((), (), s32[]{:S(2)}) async-start(), calls=%async_computation.1 | async-start | bytes 2654208 | tf_op jit(solution)/shard_map/all_gather | solution.py:36
  10.6 0.8 copy-start.2
  12.2 162.2 %reduce-scatter.3.cloned.1.call-start = ((), (), s32[]{:S(2)}) async-start(), calls=%async_computation.2 | async-start | bytes 5308416 | tf_op jit(solution)/shard_map/reduce_scatter | solution.py:52
  79.5 0.8 copy-start.4
  83.5 332.3 %all-reduce.6.cloned.1.call-start = ((), (), s32[]{:S(2)}) async-start(), calls=%async_computation.4 | async-start | bytes 10616832
  174.4 4.5 copy-start.1
  181.7 0.7 copy-start.5
  181.7 331.4 %all-reduce.4.cloned.1.call-start = ((), (), s32[]{:S(2)}) async-start(), calls=%async_computation.3 | async-start | bytes 2359296 | tf_op jit(solution)/shard_map/psum | solution.py:69
Sparse Core Ops, SparseCore 0:
  12.3 63.6 all-gather.1
  83.6 90.8 reduce-scatter.2
  181.8 233.8 all-reduce.5
  418.4 94.6 all-reduce.3
where the time goes:
time: 525 us
  waiting for transfers between devices  447 us (85%)
  blocking collectives  24.9 us (5%)
  matrix products  17.9 us (3%)
  between operations  16.5 us (3%)
  local copies, waits for them, and re-layouts  9.54 us (2%)
  other arithmetic  9.16 us (2%)
    unnamed x5, waiting for transfers between devices  232 us
    reduce_scatter x1, waiting for transfers between devices, on_device(): lax.psum_scatter(text_part, 'blk', scatter_dimension=0, tiled=True)  85 us
    psum x1, waiting for transfers between devices, on_device(): weight_grads, loss_total = lax.psum((summed, loss_term), 'blk')  69.3 us
    all_gather x1, waiting for transfers between devices, on_device(): text_block = lax.all_gather(text_emb, 'blk', axis=0, tiled=True)  60 us
    psum x1, blocking collectives, on_device(): weight_grads, loss_total = lax.psum((summed, loss_term), 'blk')  24.9 us
  transfers between devices with their start and end apart: 4, of which 4 were waited for; matrix products, arithmetic and copies ran while one was open for 2% of the time, Pallas kernels for 0%

commit v1 on v0

v1 whole, which is shorter than its diff:
```python
import jax
import jax.numpy as jnp
from jax import lax
from jax.sharding import Mesh, PartitionSpec as P

epsilon = 1e-06
contract_rows = (((0,), (0,)), ((), ()))
contract_cols = (((1,), (1,)), ((), ()))
AXES = ("xh", "y", "xl", "z", "c")
XH, Y, XL, Z, C = 2, 4, 2, 8, 2
f32, bf16 = jnp.float32, jnp.bfloat16


def trade(x):
    return lax.ppermute(x, ("xh", "c"), [(1, 2), (2, 1)])


def other_core(x):
    return lax.ppermute(x, "c", [(0, 1), (1, 0)])


def from_y(x, k):
    return lax.ppermute(x, "y", [(i, (i + k) % Y) for i in range(Y)])


def gather(x, keep):
    own = jnp.where(keep, x, trade(x))
    return jnp.concatenate([own, from_y(own, 1), from_y(own, -1), from_y(own, 2)], axis=0)


def project(features, weight):
    pre = jnp.dot(features, weight, preferred_element_type=f32)
    inverse = lax.rsqrt(jnp.sum(pre * pre, axis=-1, keepdims=True) + epsilon)
    unit = pre * inverse
    return unit, inverse, unit.astype(bf16)


def on_device(image_feats, text_feats, image_proj, text_proj, logit_scale, logit_bias):
    c, y = lax.axis_index("c"), lax.axis_index("y")
    keep = lax.axis_index("xh") == c
    scale, bias = logit_scale[0], logit_bias[0]
    width = image_proj.shape[1]
    cols = width // Y
    rows = image_feats.shape[1] * Y
    own_rows = image_feats.shape[1]

    text = gather(text_feats[0], keep)
    image = gather(image_feats[0], keep)
    text_unit, text_inv, text_emb = project(text, text_proj)
    text_other = other_core(text_emb)
    image_unit, image_inv, image_emb = project(image, image_proj)
    text_all = jnp.concatenate([text_emb, text_other], axis=0)

    cosine = lax.dot_general(image_emb, text_all, contract_cols, preferred_element_type=f32)
    logits = scale * cosine + bias
    target = jnp.where(
        lax.broadcasted_iota(jnp.int32, logits.shape, 0)
        == lax.broadcasted_iota(jnp.int32, logits.shape, 1),
        1.0,
        -1.0,
    ).astype(f32)
    loss = -jnp.sum(jax.nn.log_sigmoid(target * logits)) / (rows * C)
    slopes = (-target * jax.nn.sigmoid(-target * logits)).astype(bf16)
    weighted = slopes.astype(f32) * cosine
    image_radial = scale * jnp.sum(weighted, axis=1, keepdims=True)
    text_radial = scale * jnp.sum(weighted, axis=0)[:, None]

    def cut(x):
        return lax.dynamic_slice_in_dim(x, y * cols, cols, axis=1)

    image_grad = scale * jnp.dot(slopes, cut(text_all), preferred_element_type=f32)
    text_part = scale * lax.dot_general(
        slopes, cut(image_emb), contract_rows, preferred_element_type=f32
    )
    text_grad = text_part[:rows] + other_core(text_part[rows:])
    text_radial = text_radial[:rows] + other_core(text_radial[rows:])
    image_back = ((image_grad - cut(image_unit) * image_radial) * image_inv).astype(bf16)
    text_back = ((text_grad - cut(text_unit) * text_radial) * text_inv).astype(bf16)
    image_term = lax.dot_general(image, image_back, contract_rows, preferred_element_type=f32)
    text_term = lax.dot_general(text, text_back, contract_rows, preferred_element_type=f32)
    term = jnp.concatenate([image_term, text_term], axis=1)
    term = term.reshape(XL * Z, C, -1, 2 * cols)
    give = lax.dynamic_index_in_dim(term, 1 - c, axis=1, keepdims=False).astype(bf16)
    mine = lax.dynamic_index_in_dim(term, c, axis=1, keepdims=False)
    mine = (mine + other_core(give).astype(f32)).astype(bf16)
    got = lax.all_to_all(mine, ("xl", "z"), 0, 0)
    summed = jnp.sum(got.astype(f32), axis=0).astype(bf16)
    spread = lax.all_to_all(
        jnp.broadcast_to(summed[None], (XH * Y,) + summed.shape), ("xh", "y"), 0, 0
    )
    spread = spread.astype(f32)
    spread = spread[:Y] + spread[Y:]
    grads = [
        jnp.concatenate([spread[i, :, s * cols : (s + 1) * cols] for i in range(Y)], axis=1)
        for s in range(2)
    ]

    image_out = scale * jnp.dot(slopes[:own_rows], text_all, preferred_element_type=f32)
    parts = [
        lax.dot_general(
            slopes[:, i : i + own_rows], image_emb, contract_rows, preferred_element_type=f32
        )
        for i in (0, rows)
    ]
    text_out = scale * (parts[0] + other_core(parts[1]))
    outs = jnp.concatenate([image_out.astype(bf16), text_out.astype(bf16)], axis=0)
    loss = jnp.broadcast_to(loss, (8, 128))
    loss = loss + other_core(loss)
    outs = jnp.where(keep, outs, trade(outs))
    loss = jnp.where(keep, loss, trade(loss))
    return (
        loss[0, :1],
        grads[0],
        grads[1],
        outs[:own_rows][None],
        outs[own_rows:][None],
    )


def solution(mesh):
    fine = Mesh(mesh.devices.reshape(XH, Y, XL, Z, C), AXES)
    dp, blk = ("xl", "z", "c"), ("xh", "y")
    in_specs = (P(dp, blk, None), P(dp, blk, None), P(), P(), P(), P())
    out_specs = (P(dp), P(dp, None), P(dp, None), P(dp, blk, None), P(dp, blk, None))
    return jax.shard_map(
        on_device, mesh=fine, in_specs=in_specs, out_specs=out_specs, check_vma=False
    )
```

time: 525 us -> 129 us (0.25)
  waiting for transfers between devices: 447 us -> 29.4 us
  starting transfers between devices: 0.16 us -> 40.1 us
  blocking collectives: 24.9 us -> 0 us
  between operations: 16.5 us -> 2.95 us
  local copies, waits for them, and re-layouts: 9.54 us -> 20.5 us
  matrix products: 17.9 us -> 23.7 us
    unnamed x5 -> x0, waiting for transfers between devices: 232 us -> none
    reduce_scatter x1 -> x0, waiting for transfers between devices: 85 us -> none  [on_device(): lax.psum_scatter(text_part, 'blk', scatter_dimension=0, tiled=True)]
    psum x1 -> x0, waiting for transfers between devices: 69.3 us -> none  [on_device(): weight_grads, loss_total = lax.psum((summed, loss_term), 'blk')]
    all_gather x1 -> x0, waiting for transfers between devices: 60 us -> none  [on_device(): text_block = lax.all_gather(text_emb, 'blk', axis=0, tiled=True)]
    ppermute x0 -> x16, starting transfers between devices: none -> 25 us  [the longest x6 12.4 us: other_core(): return lax.ppermute(x, 'c', [(0, 1), (1, 0)])]
    psum x1 -> x0, blocking collectives: 24.9 us -> none  [on_device(): weight_grads, loss_total = lax.psum((summed, loss_term), 'blk')]
    all_to_all x0 -> x2, waiting for transfers between devices: none -> 19.3 us  [the longest x1 11.3 us: on_device(): got = lax.all_to_all(mine, ('xl', 'z'), 0, 0)]
    all_to_all x0 -> x2, starting transfers between devices: none -> 15.1 us  [the longest x1 9.51 us: on_device(): got = lax.all_to_all(mine, ('xl', 'z'), 0, 0)]
  transfers between devices with their start and end apart: 4 -> 18, of which waited for: 4 -> 5; matrix products, arithmetic and copies ran while one was open for 2% -> 34% of each run, Pallas kernels for 0% -> 0%
where the time goes in v1:
time: 129 us; the launch traced here: 128 us
  starting transfers between devices  40.1 us (31%)
  waiting for transfers between devices  29.4 us (23%)
  matrix products  23.7 us (18%)
  local copies, waits for them, and re-layouts  20.5 us (16%)
  other arithmetic  11.7 us (9%)
  between operations  2.95 us (2%)
    ppermute x6, starting transfers between devices, other_core(): return lax.ppermute(x, 'c', [(0, 1), (1, 0)])  12.4 us
    all_to_all x1, waiting for transfers between devices, on_device(): got = lax.all_to_all(mine, ('xl', 'z'), 0, 0)  11.3 us
    all_to_all x1, starting transfers between devices, on_device(): got = lax.all_to_all(mine, ('xl', 'z'), 0, 0)  9.51 us
    ppermute x6, waiting for transfers between devices, from_y(): return lax.ppermute(x, 'y', [(i, (i + k) % Y) for i in range(Y)])  9.23 us
    ppermute x6, starting transfers between devices, from_y(): return lax.ppermute(x, 'y', [(i, (i + k) % Y) for i in range(Y)])  8.97 us
    all_to_all x1, waiting for transfers between devices, on_device(): lax.all_to_all(jnp.broadcast_to(summed[None], (XH * Y,) + summed.shape),...  8.04 us
    dot_general x1, matrix products, on_device(): lax.dot_general(image_emb, text_all, contract_cols, preferred_element_typ...  5.63 us
    all_to_all x1, starting transfers between devices, on_device(): lax.all_to_all(jnp.broadcast_to(summed[None], (XH * Y,) + summed.shape),...  5.57 us
  transfers between devices with their start and end apart: 18, of which 5 were waited for; matrix products, arithmetic and copies ran while one was open for 34% of the time, Pallas kernels for 0%

profile of v1, /device:TPU:32, one launch (start us, length us, event | category | flops | bytes accessed | tf_op | source)
XLA Modules:
  0.0 128.5 jit_solution(3679911816792966617)
XLA Ops:
  4.5 3.3 %collective-permute-start.7 = (bf16[128,1152]{1,0:T(8,128)(2,1)S(1)}, bf16[128,1152]{1,0:T(8,128)(2,1)S(1)}, u32[]{:S(2)}, u32[]{:S(2)}) collective-permute-start(bf16[128,1152]{1,0:T(8,128)(2,1)S(1)} %broadcast_select_fusion.1), channel_id=1, source_target_pairs={{0,64},{32,96},{64,0},{96,32},{1,65},{33,97},{65,1},{97,33},{2,66}... | collective-permute-start | bytes 884744 | tf_op jit(solution)/shard_map/ppermute | solution.py:23
  11.6 2.6 %collective-permute-start.2 = (bf16[128,1152]{1,0:T(8,128)(2,1)S(1)}, bf16[128,1152]{1,0:T(8,128)(2,1)S(1)}, u32[]{:S(2)}, u32[]{:S(2)}) collective-permute-start(bf16[128,1152]{1,0:T(8,128)(2,1)S(1)} %broadcast_select_fusion.2), channel_id=1, source_target_pairs={{0,96},{32,0},{64,32},{96,64},{1,97},{33,1},{65,33},{97,65},{2,98}... | collective-permute-start | bytes 884744 | tf_op jit(solution)/shard_map/ppermute | solution.py:23
  14.5 1.9 %collective-permute-done.6 = bf16[128,1152]{1,0:T(8,128)(2,1)S(1)} collective-permute-done((bf16[128,1152]{1,0:T(8,128)(2,1)S(1)}, bf16[128,1152]{1,0:T(8,128)(2,1)S(1)}, u32[]{:S(2)}, u32[]{:S(2)}) %collective-permute-start.6) | collective-permute-done | bytes 294944 | tf_op jit(solution)/shard_map/ppermute | solution.py:23
  16.3 7.4 %collective-permute-done.5 = bf16[128,1152]{1,0:T(8,128)(2,1)S(1)} collective-permute-done((bf16[128,1152]{1,0:T(8,128)(2,1)S(1)}, bf16[128,1152]{1,0:T(8,128)(2,1)S(1)}, u32[]{:S(2)}, u32[]{:S(2)}) %collective-permute-start.5) | collective-permute-done | bytes 294944 | tf_op jit(solution)/shard_map/ppermute | solution.py:23
  23.7 1.9 %multiply_reduce_fusion = (f32[512]{0:T(512)S(1)}, f32[512,1152]{1,0:T(8,128)S(1)}) fusion(bf16[1152,1152]{1,0:T(8,128)(2,1)S(1)} %copy-done, bf16[128,1152]{1,0:T(8,128)(2,1)S(1)} %collective-permute-done.7, bf16[128,1152]{1,0:T(8,128)(2,1)S(1)} %collective-permute-done.6, bf16[128,1152]{1,0:T(8,128)(2,1)S(1)} %collective-permute-done.5, ...), kind=kOutput, calls=%fused_computation.14 | convolution fusion | flops 1364852224 | bytes 6195200 | tf_op jit(solution)/shard_map/dot_general | solution.py:32
  25.7 1.7 %fusion.55 = (bf16[512,1152]{1,0:T(8,128)(2,1)S(1)}, f32[512,1152]{1,0:T(8,128)}) fusion(f32[512,1152]{1,0:T(8,128)S(1)} %get-tuple-element.28, f32[512]{0:T(512)S(1)} %add_rsqrt_fusion), kind=kLoop, calls=%fused_computation.95 | loop fusion | flops 1179648 | bytes 5900288 | tf_op jit(solution)/shard_map/convert_element_type | solution.py:35
  27.4 8.3 %collective-permute-start.8 = (bf16[512,1152]{1,0:T(8,128)(2,1)S(1)}, bf16[512,1152]{1,0:T(8,128)(2,1)S(1)}, u32[]{:S(2)}, u32[]{:S(2)}) collective-permute-start(bf16[512,1152]{1,0:T(8,128)(2,1)S(1)} %get-tuple-element.9), channel_id=1, source_target_pairs={{0,1},{1,0},{2,3},{3,2},{4,5},{5,4},{6,7},{7,6},{8,9},{9,8},{10,11... | collective-permute-start | bytes 3538952 | tf_op jit(solution)/shard_map/ppermute | solution.py:19
  35.9 2.0 %multiply_reduce_fusion.1 = (f32[512]{0:T(512)S(1)}, f32[512,1152]{1,0:T(8,128)S(1)}) fusion(bf16[1152,1152]{1,0:T(8,128)(2,1)S(1)} %copy-done.11, bf16[128,1152]{1,0:T(8,128)(2,1)S(1)} %collective-permute-done.3, bf16[128,1152]{1,0:T(8,128)(2,1)S(1)} %collective-permute-done.2, bf16[128,1152]{1,0:T(8,128)(2,1)S(1)} %collective-permute-done.1, ...), kind=kOutput, calls=%fused_computation.15 | convolution fusion | flops 1364852224 | bytes 6195200 | tf_op jit(solution)/shard_map/dot_general | solution.py:32
  37.8 1.8 %fusion.56 = (bf16[512,1152]{1,0:T(8,128)(2,1)S(1)}, f32[512,1152]{1,0:T(8,128)}) fusion(f32[512,1152]{1,0:T(8,128)S(1)} %get-tuple-element.26, f32[512]{0:T(512)S(1)} %add_rsqrt_fusion.1), kind=kLoop, calls=%fused_computation.96 | loop fusion | flops 1179648 | bytes 5900288 | tf_op jit(solution)/shard_map/convert_element_type | solution.py:35
  39.6 5.6 %fusion.15 = (f32[512]{0:T(512)S(1)}, f32[1024]{0:T(1024)S(1)}, f32[]{:T(128)}, bf16[512,1024]{1,0:T(8,128)(2,1)S(1)}) fusion(f32[]{:T(128)} %bitcast.51, f32[]{:T(128)} %bitcast.44, bf16[512,1152]{1,0:T(8,128)(2,1)S(1)} %get-tuple-element.11, bf16[512,1152]{1,0:T(8,128)(2,1)S(1)} %collective-permute-done.8, bf16[512,1152]{1,0:T(8,128)(2,1)S(1)} %get-tuple-element.9), kind=kOutput, calls=%fused_computation.32 | convolution fusion | flops 1225259520 | bytes 4593676 | tf_op jit(solution)/shard_map/dot_general | solution.py:54
  46.3 1.2 fusion.40
  48.4 1.2 copy-done.4
  49.6 1.1 copy.30
  51.2 4.8 %fusion.19 = f32[1152,288]{0,1:T(8,128)} fusion(bf16[512,1024]{1,0:T(8,128)(2,1)} %copy-done.5, s32[]{:T(128)S(6)} %select_n.61, bf16[512,1152]{1,0:T(8,128)(2,1)} %copy-done.7, bf16[512,1152]{1,0:T(8,128)(2,1)} %copy-done.12, f32[512,1152]{1,0:T(8,128)} %get-tuple-element.12, f32[512]{0:T(512)S(1)} %add_rsqrt_fusion.1, ...), kind=kOutput, calls=%fused_computation.37 | convolution fusion | flops 648364032 | bytes 6706688 | tf_op jit(solution)/shard_map/dot_general | solution.py:79
  56.0 1.3 %copy.31 = f32[512,288]{1,0:T(8,128)S(1)} copy(f32[512,288]{0,1:T(8,128)} %collective-permute-done.11) | data formatting | bytes 1179648 | tf_op jit(solution)/shard_map/ppermute | solution.py:19
  57.3 2.9 %fusion.29 = f32[1152,288]{0,1:T(8,128)S(1)} fusion(f32[512,288]{1,0:T(8,128)S(1)} %copy.31, f32[1024,288]{1,0:T(8,128)} %copy-done.4, f32[512,1152]{1,0:T(8,128)} %get-tuple-element.10, s32[]{:T(128)S(6)} %select_n.61, f32[512]{0:T(512)S(1)} %add_rsqrt_fusion, f32[512]{0:T(512)S(1)} %bitcast.56, bf16[128,1152]{1,0:T(8,128)(2,1)} %copy-done.14, ...), kind=kOutput, calls=%fused_computation.53 | convolution fusion | flops 345194496 | bytes 4673540 | tf_op jit(solution)/shard_map/dot_general | solution.py:80
  60.2 1.7 %pad_maximum_fusion.1 = f32[1152,576]{0,1:T(8,128)} fusion(f32[1152,288]{0,1:T(8,128)S(1)} %fusion.29, f32[1152,288]{0,1:T(8,128)S(1)} %copy-done.6), kind=kLoop, calls=%fused_computation.6 | loop fusion | flops 663552 | bytes 5308416 | tf_op jit(solution)/shard_map/concatenate | solution.py:81
  61.9 3.5 %copy.32 = f32[1152,576]{1,0:T(8,128)} copy(f32[1152,576]{0,1:T(8,128)} %pad_maximum_fusion.1) | data formatting | bytes 5308416 | tf_op jit(solution)/shard_map/concatenate | solution.py:81
  65.4 4.1 %reshape.43 = f32[16,2,36,576]{3,2,1,0:T(8,128)} reshape(f32[1152,576]{1,0:T(8,128)} %copy.32) | data formatting | bytes 5308416 | tf_op jit(solution)/shard_map/reshape | solution.py:82
  69.5 1.7 %constant_dynamic-slice_fusion.1 = bf16[16,1,36,576]{3,2,1,0:T(8,128)(2,1)S(1)} fusion(f32[16,2,36,576]{3,2,1,0:T(8,128)} %reshape.43, s32[]{:T(128)S(6)} %select_n.63), kind=kLoop, calls=%fused_computation.86 | loop fusion | bytes 1327108 | tf_op jit(solution)/shard_map/jit(dynamic_index_in_dim)/dynamic_slice | solution.py:83
  71.6 2.3 %fusion.3 = bf16[128,1152]{1,0:T(8,128)(2,1)} fusion(bf16[512,1152]{1,0:T(8,128)(2,1)S(1)} %copy-done.13, bf16[512,1152]{1,0:T(8,128)(2,1)S(1)} %copy-done.8, f32[]{:T(128)} %bitcast.49, bf16[512,1024]{1,0:T(8,128)(2,1)} %copy-done.5), kind=kOutput, calls=%fused_computation.12 | convolution fusion | flops 307003392 | bytes 2916864 | tf_op jit(solution)/shard_map/dot_general | solution.py:98
  74.1 1.1 copy-done.2
  75.2 2.2 %fusion.4 = bf16[128,1152]{1,0:T(8,128)(2,1)} fusion(f32[128,1152]{1,0:T(8,128)} %collective-permute-done.14, bf16[512,1152]{1,0:T(8,128)(2,1)S(1)} %copy-done.2, f32[]{:T(128)} %bitcast.50, bf16[512,1024]{1,0:T(8,128)(2,1)} %copy-done.5), kind=kOutput, calls=%fused_computation.13 | convolution fusion | flops 151437312 | bytes 2195968 | tf_op jit(solution)/shard_map/dot_general | solution.py:100
  78.8 9.5 %all-to-all-start = ((bf16[16,36,576]{2,1,0:T(8,128)(2,1)}), bf16[16,36,576]{2,1,0:T(8,128)(2,1)S(1)}, u32[]{:S(2)}, u32[]{:S(2)}) async-start(bf16[16,36,576]{2,1,0:T(8,128)(2,1)} %copy.35), calls=%async_computation | async-start | bytes 1638400 | tf_op jit(solution)/shard_map/all_to_all | solution.py:86
  88.3 1.9 %pad_maximum_fusion.6 = bf16[256,1152]{1,0:T(8,128)(2,1)} fusion(bf16[128,1152]{1,0:T(8,128)(2,1)} %fusion.4, bf16[128,1152]{1,0:T(8,128)(2,1)} %fusion.3), kind=kLoop, calls=%fused_computation.50 | loop fusion | flops 1179648 | bytes 1179648 | tf_op jit(solution)/shard_map/concatenate | solution.py:106
  90.3 1.5 %collective-permute-start.15 = (bf16[256,1152]{1,0:T(8,128)(2,1)}, bf16[256,1152]{1,0:T(8,128)(2,1)}, u32[]{:S(2)}, u32[]{:S(2)}) collective-permute-start(bf16[256,1152]{1,0:T(8,128)(2,1)} %pad_maximum_fusion.6), channel_id=1, source_target_pairs={{1,128},{128,1},{3,130},{130,3},{5,132},{132,5},{7,134},{134,7},{9... | collective-permute-start | bytes 1769480 | tf_op jit(solution)/shard_map/ppermute | solution.py:15
  92.4 2.4 %collective-permute-start.9 = (f32[8,128]{1,0:T(8,128)S(1)}, f32[8,128]{1,0:T(8,128)S(1)}, u32[]{:S(2)}, u32[]{:S(2)}) collective-permute-start(f32[8,128]{1,0:T(8,128)S(1)} %broadcast_in_dim.29), channel_id=1, source_target_pairs={{0,1},{1,0},{2,3},{3,2},{4,5},{5,4},{6,7},{7,6},{8,9},{9,8},{10,11... | collective-permute-start | bytes 12296 | tf_op jit(solution)/shard_map/ppermute | solution.py:19
  96.9 2.0 %broadcast_select_fusion = bf16[256,1152]{1,0:T(8,128)(2,1)} fusion(bf16[256,1152]{1,0:T(8,128)(2,1)} %collective-permute-done.15, pred[]{:T(512)S(6)} %eq.10, bf16[128,1152]{1,0:T(8,128)(2,1)} %fusion.4, bf16[128,1152]{1,0:T(8,128)(2,1)} %fusion.3), kind=kLoop, calls=%fused_computation.51 | loop fusion | flops 1474560 | bytes 1769473 | tf_op jit(solution)/shard_map/jit(_where)/select_n | solution.py:109
  98.9 11.3 %all-to-all-done = bf16[16,36,576]{2,1,0:T(8,128)(2,1)S(1)} async-done(((bf16[16,36,576]{2,1,0:T(8,128)(2,1)}), bf16[16,36,576]{2,1,0:T(8,128)(2,1)S(1)}, u32[]{:S(2)}, u32[]{:S(2)}) %all-to-all-start) | async-done | bytes 663584 | tf_op jit(solution)/shard_map/all_to_all | solution.py:86
  111.1 5.6 %all-to-all-start.1 = ((bf16[8,36,576]{2,1,0:T(8,128)(2,1)}), bf16[8,36,576]{2,1,0:T(8,128)(2,1)S(1)}, u32[]{:S(2)}, u32[]{:S(2)}) async-start(bf16[8,36,576]{2,1,0:T(8,128)(2,1)} %broadcast_in_dim.30), calls=%async_computation.1 | async-start | bytes 819200 | tf_op jit(solution)/shard_map/all_to_all | solution.py:88
  116.7 1.9 %slice_bitcast_fusion = (bf16[1,128,1152]{2,1,0:T(8,128)(2,1)}, bf16[1,128,1152]{2,1,0:T(8,128)(2,1)}) fusion(bf16[256,1152]{1,0:T(8,128)(2,1)} %broadcast_select_fusion), kind=kLoop, calls=%fused_computation.60 | loop fusion | bytes 1179648 | tf_op jit(solution)/shard_map/broadcast_in_dim | solution.py:116
  118.6 8.0 %all-to-all-done.1 = bf16[8,36,576]{2,1,0:T(8,128)(2,1)S(1)} async-done(((bf16[8,36,576]{2,1,0:T(8,128)(2,1)}), bf16[8,36,576]{2,1,0:T(8,128)(2,1)S(1)}, u32[]{:S(2)}, u32[]{:S(2)}) %all-to-all-start.1) | async-done | bytes 331808 | tf_op jit(solution)/shard_map/all_to_all | solution.py:88
  (88 shorter events, 15.7 us)
Async XLA Ops:
  0.6 23.1 %copy-start = (bf16[1152,1152]{1,0:T(8,128)(2,1)S(1)}, bf16[1152,1152]{1,0:T(8,128)(2,1)}, u32[]{:S(2)}) copy-start(bf16[1152,1152]{1,0:T(8,128)(2,1)} %param.9) | copy-start | bytes 7962628
  0.6 2.8 %collective-permute-start.4 = (bf16[128,1152]{1,0:T(8,128)(2,1)}, bf16[128,1152]{1,0:T(8,128)(2,1)S(1)}, u32[]{:S(2)}, u32[]{:S(2)}) collective-permute-start(bf16[128,1152]{1,0:T(8,128)(2,1)} %bitcast.53), channel_id=1, source_target_pairs={{1,128},{128,1},{3,130},{130,3},{5,132},{132,5},{7,134},{134,7},{9... | collective-permute-start | bytes 884744 | tf_op jit(solution)/shard_map/ppermute | solution.py:15
  1.5 8.3 %collective-permute-start = (bf16[128,1152]{1,0:T(8,128)(2,1)}, bf16[128,1152]{1,0:T(8,128)(2,1)S(1)}, u32[]{:S(2)}, u32[]{:S(2)}) collective-permute-start(bf16[128,1152]{1,0:T(8,128)(2,1)} %bitcast.54), channel_id=1, source_target_pairs={{1,128},{128,1},{3,130},{130,3},{5,132},{132,5},{7,134},{134,7},{9... | collective-permute-start | bytes 884744 | tf_op jit(solution)/shard_map/ppermute | solution.py:15
  4.5 21.2 %copy-start.9 = (bf16[128,1152]{1,0:T(8,128)(2,1)}, bf16[128,1152]{1,0:T(8,128)(2,1)S(1)}, u32[]{:S(2)}) copy-start(bf16[128,1152]{1,0:T(8,128)(2,1)S(1)} %broadcast_select_fusion.1) | copy-start | bytes 884740
  4.5 9.8 %collective-permute-start.7 = (bf16[128,1152]{1,0:T(8,128)(2,1)S(1)}, bf16[128,1152]{1,0:T(8,128)(2,1)S(1)}, u32[]{:S(2)}, u32[]{:S(2)}) collective-permute-start(bf16[128,1152]{1,0:T(8,128)(2,1)S(1)} %broadcast_select_fusion.1), channel_id=1, source_target_pairs={{0,64},{32,96},{64,0},{96,32},{1,65},{33,97},{65,1},{97,33},{2,66}... | collective-permute-start | bytes 884744 | tf_op jit(solution)/shard_map/ppermute | solution.py:23
  7.8 8.6 %collective-permute-start.6 = (bf16[128,1152]{1,0:T(8,128)(2,1)S(1)}, bf16[128,1152]{1,0:T(8,128)(2,1)S(1)}, u32[]{:S(2)}, u32[]{:S(2)}) collective-permute-start(bf16[128,1152]{1,0:T(8,128)(2,1)S(1)} %broadcast_select_fusion.1), channel_id=1, source_target_pairs={{0,96},{32,0},{64,32},{96,64},{1,97},{33,1},{65,33},{97,65},{2,98}... | collective-permute-start | bytes 884744 | tf_op jit(solution)/shard_map/ppermute | solution.py:23
  8.8 14.9 %collective-permute-start.5 = (bf16[128,1152]{1,0:T(8,128)(2,1)S(1)}, bf16[128,1152]{1,0:T(8,128)(2,1)S(1)}, u32[]{:S(2)}, u32[]{:S(2)}) collective-permute-start(bf16[128,1152]{1,0:T(8,128)(2,1)S(1)} %broadcast_select_fusion.1), channel_id=1, source_target_pairs={{0,32},{32,64},{64,96},{96,0},{1,33},{33,65},{65,97},{97,1},{2,34}... | collective-permute-start | bytes 884744 | tf_op jit(solution)/shard_map/ppermute | solution.py:23
  10.8 25.0 %copy-start.10 = (bf16[128,1152]{1,0:T(8,128)(2,1)}, bf16[128,1152]{1,0:T(8,128)(2,1)S(1)}, u32[]{:S(2)}) copy-start(bf16[128,1152]{1,0:T(8,128)(2,1)S(1)} %broadcast_select_fusion.2) | copy-start | bytes 884740
  10.8 25.0 %collective-permute-start.3 = (bf16[128,1152]{1,0:T(8,128)(2,1)S(1)}, bf16[128,1152]{1,0:T(8,128)(2,1)S(1)}, u32[]{:S(2)}, u32[]{:S(2)}) collective-permute-start(bf16[128,1152]{1,0:T(8,128)(2,1)S(1)} %broadcast_select_fusion.2), channel_id=1, source_target_pairs={{0,64},{32,96},{64,0},{96,32},{1,65},{33,97},{65,1},{97,33},{2,66}... | collective-permute-start | bytes 884744 | tf_op jit(solution)/shard_map/ppermute | solution.py:23
  11.6 24.2 %collective-permute-start.2 = (bf16[128,1152]{1,0:T(8,128)(2,1)S(1)}, bf16[128,1152]{1,0:T(8,128)(2,1)S(1)}, u32[]{:S(2)}, u32[]{:S(2)}) collective-permute-start(bf16[128,1152]{1,0:T(8,128)(2,1)S(1)} %broadcast_select_fusion.2), channel_id=1, source_target_pairs={{0,96},{32,0},{64,32},{96,64},{1,97},{33,1},{65,33},{97,65},{2,98}... | collective-permute-start | bytes 884744 | tf_op jit(solution)/shard_map/ppermute | solution.py:23
  14.2 11.4 %copy-start.14 = (bf16[128,1152]{1,0:T(8,128)(2,1)}, bf16[128,1152]{1,0:T(8,128)(2,1)S(1)}, u32[]{:S(2)}) copy-start(bf16[128,1152]{1,0:T(8,128)(2,1)S(1)} %collective-permute-done.7) | copy-start | bytes 884740
  14.2 21.6 %collective-permute-start.1 = (bf16[128,1152]{1,0:T(8,128)(2,1)S(1)}, bf16[128,1152]{1,0:T(8,128)(2,1)S(1)}, u32[]{:S(2)}, u32[]{:S(2)}) collective-permute-start(bf16[128,1152]{1,0:T(8,128)(2,1)S(1)} %broadcast_select_fusion.2), channel_id=1, source_target_pairs={{0,32},{32,64},{64,96},{96,0},{1,33},{33,65},{65,97},{97,1},{2,34}... | collective-permute-start | bytes 884744 | tf_op jit(solution)/shard_map/ppermute | solution.py:23
  16.3 9.3 %copy-start.15 = (bf16[128,1152]{1,0:T(8,128)(2,1)}, bf16[128,1152]{1,0:T(8,128)(2,1)S(1)}, u32[]{:S(2)}) copy-start(bf16[128,1152]{1,0:T(8,128)(2,1)S(1)} %collective-permute-done.6) | copy-start | bytes 884740
  25.7 10.1 %copy-start.11 = (bf16[1152,1152]{1,0:T(8,128)(2,1)S(1)}, bf16[1152,1152]{1,0:T(8,128)(2,1)}, u32[]{:S(2)}) copy-start(bf16[1152,1152]{1,0:T(8,128)(2,1)} %param.8) | copy-start | bytes 7962628
  27.4 12.2 %copy-start.7 = (bf16[512,1152]{1,0:T(8,128)(2,1)}, bf16[512,1152]{1,0:T(8,128)(2,1)S(1)}, u32[]{:S(2)}) copy-start(bf16[512,1152]{1,0:T(8,128)(2,1)S(1)} %get-tuple-element.9) | copy-start | bytes 3538948
  27.4 12.2 %collective-permute-start.8 = (bf16[512,1152]{1,0:T(8,128)(2,1)S(1)}, bf16[512,1152]{1,0:T(8,128)(2,1)S(1)}, u32[]{:S(2)}, u32[]{:S(2)}) collective-permute-start(bf16[512,1152]{1,0:T(8,128)(2,1)S(1)} %get-tuple-element.9), channel_id=1, source_target_pairs={{0,1},{1,0},{2,3},{3,2},{4,5},{5,4},{6,7},{7,6},{8,9},{9,8},{10,11... | collective-permute-start | bytes 3538952 | tf_op jit(solution)/shard_map/ppermute | solution.py:19
  35.8 2.0 %copy-start.18 = (bf16[128,1152]{1,0:T(8,128)(2,1)}, bf16[128,1152]{1,0:T(8,128)(2,1)S(1)}, u32[]{:S(2)}) copy-start(bf16[128,1152]{1,0:T(8,128)(2,1)S(1)} %collective-permute-done.2) | copy-start | bytes 884740
  39.6 7.9 %copy-start.1 = (bf16[512,1152]{1,0:T(8,128)(2,1)}, bf16[512,1152]{1,0:T(8,128)(2,1)S(1)}, u32[]{:S(2)}) copy-start(bf16[512,1152]{1,0:T(8,128)(2,1)S(1)} %get-tuple-element.11) | copy-start | bytes 3538948
  39.6 5.6 %copy-start.12 = (bf16[512,1152]{1,0:T(8,128)(2,1)}, bf16[512,1152]{1,0:T(8,128)(2,1)S(1)}, u32[]{:S(2)}) copy-start(bf16[512,1152]{1,0:T(8,128)(2,1)S(1)} %collective-permute-done.8) | copy-start | bytes 3538948
  45.3 3.1 %copy-start.5 = (bf16[512,1024]{1,0:T(8,128)(2,1)}, bf16[512,1024]{1,0:T(8,128)(2,1)S(1)}, u32[]{:S(2)}) copy-start(bf16[512,1024]{1,0:T(8,128)(2,1)S(1)} %get-tuple-element.8) | copy-start | bytes 3145732
  45.3 10.7 %collective-permute-start.12 = (f32[512,1]{0,1:T(1,128)S(1)}, f32[512,1]{0,1:T(1,128)S(1)}, u32[]{:S(2)}, u32[]{:S(2)}) collective-permute-start(f32[512,1]{0,1:T(1,128)S(1)} %bitcast.57), channel_id=1, source_target_pairs={{0,1},{1,0},{2,3},{3,2},{4,5},{5,4},{6,7},{7,6},{8,9},{9,8},{10,11... | collective-permute-start | bytes 6152 | tf_op jit(solution)/shard_map/ppermute | solution.py:19
  47.5 26.5 %collective-permute-start.14 = (f32[128,1152]{1,0:T(8,128)}, f32[128,1152]{1,0:T(8,128)}, u32[]{:S(2)}, u32[]{:S(2)}) collective-permute-start(f32[128,1152]{1,0:T(8,128)} %fusion.40), channel_id=1, source_target_pairs={{0,1},{1,0},{2,3},{3,2},{4,5},{5,4},{6,7},{7,6},{8,9},{9,8},{10,11... | collective-permute-start | bytes 1769480 | tf_op jit(solution)/shard_map/ppermute | solution.py:19
  50.7 5.3 %collective-permute-start.11 = (f32[512,288]{0,1:T(8,128)}, f32[512,288]{0,1:T(8,128)}, u32[]{:S(2)}, u32[]{:S(2)}) collective-permute-start(f32[512,288]{0,1:T(8,128)} %copy.30), channel_id=1, source_target_pairs={{0,1},{1,0},{2,3},{3,2},{4,5},{5,4},{6,7},{7,6},{8,9},{9,8},{10,11... | collective-permute-start | bytes 1769480 | tf_op jit(solution)/shard_map/ppermute | solution.py:19
  57.3 2.9 %copy-start.6 = (f32[1152,288]{0,1:T(8,128)S(1)}, f32[1152,288]{0,1:T(8,128)}, u32[]{:S(2)}) copy-start(f32[1152,288]{0,1:T(8,128)} %fusion.19) | copy-start | bytes 3981316
  69.5 2.1 %copy-start.13 = (bf16[512,1152]{1,0:T(8,128)(2,1)S(1)}, bf16[512,1152]{1,0:T(8,128)(2,1)}, u32[]{:S(2)}) copy-start(bf16[512,1152]{1,0:T(8,128)(2,1)} %copy-done.12) | copy-start | bytes 3538948
  71.3 6.2 %collective-permute-start.13 = (bf16[16,36,576]{2,0,1:T(8,128)(2,1)S(1)}, bf16[16,36,576]{2,0,1:T(8,128)(2,1)S(1)}, u32[]{:S(2)}, u32[]{:S(2)}) collective-permute-start(bf16[16,36,576]{2,0,1:T(8,128)(2,1)S(1)} %bitcast.52), channel_id=1, source_target_pairs={{0,1},{1,0},{2,3},{3,2},{4,5},{5,4},{6,7},{7,6},{8,9},{9,8},{10,11... | collective-permute-start | bytes 1990664 | tf_op jit(solution)/shard_map/ppermute | solution.py:19
  71.6 2.3 %copy-start.3 = (f32[16,2,36,576]{3,2,1,0:T(8,128)S(1)}, f32[16,2,36,576]{3,2,1,0:T(8,128)}, u32[]{:S(2)}) copy-start(f32[16,2,36,576]{3,2,1,0:T(8,128)} %reshape.43) | copy-start | bytes 7962628
  78.8 31.4 %all-to-all-start = ((bf16[16,36,576]{2,1,0:T(8,128)(2,1)}), bf16[16,36,576]{2,1,0:T(8,128)(2,1)S(1)}, u32[]{:S(2)}, u32[]{:S(2)}) async-start(bf16[16,36,576]{2,1,0:T(8,128)(2,1)} %copy.35), calls=%async_computation | async-start | bytes 1638400 | tf_op jit(solution)/shard_map/all_to_all | solution.py:86
  90.3 6.6 %collective-permute-start.15 = (bf16[256,1152]{1,0:T(8,128)(2,1)}, bf16[256,1152]{1,0:T(8,128)(2,1)}, u32[]{:S(2)}, u32[]{:S(2)}) collective-permute-start(bf16[256,1152]{1,0:T(8,128)(2,1)} %pad_maximum_fusion.6), channel_id=1, source_target_pairs={{1,128},{128,1},{3,130},{130,3},{5,132},{132,5},{7,134},{134,7},{9... | collective-permute-start | bytes 1769480 | tf_op jit(solution)/shard_map/ppermute | solution.py:15
  92.4 3.3 %collective-permute-start.9 = (f32[8,128]{1,0:T(8,128)S(1)}, f32[8,128]{1,0:T(8,128)S(1)}, u32[]{:S(2)}, u32[]{:S(2)}) collective-permute-start(f32[8,128]{1,0:T(8,128)S(1)} %broadcast_in_dim.29), channel_id=1, source_target_pairs={{0,1},{1,0},{2,3},{3,2},{4,5},{5,4},{6,7},{7,6},{8,9},{9,8},{10,11... | collective-permute-start | bytes 12296 | tf_op jit(solution)/shard_map/ppermute | solution.py:19
  95.7 0.7 collective-permute-start.10
  111.1 15.5 %all-to-all-start.1 = ((bf16[8,36,576]{2,1,0:T(8,128)(2,1)}), bf16[8,36,576]{2,1,0:T(8,128)(2,1)S(1)}, u32[]{:S(2)}, u32[]{:S(2)}) async-start(bf16[8,36,576]{2,1,0:T(8,128)(2,1)} %broadcast_in_dim.30), calls=%async_computation.1 | async-start | bytes 819200 | tf_op jit(solution)/shard_map/all_to_all | solution.py:88
  (6 other events, 10.3 us)

commit v2 on v1

v2 whole, which is shorter than its diff:
```python
import jax
import jax.numpy as jnp
from jax import lax
from jax.experimental import pallas as pl
from jax.experimental.pallas import tpu as pltpu
from jax.sharding import Mesh, PartitionSpec as P

epsilon = 1e-06
AXES = ("xh", "y", "xl", "z", "c")
XH, Y, XL, Z, C = 2, 4, 2, 8, 2
WIDE, SLIM = 256, 128
f32, bf16 = jnp.float32, jnp.bfloat16


def trade(x):
    return lax.ppermute(x, ("xh", "c"), [(0, 0), (1, 2), (2, 1), (3, 3)])


def other_core(x):
    return lax.ppermute(x, "c", [(0, 1), (1, 0)])


def from_y(x, k):
    return lax.ppermute(x, "y", [(i, (i + k) % Y) for i in range(Y)])


def gather(own):
    return own, from_y(own, 1), from_y(own, -1), from_y(own, 2)


def dot(a, b):
    return lax.dot_general(a, b, (((1,), (0,)), ((), ())), preferred_element_type=f32)


def dot_cols(a, b):
    return lax.dot_general(a, b, (((1,), (1,)), ((), ())), preferred_element_type=f32)


def dot_rows(a, b):
    return lax.dot_general(a, b, (((0,), (0,)), ((), ())), preferred_element_type=f32)


def image_start(y):
    return pl.multiple_of(y * WIDE + jnp.where(y > 0, SLIM, 0), SLIM)


def text_start(y):
    return pl.multiple_of(y * WIDE, WIDE)


def join_and_project(pieces, weight, cat, emb, unit, inv):
    n = pieces[0].shape[0]
    for i, piece in enumerate(pieces):
        cat[i * n : (i + 1) * n, :] = piece[...]
    rows = cat.shape[0]
    step = rows // 2
    for r in range(0, rows, step):
        pre = dot(cat[r : r + step, :], weight[...])
        inverse = lax.rsqrt(jnp.sum(pre * pre, axis=1, keepdims=True) + epsilon)
        value = pre * inverse
        unit[r : r + step, :] = value
        emb[r : r + step, :] = value.astype(bf16)
        inv[r : r + step, :] = jnp.broadcast_to(inverse, (step, inv.shape[1]))


def text_kernel(ids, t0, t1, t2, t3, weight, cat, emb, window, inv, unit):
    join_and_project((t0, t1, t2, t3), weight, cat, emb, unit, inv)
    y = ids[0]
    window[:, :WIDE] = unit[:, pl.ds(text_start(y), WIDE)]
    window[:, WIDE:] = unit[:, unit.shape[1] - SLIM :]


def image_kernel(ids, i0, i1, i2, i3, weight, cat, emb, window, inv, unit):
    join_and_project((i0, i1, i2, i3), weight, cat, emb, unit, inv)
    y = ids[0]
    window[:, :WIDE] = unit[:, pl.ds(image_start(y), WIDE)]
    window[:, WIDE:] = unit[:, WIDE : WIDE + SLIM]


def slope_kernel(
    ids, scal, emb, own, other, slopes, radial, text_radial, give, give_out, loss
):
    y = ids[0]
    scale, bias = scal[0], scal[1]
    rows = emb.shape[0]
    embedded = emb[...]
    lost = jnp.zeros((8, WIDE), f32)
    along = jnp.zeros((rows, WIDE), f32)
    for j in range(2 * rows // WIDE):
        mine = j * WIDE < rows
        side, at = (own, j * WIDE) if mine else (other, j * WIDE - rows)
        cosine = dot_cols(embedded, side[at : at + WIDE, :])
        logits = scale * cosine + bias
        if mine:
            same = (
                lax.broadcasted_iota(jnp.int32, logits.shape, 0)
                == lax.broadcasted_iota(jnp.int32, logits.shape, 1) + at
            )
            logits = jnp.where(same, -logits, logits)
        small = jnp.exp(-jnp.abs(logits))
        term = jnp.maximum(logits, 0.0) + jnp.log1p(small)
        lost = lost + jnp.sum(term.reshape(rows // 8, 8, WIDE), axis=0)
        slope = jnp.where(logits >= 0, 1.0, small) / (1.0 + small)
        if mine:
            slope = jnp.where(same, -slope, slope)
        slope = slope.astype(bf16)
        slopes[:, j * WIDE : (j + 1) * WIDE] = slope
        weighted = slope.astype(f32) * cosine
        along = along + weighted
        down = jnp.sum(weighted, axis=0, keepdims=True)
        down = jnp.transpose(jnp.broadcast_to(down, (SLIM, WIDE)))
        if mine:
            text_radial[at : at + WIDE, :] = down
        else:
            give[at : at + WIDE, WIDE + SLIM :] = down
    radial[...] = jnp.broadcast_to(jnp.sum(along, axis=1, keepdims=True), radial.shape)
    loss[...] = jnp.broadcast_to(jnp.sum(lost, keepdims=True), loss.shape)
    give[:, :WIDE] = dot_rows(slopes[:, rows:], emb[:, pl.ds(text_start(y), WIDE)])

    @pl.when(y == Y - 1)
    def _():
        give[:, WIDE : WIDE + SLIM] = dot_rows(slopes[:, rows:], emb[:, emb.shape[1] - SLIM :])

    @pl.when(y != Y - 1)
    def _():
        give[:, WIDE : WIDE + SLIM] = jnp.zeros((rows, SLIM), f32)

    give_out[...] = dot_rows(slopes[:, rows : rows + give_out.shape[0]], embedded)


def wide(x, n):
    return jnp.concatenate([x] * (n // x.shape[1]), axis=1)


def back(grad, window, radial, inv):
    n = grad.shape[1]
    return ((grad - window * wide(radial, n)) * wide(inv, n)).astype(bf16)


def grad_kernel(
    ids, scal, cat, emb, window, inv, slopes, radial, own, other,
    term, part, out, part_out,
):
    y = ids[0]
    scale = scal[0]
    rows = cat.shape[0]
    n = out.shape[0]

    def columns(cols, at, size):
        grad = dot(slopes[:, :rows], own[:, cols]) + dot(slopes[:, rows:], other[:, cols])
        grad = back(scale * grad, window[:, at : at + size], scale * radial[...], inv[...])
        term[:, at : at + size] = dot_rows(cat[...], grad)

    columns(pl.ds(image_start(y), WIDE), 0, WIDE)
    part[:, :WIDE] = dot_rows(slopes[:, :rows], emb[:, pl.ds(text_start(y), WIDE)])

    @pl.when(y == 0)
    def _():
        columns(slice(WIDE, WIDE + SLIM), WIDE, SLIM)

    @pl.when(y == Y - 1)
    def _():
        part[:, WIDE:] = dot_rows(slopes[:, :rows], emb[:, emb.shape[1] - SLIM :])

    @pl.when(y != Y - 1)
    def _():
        part[:, WIDE:] = jnp.zeros((rows, SLIM), f32)

    out[...] = (scale * (dot(slopes[:n, :rows], own[...]) + dot(slopes[:n, rows:], other[...]))).astype(bf16)
    part_out[...] = dot_rows(slopes[:, :n], emb[...])


def sum_kernel(
    ids, scal, cat, window, inv, text_radial, part, got, part_out, got_out, image_term,
    give, keep, out, term,
):
    y, c = ids[0], ids[1]
    scale = scal[0]
    grad = scale * (part[...] + got[:, : WIDE + SLIM])
    radial = scale * (text_radial[...] + got[:, WIDE + SLIM :])
    grad = back(grad, window[...], radial, inv[...])
    term[:, :WIDE] = dot_rows(cat[...], grad[:, :WIDE])

    @pl.when(y == Y - 1)
    def _():
        term[:, WIDE:] = dot_rows(cat[...], grad[:, WIDE:])

    @pl.when(y == 0)
    def _():
        term[:, WIDE:] = image_term[:, WIDE:]

    @pl.when((y != 0) & (y != Y - 1))
    def _():
        term[:, WIDE:] = jnp.zeros((term.shape[0], SLIM), f32)

    first = c == 0
    half = keep.shape[1]
    for k in range(keep.shape[0]):
        for source, at, size in ((image_term, 0, WIDE), (term, WIDE, WIDE + SLIM)):
            low = source[2 * half * k : 2 * half * k + half, :size]
            high = source[2 * half * k + half : 2 * half * (k + 1), :size]
            keep[k, :, at : at + size] = jnp.where(first, low, high)
            give[k, :, at : at + size] = jnp.where(first, high, low).astype(bf16)
    out[...] = (scale * (part_out[...] + got_out[...])).astype(bf16)


def call(kernel, outs, scratch=(), macs=0):
    def in_vmem(x):
        return pl.BlockSpec(memory_space=pltpu.SMEM if x.ndim == 1 else pltpu.VMEM)

    def run(*args):
        return pl.pallas_call(
            kernel,
            out_shape=[jax.ShapeDtypeStruct(s, d) for s, d in outs],
            in_specs=[in_vmem(a) for a in args],
            out_specs=[pl.BlockSpec(memory_space=pltpu.VMEM) for _ in outs],
            scratch_shapes=list(scratch),
            compiler_params=pltpu.CompilerParams(vmem_limit_bytes=40 * 2**20),
            cost_estimate=pl.CostEstimate(flops=2 * macs, bytes_accessed=0, transcendentals=0),
        )(*args)

    return run


def on_device(image_feats, text_feats, image_proj, text_proj, logit_scale, logit_bias):
    c, y = lax.axis_index("c"), lax.axis_index("y")
    ids = jnp.stack([y, c]).astype(jnp.int32)
    scal = jnp.concatenate([logit_scale, logit_bias])
    n, depth = image_feats.shape[1:]
    width = image_proj.shape[1]
    rows = n * Y

    text_own, image_own = trade(text_feats[0]), trade(image_feats[0])
    text = gather(text_own)
    image = gather(image_own)
    projected = [
        ((rows, depth), bf16), ((rows, width), bf16), ((rows, WIDE + SLIM), f32), ((rows, SLIM), f32),
    ]
    unit = [pltpu.VMEM((rows, width), f32)]
    macs = 20 * rows * depth * width
    text_cat, text_emb, text_window, text_inv = call(text_kernel, projected, unit, macs)(ids, *text, text_proj)
    text_other = other_core(text_emb)
    image_cat, image_emb, image_window, image_inv = call(image_kernel, projected, unit, macs)(ids, *image, image_proj)
    slopes, image_radial, text_radial, give, give_out, loss = call(
        slope_kernel,
        [
            ((rows, C * rows), bf16), ((rows, SLIM), f32), ((rows, SLIM), f32),
            ((rows, WIDE + 2 * SLIM), f32), ((n, width), f32), ((8, SLIM), f32),
        ],
    )(ids, scal, image_emb, text_emb, text_other)
    got, got_out = other_core(give), other_core(give_out)
    image_term, part, image_out, part_out = call(
        grad_kernel,
        [((depth, WIDE + SLIM), f32), ((rows, WIDE + SLIM), f32), ((n, width), bf16), ((n, width), f32)],
    )(ids, scal, image_cat, image_emb, image_window, image_inv, slopes, image_radial, text_emb, text_other)
    each = depth // (XL * Z * C)
    wide_term = 2 * WIDE + SLIM
    give, keep, text_out = call(
        sum_kernel,
        [((XL * Z, each, wide_term), bf16), ((XL * Z, each, wide_term), f32), ((n, width), bf16)],
        [pltpu.VMEM((depth, WIDE + SLIM), f32)],
    )(
        ids, scal, text_cat, text_window, text_inv, text_radial, part, got, part_out, got_out, image_term,
    )
    mine = (keep + other_core(give).astype(f32)).astype(bf16)
    arrived = lax.all_to_all(mine, ("xl", "z"), 0, 0)
    summed = jnp.sum(arrived.astype(f32), axis=0).astype(bf16)
    spread = lax.all_to_all(
        jnp.broadcast_to(summed[None], (XH * Y,) + summed.shape), ("xh", "y"), 0, 0
    )
    spread = spread.astype(f32)
    spread = spread[:Y] + spread[Y:]
    image_grad = [spread[0, :, :WIDE], spread[0, :, 2 * WIDE :]] + [spread[i, :, :WIDE] for i in range(1, Y)]
    text_grad = [spread[i, :, WIDE : 2 * WIDE] for i in range(Y)] + [spread[Y - 1, :, 2 * WIDE :]]

    outs = trade(jnp.concatenate([image_out, text_out], axis=0))
    loss = trade(loss + other_core(loss)) / (rows * C)
    return (
        loss[0, :1],
        jnp.concatenate(image_grad, axis=1),
        jnp.concatenate(text_grad, axis=1),
        outs[:n][None],
        outs[n:][None],
    )


def solution(mesh):
    fine = Mesh(mesh.devices.reshape(XH, Y, XL, Z, C), AXES)
    dp, blk = ("xl", "z", "c"), ("xh", "y")
    in_specs = (P(dp, blk, None), P(dp, blk, None), P(), P(), P(), P())
    out_specs = (P(dp), P(dp, None), P(dp, None), P(dp, blk, None), P(dp, blk, None))
    return jax.shard_map(
        on_device, mesh=fine, in_specs=in_specs, out_specs=out_specs, check_vma=False
    )
```

time: 129 us -> 98.8 us (0.77)
  matrix products: 23.7 us -> 0 us
  local copies, waits for them, and re-layouts: 20.5 us -> 4.74 us
  Pallas kernels: 0 us -> 15.3 us
  other arithmetic: 11.7 us -> 1.6 us
  starting transfers between devices: 40.1 us -> 45 us
    dot_general x9 -> x0, matrix products: 23.7 us -> none  [the longest x1 5.63 us: on_device(): lax.dot_general(image_emb, text_all, contract_cols, preferred_element_typ...]
    pallas_call x0 -> x5, Pallas kernels: none -> 15.3 us  [run(): pl.pallas_call(kernel, out_shape=[jax.ShapeDtypeStruct(s, d) for s, d in...]
    ppermute x6, waiting for transfers between devices: 9.23 us -> 2.88 us  [from_y(): return lax.ppermute(x, 'y', [(i, (i + k) % Y) for i in range(Y)])]
    ppermute x6 -> x5, starting transfers between devices: 12.4 us -> 18 us  [other_core(): return lax.ppermute(x, 'c', [(0, 1), (1, 0)])]
    concatenate x3 -> x2, local copies, waits for them, and re-layouts: 5.08 us -> 0.01 us  [the longest x1 0.01 us: on_device(): jnp.concatenate(text_grad, axis=1)]
    all_to_all x1, waiting for transfers between devices: 11.3 us -> 15.7 us  [on_device(): arrived = lax.all_to_all(mine, ('xl', 'z'), 0, 0)]
    reshape x1 -> x0, local copies, waits for them, and re-layouts: 4.06 us -> none  [on_device(): term = term.reshape(XL * Z, C, -1, 2 * cols)]
    select_n x4 -> x0, other arithmetic: 4.04 us -> none  [the longest x1 2.03 us: on_device(): outs = jnp.where(keep, outs, trade(outs))]
  transfers between devices with their start and end apart: 18 -> 17, of which waited for: 5 -> 5; matrix products, arithmetic and copies ran while one was open for 34% -> 3% of each run, Pallas kernels for 0% -> 9%
where the time goes in v2:
time: 98.8 us; the launch traced here: 98.4 us
  starting transfers between devices  45 us (46%)
  waiting for transfers between devices  29.7 us (30%)
  Pallas kernels  15.3 us (15%)
  local copies, waits for them, and re-layouts  4.74 us (5%)
  between operations  2.16 us (2%)
  other arithmetic  1.6 us (2%)
    ppermute x5, starting transfers between devices, other_core(): return lax.ppermute(x, 'c', [(0, 1), (1, 0)])  18 us
    all_to_all x1, waiting for transfers between devices, on_device(): arrived = lax.all_to_all(mine, ('xl', 'z'), 0, 0)  15.7 us
    pallas_call x5, Pallas kernels, run(): pl.pallas_call(kernel, out_shape=[jax.ShapeDtypeStruct(s, d) for s, d in...  15.3 us
    all_to_all x1, starting transfers between devices, on_device(): arrived = lax.all_to_all(mine, ('xl', 'z'), 0, 0)  9.52 us
    ppermute x6, starting transfers between devices, from_y(): return lax.ppermute(x, 'y', [(i, (i + k) % Y) for i in range(Y)])  8.81 us
    all_to_all x1, waiting for transfers between devices, on_device(): lax.all_to_all(jnp.broadcast_to(summed[None], (XH * Y,) + summed.shape),...  8.46 us
    ppermute x4, starting transfers between devices, trade(): return lax.ppermute(x, ('xh', 'c'), [(0, 0), (1, 2), (2, 1), (3, 3)])  4.57 us
    all_to_all x1, starting transfers between devices, on_device(): lax.all_to_all(jnp.broadcast_to(summed[None], (XH * Y,) + summed.shape),...  4.09 us
  transfers between devices with their start and end apart: 17, of which 5 were waited for; matrix products, arithmetic and copies ran while one was open for 3% of the time, Pallas kernels for 9%

profile of v2, /device:TPU:32, one launch (start us, length us, event | category | flops | bytes accessed | tf_op | source)
XLA Modules:
  0.0 98.4 jit_solution(4274251295142337979)
XLA Ops:
  0.6 1.6 %collective-permute-start.4 = (bf16[128,1152]{1,0:T(8,128)(2,1)}, bf16[128,1152]{1,0:T(8,128)(2,1)S(1)}, u32[]{:S(2)}, u32[]{:S(2)}) collective-permute-start(bf16[128,1152]{1,0:T(8,128)(2,1)} %bitcast.49), channel_id=1, source_target_pairs={{0,0},{1,128},{128,1},{129,129},{2,2},{3,130},{130,3},{131,131},{4... | collective-permute-start | bytes 884744 | tf_op jit(solution)/shard_map/ppermute | solution.py:16
  2.3 1.6 %collective-permute-start = (bf16[128,1152]{1,0:T(8,128)(2,1)}, bf16[128,1152]{1,0:T(8,128)(2,1)S(1)}, u32[]{:S(2)}, u32[]{:S(2)}) collective-permute-start(bf16[128,1152]{1,0:T(8,128)(2,1)} %bitcast.50), channel_id=1, source_target_pairs={{0,0},{1,128},{128,1},{129,129},{2,2},{3,130},{130,3},{131,131},{4... | collective-permute-start | bytes 884744 | tf_op jit(solution)/shard_map/ppermute | solution.py:16
  3.9 1.6 %collective-permute-start.5 = (bf16[128,1152]{1,0:T(8,128)(2,1)S(1)}, bf16[128,1152]{1,0:T(8,128)(2,1)S(1)}, u32[]{:S(2)}, u32[]{:S(2)}) collective-permute-start(bf16[128,1152]{1,0:T(8,128)(2,1)S(1)} %collective-permute-done.4.t0), channel_id=1, source_target_pairs={{0,32},{32,64},{64,96},{96,0},{1,33},{33,65},{65,97},{97,1},{2,34}... | collective-permute-start | bytes 884744 | tf_op jit(solution)/shard_map/ppermute | solution.py:24
  5.4 1.7 %collective-permute-start.6 = (bf16[128,1152]{1,0:T(8,128)(2,1)S(1)}, bf16[128,1152]{1,0:T(8,128)(2,1)S(1)}, u32[]{:S(2)}, u32[]{:S(2)}) collective-permute-start(bf16[128,1152]{1,0:T(8,128)(2,1)S(1)} %collective-permute-done.4.t0), channel_id=1, source_target_pairs={{0,96},{32,0},{64,32},{96,64},{1,97},{33,1},{65,33},{97,65},{2,98}... | collective-permute-start | bytes 884744 | tf_op jit(solution)/shard_map/ppermute | solution.py:24
  7.1 2.0 %collective-permute-start.7 = (bf16[128,1152]{1,0:T(8,128)(2,1)S(1)}, bf16[128,1152]{1,0:T(8,128)(2,1)S(1)}, u32[]{:S(2)}, u32[]{:S(2)}) collective-permute-start(bf16[128,1152]{1,0:T(8,128)(2,1)S(1)} %collective-permute-done.4.t0), channel_id=1, source_target_pairs={{0,64},{32,96},{64,0},{96,32},{1,65},{33,97},{65,1},{97,33},{2,66}... | collective-permute-start | bytes 884744 | tf_op jit(solution)/shard_map/ppermute | solution.py:24
  10.5 0.7 collective-permute-start.1
  11.2 2.6 %collective-permute-start.2 = (bf16[128,1152]{1,0:T(8,128)(2,1)S(1)}, bf16[128,1152]{1,0:T(8,128)(2,1)S(1)}, u32[]{:S(2)}, u32[]{:S(2)}) collective-permute-start(bf16[128,1152]{1,0:T(8,128)(2,1)S(1)} %collective-permute-done.i0), channel_id=1, source_target_pairs={{0,96},{32,0},{64,32},{96,64},{1,97},{33,1},{65,33},{97,65},{2,98}... | collective-permute-start | bytes 884744 | tf_op jit(solution)/shard_map/ppermute | solution.py:24
  13.8 0.3 collective-permute-start.3
  14.1 2.9 %collective-permute-done.7.t3 = bf16[128,1152]{1,0:T(8,128)(2,1)S(1)} collective-permute-done((bf16[128,1152]{1,0:T(8,128)(2,1)S(1)}, bf16[128,1152]{1,0:T(8,128)(2,1)S(1)}, u32[]{:S(2)}, u32[]{:S(2)}) %collective-permute-start.7) | collective-permute-done | bytes 294944 | tf_op jit(solution)/shard_map/ppermute | solution.py:24
  17.0 1.7 %copy-done = bf16[1152,1152]{1,0:T(8,128)(2,1)S(1)} copy-done((bf16[1152,1152]{1,0:T(8,128)(2,1)S(1)}, bf16[1152,1152]{1,0:T(8,128)(2,1)}, u32[]{:S(2)}) %copy-start) | copy-done | bytes 2654232
  18.7 2.7 %shard_map.102 = (bf16[512,1152]{1,0:T(8,128)(2,1)S(1)}, bf16[512,1152]{1,0:T(8,128)(2,1)S(1)}, f32[512,384]{1,0:T(8,128)S(1)}, f32[512,128]{1,0:T(8,128)S(1)}) custom-call(s32[2]{0:T(128)S(1)} %pad_add_fusion.ids, bf16[128,1152]{1,0:T(8,128)(2,1)S(1)} %collective-permute-done.4.t0, bf16[128,1152]{1,0:T(8,128)(2,1)S(1)} %collective-permute-done.5.t1, ...), custom_call_target="tpu_custom_call" | custom-call | flops 27179089920 | tf_op jit(solution)/shard_map/pallas_call | solution.py:212
  21.5 11.3 %collective-permute-start.8 = (bf16[512,1152]{1,0:T(8,128)(2,1)S(1)}, bf16[512,1152]{1,0:T(8,128)(2,1)S(1)}, u32[]{:S(2)}, u32[]{:S(2)}) collective-permute-start(bf16[512,1152]{1,0:T(8,128)(2,1)S(1)} %get-tuple-element.27.own), channel_id=1, source_target_pairs={{0,1},{1,0},{2,3},{3,2},{4,5},{5,4},{6,7},{7,6},{8,9},{9,8},{10,11... | collective-permute-start | bytes 3538952 | tf_op jit(solution)/shard_map/ppermute | solution.py:20
  32.8 2.7 %shard_map.101 = (bf16[512,1152]{1,0:T(8,128)(2,1)S(1)}, bf16[512,1152]{1,0:T(8,128)(2,1)S(1)}, f32[512,384]{1,0:T(8,128)S(1)}, f32[512,128]{1,0:T(8,128)S(1)}) custom-call(s32[2]{0:T(128)S(1)} %pad_add_fusion.ids, bf16[128,1152]{1,0:T(8,128)(2,1)S(1)} %collective-permute-done.i0, bf16[128,1152]{1,0:T(8,128)(2,1)S(1)} %collective-permute-done.1.i1, ...), custom_call_target="tpu_custom_call" | custom-call | flops 27179089920 | tf_op jit(solution)/shard_map/pallas_call | solution.py:212
  35.6 4.2 %shard_map.103 = (bf16[512,1024]{1,0:T(8,128)(2,1)S(1)}, f32[512,128]{1,0:T(8,128)S(1)}, f32[512,128]{1,0:T(8,128)S(1)}, f32[512,512]{1,0:T(8,128)S(1)}, f32[128,1152]{1,0:T(8,128)S(1)}, /*index=5*/f32[8,128]{1,0:T(8,128)S(1)}) custom-call(s32[2]{0:T(128)S(1)} %pad_add_fusion.ids, f32[2]{0:T(128)S(1)} %pad_maximum_fusion.1.scal, ...), custom_call_target="tpu_custom_call" | custom-call | tf_op jit(solution)/shard_map/pallas_call | solution.py:212
  39.7 2.5 %collective-permute-start.11 = (f32[512,512]{1,0:T(8,128)S(1)}, f32[512,512]{1,0:T(8,128)S(1)}, u32[]{:S(2)}, u32[]{:S(2)}) collective-permute-start(f32[512,512]{1,0:T(8,128)S(1)} %get-tuple-element.39), channel_id=1, source_target_pairs={{0,1},{1,0},{2,3},{3,2},{4,5},{5,4},{6,7},{7,6},{8,9},{9,8},{10,11... | collective-permute-start | bytes 3145736 | tf_op jit(solution)/shard_map/ppermute | solution.py:20
  42.3 3.9 %shard_map.104 = (f32[1152,384]{1,0:T(8,128)S(1)}, f32[512,384]{1,0:T(8,128)S(1)}, bf16[128,1152]{1,0:T(8,128)(2,1)S(1)}, f32[128,1152]{1,0:T(8,128)S(1)}) custom-call(s32[2]{0:T(128)S(1)} %pad_add_fusion.ids, f32[2]{0:T(128)S(1)} %pad_maximum_fusion.1.scal, bf16[512,1152]{1,0:T(8,128)(2,1)S(1)} %get-tuple-element.33.cat, ...), custom_call_target="tpu_custom_call" | custom-call | tf_op jit(solution)/shard_map/pallas_call | solution.py:212
  46.2 1.8 %shard_map.105 = (bf16[16,36,640]{2,1,0:T(8,128)(2,1)S(1)}, f32[16,36,640]{2,1,0:T(8,128)S(1)}, bf16[128,1152]{1,0:T(8,128)(2,1)S(1)}) custom-call(s32[2]{0:T(128)S(1)} %pad_add_fusion.ids, f32[2]{0:T(128)S(1)} %pad_maximum_fusion.1.scal, bf16[512,1152]{1,0:T(8,128)(2,1)S(1)} %get-tuple-element.29.cat, f32[512,384]{1,0:T(8,128)S(1)} %get-tuple-element.30.window, ...), custom_call_target="tpu_custom_call" | custom-call | tf_op jit(solution)/shard_map/pallas_call | solution.py:212
  48.1 0.5 collective-permute-start.13
  48.6 1.8 %collective-permute-done.13 = bf16[16,36,640]{2,0,1:T(8,128)(2,1)S(1)} collective-permute-done((bf16[16,36,640]{2,0,1:T(8,128)(2,1)S(1)}, bf16[16,36,640]{2,0,1:T(8,128)(2,1)S(1)}, u32[]{:S(2)}, u32[]{:S(2)}) %collective-permute-start.13) | collective-permute-done | bytes 737312 | tf_op jit(solution)/shard_map/ppermute | solution.py:20
  50.4 1.2 %add_convert_fusion = bf16[16,36,640]{2,1,0:T(8,128)(2,1)} fusion(f32[16,36,640]{2,1,0:T(8,128)S(1)} %get-tuple-element.43, bf16[16,36,640]{2,0,1:T(8,128)(2,1)S(1)} %collective-permute-done.13), kind=kLoop, calls=%fused_computation | loop fusion | flops 1105920 | bytes 2949120 | tf_op jit(solution)/shard_map/convert_element_type | solution.py:265
  51.6 9.5 %all-to-all-start = ((bf16[16,36,640]{2,1,0:T(8,128)(2,1)}), bf16[16,36,640]{2,1,0:T(8,128)(2,1)S(1)}, u32[]{:S(2)}, u32[]{:S(2)}) async-start(bf16[16,36,640]{2,1,0:T(8,128)(2,1)} %add_convert_fusion), calls=%async_computation | async-start | bytes 1638400 | tf_op jit(solution)/shard_map/all_to_all | solution.py:266
  61.1 0.7 collective-permute-start.14
  61.9 3.6 %collective-permute-start.9 = (f32[8,128]{1,0:T(8,128)S(1)}, f32[8,128]{1,0:T(8,128)S(1)}, u32[]{:S(2)}, u32[]{:S(2)}) collective-permute-start(f32[8,128]{1,0:T(8,128)S(1)} %get-tuple-element.28), channel_id=1, source_target_pairs={{0,1},{1,0},{2,3},{3,2},{4,5},{5,4},{6,7},{7,6},{8,9},{9,8},{10,11... | collective-permute-start | bytes 12296 | tf_op jit(solution)/shard_map/ppermute | solution.py:20
  65.4 0.8 collective-permute-done.9
  66.3 0.6 collective-permute-start.10
  66.9 0.5 slice.45
  67.4 15.7 %all-to-all-done = bf16[16,36,640]{2,1,0:T(8,128)(2,1)S(1)} async-done(((bf16[16,36,640]{2,1,0:T(8,128)(2,1)}), bf16[16,36,640]{2,1,0:T(8,128)(2,1)S(1)}, u32[]{:S(2)}, u32[]{:S(2)}) %all-to-all-start) | async-done | bytes 737312 | tf_op jit(solution)/shard_map/all_to_all | solution.py:266
  83.3 0.8 broadcast_in_dim.12
  84.1 4.1 %all-to-all-start.1 = ((bf16[8,36,640]{2,1,0:T(8,128)(2,1)}), bf16[8,36,640]{2,1,0:T(8,128)(2,1)S(1)}, u32[]{:S(2)}, u32[]{:S(2)}) async-start(bf16[8,36,640]{2,1,0:T(8,128)(2,1)} %broadcast_in_dim.12), calls=%async_computation.1 | async-start | bytes 819200 | tf_op jit(solution)/shard_map/all_to_all | solution.py:268
  88.2 0.9 slice_bitcast_fusion
  89.0 8.5 %all-to-all-done.1 = bf16[8,36,640]{2,1,0:T(8,128)(2,1)S(1)} async-done(((bf16[8,36,640]{2,1,0:T(8,128)(2,1)}), bf16[8,36,640]{2,1,0:T(8,128)(2,1)S(1)}, u32[]{:S(2)}, u32[]{:S(2)}) %all-to-all-start.1) | async-done | bytes 368672 | tf_op jit(solution)/shard_map/all_to_all | solution.py:268
  97.8 0.6 copy-done.3
  (36 shorter events, 0.8 us)
Async XLA Ops:
  0.6 3.2 %collective-permute-start.4 = (bf16[128,1152]{1,0:T(8,128)(2,1)}, bf16[128,1152]{1,0:T(8,128)(2,1)S(1)}, u32[]{:S(2)}, u32[]{:S(2)}) collective-permute-start(bf16[128,1152]{1,0:T(8,128)(2,1)} %bitcast.49), channel_id=1, source_target_pairs={{0,0},{1,128},{128,1},{129,129},{2,2},{3,130},{130,3},{131,131},{4... | collective-permute-start | bytes 884744 | tf_op jit(solution)/shard_map/ppermute | solution.py:16
  2.3 8.3 %collective-permute-start = (bf16[128,1152]{1,0:T(8,128)(2,1)}, bf16[128,1152]{1,0:T(8,128)(2,1)S(1)}, u32[]{:S(2)}, u32[]{:S(2)}) collective-permute-start(bf16[128,1152]{1,0:T(8,128)(2,1)} %bitcast.50), channel_id=1, source_target_pairs={{0,0},{1,128},{128,1},{129,129},{2,2},{3,130},{130,3},{131,131},{4... | collective-permute-start | bytes 884744 | tf_op jit(solution)/shard_map/ppermute | solution.py:16
  3.9 9.9 %collective-permute-start.5 = (bf16[128,1152]{1,0:T(8,128)(2,1)S(1)}, bf16[128,1152]{1,0:T(8,128)(2,1)S(1)}, u32[]{:S(2)}, u32[]{:S(2)}) collective-permute-start(bf16[128,1152]{1,0:T(8,128)(2,1)S(1)} %collective-permute-done.4.t0), channel_id=1, source_target_pairs={{0,32},{32,64},{64,96},{96,0},{1,33},{33,65},{65,97},{97,1},{2,34}... | collective-permute-start | bytes 884744 | tf_op jit(solution)/shard_map/ppermute | solution.py:24
  5.4 8.7 %collective-permute-start.6 = (bf16[128,1152]{1,0:T(8,128)(2,1)S(1)}, bf16[128,1152]{1,0:T(8,128)(2,1)S(1)}, u32[]{:S(2)}, u32[]{:S(2)}) collective-permute-start(bf16[128,1152]{1,0:T(8,128)(2,1)S(1)} %collective-permute-done.4.t0), channel_id=1, source_target_pairs={{0,96},{32,0},{64,32},{96,64},{1,97},{33,1},{65,33},{97,65},{2,98}... | collective-permute-start | bytes 884744 | tf_op jit(solution)/shard_map/ppermute | solution.py:24
  7.1 9.9 %collective-permute-start.7 = (bf16[128,1152]{1,0:T(8,128)(2,1)S(1)}, bf16[128,1152]{1,0:T(8,128)(2,1)S(1)}, u32[]{:S(2)}, u32[]{:S(2)}) collective-permute-start(bf16[128,1152]{1,0:T(8,128)(2,1)S(1)} %collective-permute-done.4.t0), channel_id=1, source_target_pairs={{0,64},{32,96},{64,0},{96,32},{1,65},{33,97},{65,1},{97,33},{2,66}... | collective-permute-start | bytes 884744 | tf_op jit(solution)/shard_map/ppermute | solution.py:24
  10.5 22.2 %collective-permute-start.1 = (bf16[128,1152]{1,0:T(8,128)(2,1)S(1)}, bf16[128,1152]{1,0:T(8,128)(2,1)S(1)}, u32[]{:S(2)}, u32[]{:S(2)}) collective-permute-start(bf16[128,1152]{1,0:T(8,128)(2,1)S(1)} %collective-permute-done.i0), channel_id=1, source_target_pairs={{0,32},{32,64},{64,96},{96,0},{1,33},{33,65},{65,97},{97,1},{2,34}... | collective-permute-start | bytes 884744 | tf_op jit(solution)/shard_map/ppermute | solution.py:24
  11.2 21.5 %collective-permute-start.2 = (bf16[128,1152]{1,0:T(8,128)(2,1)S(1)}, bf16[128,1152]{1,0:T(8,128)(2,1)S(1)}, u32[]{:S(2)}, u32[]{:S(2)}) collective-permute-start(bf16[128,1152]{1,0:T(8,128)(2,1)S(1)} %collective-permute-done.i0), channel_id=1, source_target_pairs={{0,96},{32,0},{64,32},{96,64},{1,97},{33,1},{65,33},{97,65},{2,98}... | collective-permute-start | bytes 884744 | tf_op jit(solution)/shard_map/ppermute | solution.py:24
  13.8 19.0 %collective-permute-start.3 = (bf16[128,1152]{1,0:T(8,128)(2,1)S(1)}, bf16[128,1152]{1,0:T(8,128)(2,1)S(1)}, u32[]{:S(2)}, u32[]{:S(2)}) collective-permute-start(bf16[128,1152]{1,0:T(8,128)(2,1)S(1)} %collective-permute-done.i0), channel_id=1, source_target_pairs={{0,64},{32,96},{64,0},{96,32},{1,65},{33,97},{65,1},{97,33},{2,66}... | collective-permute-start | bytes 884744 | tf_op jit(solution)/shard_map/ppermute | solution.py:24
  17.0 1.8 %copy-start = (bf16[1152,1152]{1,0:T(8,128)(2,1)S(1)}, bf16[1152,1152]{1,0:T(8,128)(2,1)}, u32[]{:S(2)}) copy-start(bf16[1152,1152]{1,0:T(8,128)(2,1)} %weight.3) | copy-start | bytes 7962628
  18.7 14.0 %copy-start.1 = (bf16[1152,1152]{1,0:T(8,128)(2,1)S(1)}, bf16[1152,1152]{1,0:T(8,128)(2,1)}, u32[]{:S(2)}) copy-start(bf16[1152,1152]{1,0:T(8,128)(2,1)} %weight.2) | copy-start | bytes 7962628
  21.5 14.1 %collective-permute-start.8 = (bf16[512,1152]{1,0:T(8,128)(2,1)S(1)}, bf16[512,1152]{1,0:T(8,128)(2,1)S(1)}, u32[]{:S(2)}, u32[]{:S(2)}) collective-permute-start(bf16[512,1152]{1,0:T(8,128)(2,1)S(1)} %get-tuple-element.27.own), channel_id=1, source_target_pairs={{0,1},{1,0},{2,3},{3,2},{4,5},{5,4},{6,7},{7,6},{8,9},{9,8},{10,11... | collective-permute-start | bytes 3538952 | tf_op jit(solution)/shard_map/ppermute | solution.py:20
  39.7 6.5 %collective-permute-start.11 = (f32[512,512]{1,0:T(8,128)S(1)}, f32[512,512]{1,0:T(8,128)S(1)}, u32[]{:S(2)}, u32[]{:S(2)}) collective-permute-start(f32[512,512]{1,0:T(8,128)S(1)} %get-tuple-element.39), channel_id=1, source_target_pairs={{0,1},{1,0},{2,3},{3,2},{4,5},{5,4},{6,7},{7,6},{8,9},{9,8},{10,11... | collective-permute-start | bytes 3145736 | tf_op jit(solution)/shard_map/ppermute | solution.py:20
  42.2 4.0 %collective-permute-start.12 = (f32[128,1152]{1,0:T(8,128)S(1)}, f32[128,1152]{1,0:T(8,128)S(1)}, u32[]{:S(2)}, u32[]{:S(2)}) collective-permute-start(f32[128,1152]{1,0:T(8,128)S(1)} %get-tuple-element.41), channel_id=1, source_target_pairs={{0,1},{1,0},{2,3},{3,2},{4,5},{5,4},{6,7},{7,6},{8,9},{9,8},{10,11... | collective-permute-start | bytes 1769480 | tf_op jit(solution)/shard_map/ppermute | solution.py:20
  48.1 2.3 %collective-permute-start.13 = (bf16[16,36,640]{2,0,1:T(8,128)(2,1)S(1)}, bf16[16,36,640]{2,0,1:T(8,128)(2,1)S(1)}, u32[]{:S(2)}, u32[]{:S(2)}) collective-permute-start(bf16[16,36,640]{2,0,1:T(8,128)(2,1)S(1)} %copy.11), channel_id=1, source_target_pairs={{0,1},{1,0},{2,3},{3,2},{4,5},{5,4},{6,7},{7,6},{8,9},{9,8},{10,11... | collective-permute-start | bytes 2211848 | tf_op jit(solution)/shard_map/ppermute | solution.py:20
  51.6 31.6 %all-to-all-start = ((bf16[16,36,640]{2,1,0:T(8,128)(2,1)}), bf16[16,36,640]{2,1,0:T(8,128)(2,1)S(1)}, u32[]{:S(2)}, u32[]{:S(2)}) async-start(bf16[16,36,640]{2,1,0:T(8,128)(2,1)} %add_convert_fusion), calls=%async_computation | async-start | bytes 1638400 | tf_op jit(solution)/shard_map/all_to_all | solution.py:266
  61.1 27.0 %collective-permute-start.14 = (bf16[256,1152]{1,0:T(8,128)(2,1)S(1)}, bf16[256,1152]{1,0:T(8,128)(2,1)S(1)}, u32[]{:S(2)}, u32[]{:S(2)}) collective-permute-start(bf16[256,1152]{1,0:T(8,128)(2,1)S(1)} %pad_maximum_fusion), channel_id=1, source_target_pairs={{0,0},{1,128},{128,1},{129,129},{2,2},{3,130},{130,3},{131,131},{4... | collective-permute-start | bytes 1769480 | tf_op jit(solution)/shard_map/ppermute | solution.py:16
  61.9 4.4 %collective-permute-start.9 = (f32[8,128]{1,0:T(8,128)S(1)}, f32[8,128]{1,0:T(8,128)S(1)}, u32[]{:S(2)}, u32[]{:S(2)}) collective-permute-start(f32[8,128]{1,0:T(8,128)S(1)} %get-tuple-element.28), channel_id=1, source_target_pairs={{0,1},{1,0},{2,3},{3,2},{4,5},{5,4},{6,7},{7,6},{8,9},{9,8},{10,11... | collective-permute-start | bytes 12296 | tf_op jit(solution)/shard_map/ppermute | solution.py:20
  66.3 0.7 collective-permute-start.10
  84.1 13.4 %all-to-all-start.1 = ((bf16[8,36,640]{2,1,0:T(8,128)(2,1)}), bf16[8,36,640]{2,1,0:T(8,128)(2,1)S(1)}, u32[]{:S(2)}, u32[]{:S(2)}) async-start(bf16[8,36,640]{2,1,0:T(8,128)(2,1)} %broadcast_in_dim.12), calls=%async_computation.1 | async-start | bytes 819200 | tf_op jit(solution)/shard_map/all_to_all | solution.py:268
  97.7 0.7 copy-start.3
  97.7 0.7 copy-start.2

commit v3 on v2

v3 whole, which is shorter than its diff:
```python
import jax
import jax.numpy as jnp
from jax import lax
from jax.experimental import pallas as pl
from jax.experimental.pallas import tpu as pltpu
from jax.sharding import Mesh, PartitionSpec as P

epsilon = 1e-06
AXES = ("xh", "y", "xl", "z", "c")
XH, Y, XL, Z, C = 2, 4, 2, 8, 2
WIDE, SLIM, PACK, TERMS = 256, 128, 192, 16
f32, bf16 = jnp.float32, jnp.bfloat16


def trade(x):
    return lax.ppermute(x, ("xh", "c"), [(0, 0), (1, 2), (2, 1), (3, 3)])


def other_core(x):
    return lax.ppermute(x, "c", [(0, 1), (1, 0)])


def from_y(x, k):
    return lax.ppermute(x, "y", [(i, (i + k) % Y) for i in range(Y)])


def gather(own):
    return own, from_y(own, 1), from_y(own, -1), from_y(own, 2)


def dot(a, b):
    return lax.dot_general(a, b, (((1,), (0,)), ((), ())), preferred_element_type=f32)


def dot_cols(a, b):
    return lax.dot_general(a, b, (((1,), (1,)), ((), ())), preferred_element_type=f32)


def image_start(y):
    return pl.multiple_of(y * WIDE + jnp.where(y > 0, SLIM, 0), SLIM)


def text_start(y):
    return pl.multiple_of(y * WIDE, WIDE)


def join(parts, whole):
    at = 0
    for part in parts:
        whole[at : at + part.shape[0], :] = part[...]
        at += part.shape[0]


def finish(pre, square, emb, window, inv, unit, start, extra):
    inverse = lax.rsqrt(square + epsilon)
    value = pre * inverse
    unit[...] = value
    emb[...] = value.astype(bf16)
    inv[...] = jnp.broadcast_to(inverse, inv.shape)
    window[:, :WIDE] = unit[:, pl.ds(start, WIDE)]
    window[:, WIDE:] = unit[:, extra : extra + SLIM]


def text_kernel(ids, *refs):
    *pieces, weight, turned, emb, window, inv, joined, unit, held, arrived = refs
    copy = pltpu.make_async_copy(weight, held, arrived)
    copy.start()
    join(pieces, joined)
    features = joined[...]
    turned[...] = features.T
    copy.wait()
    pre = dot(features, held[...])
    square = jnp.sum(pre * pre, axis=1, keepdims=True)
    finish(pre, square, emb, window, inv, unit, text_start(ids[0]), weight.shape[1] - SLIM)


def image_kernel(ids, *refs):
    *pieces, weight, turned, emb, window, inv, joined, unit = refs
    join(pieces, joined)
    features = joined[...]
    pre = dot(features, weight[...])
    square = jnp.sum(pre * pre, axis=1, keepdims=True)
    finish(pre, square, emb, window, inv, unit, image_start(ids[0]), WIDE)
    turned[...] = features.T


def fold(x, combine):
    while x.shape[0] > 8:
        half = x.shape[0] // 2
        x = combine(x[:half], x[half:])
    return x


def stack(refs):
    return jnp.concatenate([ref[...] for ref in refs], axis=0)


def slope_kernel(
    ids, scal, far, weight, early, own, other,
    emb, turned, window, inv, slopes, slopes_turned, radial, text_radial, give, loss,
    late, joined, unit,
):
    y = ids[0]
    scale, bias = scal[0], scal[1]
    image_kernel(ids, far, weight, turned, late, window, inv, joined, unit)
    rows = emb.shape[0]
    join((early, late), emb)
    embedded = emb[...]
    lost = jnp.zeros((8, WIDE), f32)
    along = [jnp.zeros((WIDE, WIDE), f32) for _ in range(0, rows, WIDE)]
    for j in reversed(range(0, 2 * rows, WIDE)):
        mine = j < rows
        side, at = (own, j) if mine else (other, j - rows)
        cosines = dot_cols(embedded, side[at : at + WIDE, :])
        down = jnp.zeros((8, WIDE), f32)
        for i in range(0, rows, WIDE):
            cosine = cosines[i : i + WIDE]
            logits = scale * cosine + bias
            diagonal = mine and i == at
            if diagonal:
                same = lax.broadcasted_iota(jnp.int32, logits.shape, 0) == lax.broadcasted_iota(
                    jnp.int32, logits.shape, 1
                )
                logits = jnp.where(same, -logits, logits)
            small = jnp.exp(-jnp.abs(logits))
            whole = 1.0 + small
            slope = jnp.where(logits >= 0, 1.0, small) * pl.reciprocal(whole, approx=True)
            if diagonal:
                slope = jnp.where(same, -slope, slope)
            slope = slope.astype(bf16)
            lost = lost + fold(jnp.maximum(logits, 0.0), jnp.add) + jnp.log(fold(whole, jnp.multiply))
            slopes[i : i + WIDE, j : j + WIDE] = slope
            slopes_turned[j : j + WIDE, i : i + WIDE] = slope.T
            weighted = slope.astype(f32) * cosine
            along[i // WIDE] = along[i // WIDE] + weighted
            down = down + fold(weighted, jnp.add)
        down = jnp.sum(down, axis=0, keepdims=True)
        down = jnp.transpose(jnp.broadcast_to(down, (SLIM, WIDE)))
        if mine:
            text_radial[at : at + WIDE, :] = down
        else:
            give[at : at + WIDE, WIDE + SLIM :] = down
    for i, part in enumerate(along):
        part = jnp.sum(part, axis=1, keepdims=True)
        radial[i * WIDE : (i + 1) * WIDE, :] = jnp.broadcast_to(part, (WIDE, SLIM))
    loss[...] = jnp.broadcast_to(jnp.sum(lost, keepdims=True), loss.shape)
    give[:, :WIDE] = dot(slopes_turned[rows:, :], emb[:, pl.ds(text_start(y), WIDE)])

    @pl.when(y == Y - 1)
    def _():
        give[:, WIDE : WIDE + SLIM] = dot(slopes_turned[rows:, :], emb[:, emb.shape[1] - SLIM :])

    @pl.when(y != Y - 1)
    def _():
        give[:, WIDE : WIDE + SLIM] = jnp.zeros((rows, SLIM), f32)


def wide(x, n):
    return jnp.concatenate([x] * (n // x.shape[1]), axis=1)


def back(grad, window, radial, inv):
    n = grad.shape[1]
    return ((grad - window * wide(radial, n)) * wide(inv, n)).astype(bf16)


def outer(turned, grad):
    return dot(jnp.concatenate([part[...] for part in turned], axis=1), grad)


def grad_kernel(
    ids, scal, f0, f1, w0, w1, v0, v1, emb, slopes, slopes_turned, radial, own, other,
    term, part,
):
    y = ids[0]
    scale = scal[0]
    rows = emb.shape[0]
    window, inv = stack((w0, w1)), stack((v0, v1))

    def columns(cols, at, size):
        grad = scale * (dot(slopes[:, :rows], own[:, cols]) + dot(slopes[:, rows:], other[:, cols]))
        grad = back(grad, window[:, at : at + size], scale * radial[...], inv)
        term[:, at : at + size] = outer((f0, f1), grad)

    columns(pl.ds(image_start(y), WIDE), 0, WIDE)
    part[:, :WIDE] = dot(slopes_turned[:rows, :], emb[:, pl.ds(text_start(y), WIDE)])

    @pl.when(y == 0)
    def _():
        columns(slice(WIDE, WIDE + SLIM), WIDE, SLIM)

    @pl.when(y == Y - 1)
    def _():
        part[:, WIDE:] = dot(slopes_turned[:rows, :], emb[:, emb.shape[1] - SLIM :])

    @pl.when(y != Y - 1)
    def _():
        part[:, WIDE:] = jnp.zeros((rows, SLIM), f32)


def sum_kernel(
    ids, scal, turned, window, inv, text_radial, part, got, image_term,
    give, keep, token, term,
):
    y, c = ids[0], ids[1]
    scale = scal[0]
    grad = scale * (part[...] + got[:, : WIDE + SLIM])
    radial = scale * (text_radial[...] + got[:, WIDE + SLIM :])
    grad = back(grad, window[...], radial, inv[...])
    term[:, :WIDE] = dot(turned[...], grad[:, :WIDE])

    @pl.when(y == Y - 1)
    def _():
        term[:, WIDE:] = dot(turned[...], grad[:, WIDE:])

    @pl.when(y == 0)
    def _():
        term[:, WIDE:] = image_term[:, WIDE:]

    @pl.when((y != 0) & (y != Y - 1))
    def _():
        term[:, WIDE:] = jnp.zeros((term.shape[0], SLIM), f32)

    token[...] = jnp.zeros(token.shape, f32)
    for k in range(XL * Z):
        for core, out in ((c, keep), (1 - c, give)):
            packed = pack(image_term, term, k, core).astype(out.dtype)
            out[k] = packed


def pack(image_term, term, k, core):
    tiles = [(image_term, 0), (image_term, SLIM), (term, 0), (term, SLIM), (term, 2 * SLIM)]
    base = 72 * k
    whole = pl.ds(pl.multiple_of(base + 40 * core, 8), 32)
    parts = [source[whole, col : col + SLIM] for source, col in tiles]
    split = [source[base + 32 : base + 40, col : col + SLIM] for source, col in tiles]
    owned = lax.broadcasted_iota(jnp.int32, (8, SLIM), 0) // 4 == core
    parts += [jnp.where(owned, split[i], pltpu.roll(split[i + 1], 4, 0)) for i in (0, 2)]
    parts += [split[4], jnp.zeros((8, SLIM), f32)]
    return jnp.concatenate(parts, axis=0)


def add_kernel(keep, got, mine, token):
    token[...] = jnp.zeros(token.shape, f32)
    mine[...] = (keep[...] + got[...].astype(f32)).astype(bf16)


def spread_kernel(parts, spread):
    summed = jnp.sum(parts[...].astype(f32), axis=0).astype(bf16)
    for i in range(spread.shape[0]):
        spread[i] = summed


def unpack_kernel(ids, spread, outs, image_out, text_out, loss, image_emb_out, text_emb_out):
    core = ids[1]
    n = image_emb_out.shape[1]
    image_emb_out[0] = outs[:n, :]
    text_emb_out[0] = outs[n : 2 * n, :]
    loss[0] = jnp.sum(outs[2 * n :, :SLIM].astype(f32)[:, :1])

    def place(c):
        for y in range(Y):
            rows = spread[y].astype(f32) + spread[Y + y].astype(f32)
            for tile in range(5):
                if tile < 2:
                    out, col = image_out, 2 * y + tile + (1 if y > 0 else 0)
                elif tile < 4:
                    out, col = text_out, 2 * y + tile - 2
                elif y == 0:
                    out, col = image_out, 2
                elif y == Y - 1:
                    out, col = text_out, 2 * Y
                else:
                    continue
                cols = slice(col * SLIM, (col + 1) * SLIM)
                shared = 160 + 8 * (tile // 2) + 4 * (c if tile % 2 == 0 else 1 - c)
                out[4 * c : 4 * c + 32, cols] = rows[32 * tile : 32 * tile + 32]
                out[32 * (1 - c) : 32 * (1 - c) + 4, cols] = rows[shared : shared + 4]

    for c in range(C):
        pl.when(core == c)(lambda c=c: place(c))


def rest_kernel(slopes_turned, emb, loss, after, give):
    del after
    n = give.shape[0] - 8
    rows = emb.shape[0]
    give[:n, :] = dot(slopes_turned[rows : rows + n, :], emb[...])
    give[n:, :] = jnp.broadcast_to(loss[:, :1], (8, give.shape[1]))


def out_kernel(scal, slopes, slopes_turned, emb, own, other, loss, got, after, out):
    del after
    scale = scal[0]
    n = got.shape[0] - 8
    rows = emb.shape[0]
    out[:n, :] = (scale * (dot(slopes[:n, :rows], own[...]) + dot(slopes[:n, rows:], other[...]))).astype(bf16)
    out[n : 2 * n, :] = (scale * (dot(slopes_turned[:n, :], emb[...]) + got[:n, :])).astype(bf16)
    left = (loss[:1, :1] + got[n : n + 1, :1]) * (1.0 / (C * rows))
    row = lax.broadcasted_iota(jnp.int32, (TERMS, out.shape[1]), 0)
    terms = jnp.zeros(row.shape, f32)
    for i in range(3):
        term = left.astype(bf16).astype(f32)
        terms = jnp.where(row == i, term, terms)
        left = left - term
    out[2 * n :, :] = terms.astype(bf16)


def call(kernel, outs, scratch=(), macs=0, far=None):
    def space(i, x):
        if i == far:
            return pltpu.HBM
        return pltpu.SMEM if x.ndim == 1 else pltpu.VMEM

    def run(*args):
        return pl.pallas_call(
            kernel,
            out_shape=[jax.ShapeDtypeStruct(s, d) for s, d in outs],
            in_specs=[pl.BlockSpec(memory_space=space(i, a)) for i, a in enumerate(args)],
            out_specs=[pl.BlockSpec(memory_space=pltpu.SMEM if len(s) == 1 else pltpu.VMEM) for s, _ in outs],
            scratch_shapes=list(scratch),
            compiler_params=pltpu.CompilerParams(vmem_limit_bytes=16 * 2**20),
            cost_estimate=pl.CostEstimate(flops=2 * macs, bytes_accessed=0, transcendentals=0),
        )(*args)

    return run


def on_device(image_feats, text_feats, image_proj, text_proj, logit_scale, logit_bias):
    c, y = lax.axis_index("c"), lax.axis_index("y")
    ids = jnp.stack([y, c]).astype(jnp.int32)
    scal = jnp.concatenate([logit_scale, logit_bias])
    n, depth = image_feats.shape[1:]
    width = image_proj.shape[1]
    rows = n * Y
    macs = 20 * rows * depth * width

    def projected(count):
        return [((depth, count), bf16), ((count, width), bf16), ((count, WIDE + SLIM), f32), ((count, SLIM), f32)]

    def scratch(count):
        return [pltpu.VMEM((count, depth), bf16), pltpu.VMEM((count, width), f32)]

    text = gather(trade(text_feats[0]))
    image = gather(trade(image_feats[0]))
    streams = [pltpu.VMEM((depth, width), bf16), pltpu.SemaphoreType.DMA]
    text_turned, text_emb, text_window, text_inv = call(
        text_kernel, projected(rows), scratch(rows) + streams, macs, len(text) + 1
    )(ids, *text, pltpu.with_memory_space_constraint(text_proj, pltpu.HBM))
    text_other = other_core(text_emb)
    turned_a, early, window_a, inv_a = call(image_kernel, projected(3 * n), scratch(3 * n), macs)(
        ids, *image[:3], image_proj
    )
    turned, _, window, inv = projected(n)
    emb, turned_b, window_b, inv_b, slopes, slopes_turned, radial, text_radial, give, loss = call(
        slope_kernel,
        [
            ((rows, width), bf16), turned, window, inv,
            ((rows, C * rows), bf16), ((C * rows, rows), bf16), ((rows, SLIM), f32), ((rows, SLIM), f32),
            ((rows, WIDE + 2 * SLIM), f32), ((8, SLIM), f32),
        ],
        [pltpu.VMEM((n, width), bf16)] + scratch(n),
        macs,
    )(ids, scal, *image[3:], image_proj, early, text_emb, text_other)
    got = other_core(give)
    image_term, part = call(grad_kernel, [((depth, WIDE + SLIM), f32), ((rows, WIDE + SLIM), f32)], (), macs)(
        ids, scal, turned_a, turned_b, window_a, window_b, inv_a, inv_b, emb, slopes, slopes_turned,
        radial, text_emb, text_other,
    )
    packed = (XL * Z, PACK, SLIM)
    give, keep, token = call(
        sum_kernel,
        [(packed, bf16), (packed, f32), ((8, SLIM), f32)],
        [pltpu.VMEM((depth, WIDE + SLIM), f32)],
    )(ids, scal, text_turned, text_window, text_inv, text_radial, part, got, image_term)
    mine, behind = call(add_kernel, [(packed, bf16), ((8, SLIM), f32)])(keep, other_core(give))
    arrived = lax.all_to_all(mine, ("xl", "z"), 0, 0)
    (spread,) = call(spread_kernel, [((XH * Y, PACK, SLIM), bf16)])(arrived)
    spread = lax.all_to_all(spread, ("xh", "y"), 0, 0)
    (give_rest,) = call(rest_kernel, [((n + 8, width), f32)], (), macs)(slopes_turned, emb, loss, token)
    (outs,) = call(out_kernel, [((2 * n + TERMS, width), bf16)], (), macs)(
        scal, slopes, slopes_turned, emb, text_emb, text_other, loss, other_core(give_rest), behind
    )
    outs = trade(outs)
    grad = (depth // (XL * Z * C), width), f32
    image_grad, text_grad, total, image_out, text_out = call(
        unpack_kernel, [grad, grad, ((1,), f32), ((1, n, width), bf16), ((1, n, width), bf16)]
    )(ids, spread, outs)
    return total, image_grad, text_grad, image_out, text_out


def solution(mesh):
    fine = Mesh(mesh.devices.reshape(XH, Y, XL, Z, C), AXES)
    dp, blk = ("xl", "z", "c"), ("xh", "y")
    in_specs = (P(dp, blk, None), P(dp, blk, None), P(), P(), P(), P())
    out_specs = (P(dp), P(dp, None), P(dp, None), P(dp, blk, None), P(dp, blk, None))
    return jax.shard_map(
        on_device, mesh=fine, in_specs=in_specs, out_specs=out_specs, check_vma=False
    )
```

time: 98.8 us -> 96.4 us (0.976)
  Pallas kernels: 15.3 us -> 22 us
  waiting for transfers between devices: 29.7 us -> 24.3 us
  starting transfers between devices: 45 us -> 42.1 us
  other arithmetic: 1.6 us -> 0.15 us
    pallas_call x5 -> x10, Pallas kernels: 15.3 us -> 22 us  [run(): pl.pallas_call(kernel, out_shape=[jax.ShapeDtypeStruct(s, d) for s, d in...]
    ppermute x5 -> x4, starting transfers between devices: 18 us -> 13.6 us  [other_core(): return lax.ppermute(x, 'c', [(0, 1), (1, 0)])]
    all_to_all x1, waiting for transfers between devices: 15.7 us -> 12.1 us  [on_device(): arrived = lax.all_to_all(mine, ('xl', 'z'), 0, 0)]
    unnamed x14 -> x18, local copies, waits for them, and re-layouts: 2.47 us -> 5 us
    ppermute x5 -> x4, waiting for transfers between devices: 2.67 us -> 0.75 us  [other_core(): return lax.ppermute(x, 'c', [(0, 1), (1, 0)])]
    broadcast_in_dim x2 -> x0, local copies, waits for them, and re-layouts: 1.66 us -> none  [the longest x1 0.86 us: on_device(): outs[n:][None]]
    ppermute x6, starting transfers between devices: 8.81 us -> 10.1 us  [from_y(): return lax.ppermute(x, 'y', [(i, (i + k) % Y) for i in range(Y)])]
    convert_element_type x2 -> x0, other arithmetic: 1.21 us -> none  [the longest x1 1.16 us: on_device(): mine = (keep + other_core(give).astype(f32)).astype(bf16)]
  transfers between devices with their start and end apart: 17 -> 15, of which waited for: 5 -> 6; matrix products, arithmetic and copies ran while one was open for 3% -> 0% of each run, Pallas kernels for 9% -> 16%
where the time goes in v3:
time: 96.4 us; the launch traced here: 95.8 us
  starting transfers between devices  42.1 us (44%)
  waiting for transfers between devices  24.3 us (25%)
  Pallas kernels  22 us (23%)
  local copies, waits for them, and re-layouts  5 us (5%)
  between operations  2.22 us (2%)
    pallas_call x10, Pallas kernels, run(): pl.pallas_call(kernel, out_shape=[jax.ShapeDtypeStruct(s, d) for s, d in...  22 us
    ppermute x4, starting transfers between devices, other_core(): return lax.ppermute(x, 'c', [(0, 1), (1, 0)])  13.6 us
    all_to_all x1, waiting for transfers between devices, on_device(): arrived = lax.all_to_all(mine, ('xl', 'z'), 0, 0)  12.1 us
    ppermute x6, starting transfers between devices, from_y(): return lax.ppermute(x, 'y', [(i, (i + k) % Y) for i in range(Y)])  10.1 us
    all_to_all x1, starting transfers between devices, on_device(): arrived = lax.all_to_all(mine, ('xl', 'z'), 0, 0)  9.51 us
    all_to_all x1, waiting for transfers between devices, on_device(): spread = lax.all_to_all(spread, ('xh', 'y'), 0, 0)  9.25 us
    unnamed x18, local copies, waits for them, and re-layouts  5 us
    ppermute x3, starting transfers between devices, trade(): return lax.ppermute(x, ('xh', 'c'), [(0, 0), (1, 2), (2, 1), (3, 3)])  4.95 us
  transfers between devices with their start and end apart: 15, of which 6 were waited for; matrix products, arithmetic and copies ran while one was open for 0% of the time, Pallas kernels for 16%

profile of v3, /device:TPU:32, one launch (start us, length us, event | category | flops | bytes accessed | tf_op | source)
XLA Modules:
  0.0 95.8 jit_solution(6758901156658812326)
XLA Ops:
  0.6 1.6 %collective-permute-start = (bf16[128,1152]{1,0:T(8,128)(2,1)}, bf16[128,1152]{1,0:T(8,128)(2,1)S(1)}, u32[]{:S(2)}, u32[]{:S(2)}) collective-permute-start(bf16[128,1152]{1,0:T(8,128)(2,1)} %bitcast.4), channel_id=1, source_target_pairs={{0,0},{1,128},{128,1},{129,129},{2,2},{3,130},{130,3},{131,131},{4... | collective-permute-start | bytes 884744 | tf_op jit(solution)/shard_map/ppermute | solution.py:16
  2.3 1.6 %collective-permute-start.4 = (bf16[128,1152]{1,0:T(8,128)(2,1)}, bf16[128,1152]{1,0:T(8,128)(2,1)S(1)}, u32[]{:S(2)}, u32[]{:S(2)}) collective-permute-start(bf16[128,1152]{1,0:T(8,128)(2,1)} %bitcast.5), channel_id=1, source_target_pairs={{0,0},{1,128},{128,1},{129,129},{2,2},{3,130},{130,3},{131,131},{4... | collective-permute-start | bytes 884744 | tf_op jit(solution)/shard_map/ppermute | solution.py:16
  3.9 3.2 %collective-permute-start.3 = (bf16[128,1152]{1,0:T(8,128)(2,1)S(1)}, bf16[128,1152]{1,0:T(8,128)(2,1)S(1)}, u32[]{:S(2)}, u32[]{:S(2)}) collective-permute-start(bf16[128,1152]{1,0:T(8,128)(2,1)S(1)} %collective-permute-done.refs_0_), channel_id=1, source_target_pairs={{0,64},{32,96},{64,0},{96,32},{1,65},{33,97},{65,1},{97,33},{2,66}... | collective-permute-start | bytes 884744 | tf_op jit(solution)/shard_map/ppermute | solution.py:24
  7.1 1.1 %collective-permute-start.2 = (bf16[128,1152]{1,0:T(8,128)(2,1)S(1)}, bf16[128,1152]{1,0:T(8,128)(2,1)S(1)}, u32[]{:S(2)}, u32[]{:S(2)}) collective-permute-start(bf16[128,1152]{1,0:T(8,128)(2,1)S(1)} %collective-permute-done.refs_0_), channel_id=1, source_target_pairs={{0,96},{32,0},{64,32},{96,64},{1,97},{33,1},{65,33},{97,65},{2,98}... | collective-permute-start | bytes 884744 | tf_op jit(solution)/shard_map/ppermute | solution.py:24
  8.1 1.0 %collective-permute-start.1 = (bf16[128,1152]{1,0:T(8,128)(2,1)S(1)}, bf16[128,1152]{1,0:T(8,128)(2,1)S(1)}, u32[]{:S(2)}, u32[]{:S(2)}) collective-permute-start(bf16[128,1152]{1,0:T(8,128)(2,1)S(1)} %collective-permute-done.refs_0_), channel_id=1, source_target_pairs={{0,32},{32,64},{64,96},{96,0},{1,33},{33,65},{65,97},{97,1},{2,34}... | collective-permute-start | bytes 884744 | tf_op jit(solution)/shard_map/ppermute | solution.py:24
  10.5 2.3 %collective-permute-start.7 = (bf16[128,1152]{1,0:T(8,128)(2,1)S(1)}, bf16[128,1152]{1,0:T(8,128)(2,1)S(1)}, u32[]{:S(2)}, u32[]{:S(2)}) collective-permute-start(bf16[128,1152]{1,0:T(8,128)(2,1)S(1)} %collective-permute-done.4.refs_0_), channel_id=1, source_target_pairs={{0,96},{32,0},{64,32},{96,64},{1,97},{33,1},{65,33},{97,65},{2,98}... | collective-permute-start | bytes 884744 | tf_op jit(solution)/shard_map/ppermute | solution.py:24
  12.8 2.6 %collective-permute-start.5 = (bf16[128,1152]{1,0:T(8,128)(2,1)S(1)}, bf16[128,1152]{1,0:T(8,128)(2,1)S(1)}, u32[]{:S(2)}, u32[]{:S(2)}) collective-permute-start(bf16[128,1152]{1,0:T(8,128)(2,1)S(1)} %collective-permute-done.4.refs_0_), channel_id=1, source_target_pairs={{0,64},{32,96},{64,0},{96,32},{1,65},{33,97},{65,1},{97,33},{2,66}... | collective-permute-start | bytes 884744 | tf_op jit(solution)/shard_map/ppermute | solution.py:24
  15.4 0.8 collective-permute-done.2.refs_2_
  16.2 1.4 %collective-permute-done.1.refs_1_ = bf16[128,1152]{1,0:T(8,128)(2,1)S(1)} collective-permute-done((bf16[128,1152]{1,0:T(8,128)(2,1)S(1)}, bf16[128,1152]{1,0:T(8,128)(2,1)S(1)}, u32[]{:S(2)}, u32[]{:S(2)}) %collective-permute-start.1) | collective-permute-done | bytes 294944 | tf_op jit(solution)/shard_map/ppermute | solution.py:24
  17.5 4.5 %shard_map.101 = (bf16[1152,512]{1,0:T(8,128)(2,1)S(1)}, bf16[512,1152]{1,0:T(8,128)(2,1)S(1)}, f32[512,384]{1,0:T(8,128)S(1)}, f32[512,128]{1,0:T(8,128)S(1)}) custom-call(s32[2]{0:T(128)S(1)} %pad_add_fusion.ids, bf16[128,1152]{1,0:T(8,128)(2,1)S(1)} %collective-permute-done.refs_0_, bf16[128,1152]{1,0:T(8,128)(2,1)S(1)} %collective-permute-done.1.refs_1_, ...), custom_call_target="tpu_custom_call" | custom-call | flops 27179089920 | tf_op jit(solution)/shard_map/pallas_call | solution.py:316
  22.0 11.3 %collective-permute-start.8 = (bf16[512,1152]{1,0:T(8,128)(2,1)S(1)}, bf16[512,1152]{1,0:T(8,128)(2,1)S(1)}, u32[]{:S(2)}, u32[]{:S(2)}) collective-permute-start(bf16[512,1152]{1,0:T(8,128)(2,1)S(1)} %get-tuple-element.39.own), channel_id=1, source_target_pairs={{0,1},{1,0},{2,3},{3,2},{4,5},{5,4},{6,7},{7,6},{8,9},{9,8},{10,11... | collective-permute-start | bytes 3538952 | tf_op jit(solution)/shard_map/ppermute | solution.py:20
  33.3 2.3 %shard_map.102 = (bf16[1152,384]{1,0:T(8,128)(2,1)S(1)}, bf16[384,1152]{1,0:T(8,128)(2,1)S(1)}, f32[384,384]{1,0:T(8,128)S(1)}, f32[384,128]{1,0:T(8,128)S(1)}) custom-call(s32[2]{0:T(128)S(1)} %pad_add_fusion.ids, bf16[128,1152]{1,0:T(8,128)(2,1)S(1)} %collective-permute-done.4.refs_0_, bf16[128,1152]{1,0:T(8,128)(2,1)S(1)} %collective-permute-done.6.refs_1_, ...), custom_call_target="tpu_custom_call" | custom-call | flops 27179089920 | tf_op jit(solution)/shard_map/pallas_call | solution.py:316
  35.8 3.9 %shard_map.103 = (bf16[512,1152]{1,0:T(8,128)(2,1)S(1)}, bf16[1152,128]{1,0:T(8,128)(2,1)S(1)}, f32[128,384]{1,0:T(8,128)S(1)}, f32[128,128]{1,0:T(8,128)S(1)}, ...) custom-call(s32[2]{0:T(128)S(1)} %pad_add_fusion.ids, ...), custom_call_target="tpu_custom_call" | custom-call | flops 27179089920 | tf_op jit(solution)/shard_map/pallas_call | solution.py:316
  39.7 1.7 %collective-permute-start.9 = (f32[512,512]{1,0:T(8,128)S(1)}, f32[512,512]{1,0:T(8,128)S(1)}, u32[]{:S(2)}, u32[]{:S(2)}) collective-permute-start(f32[512,512]{1,0:T(8,128)S(1)} %get-tuple-element.52), channel_id=1, source_target_pairs={{0,1},{1,0},{2,3},{3,2},{4,5},{5,4},{6,7},{7,6},{8,9},{9,8},{10,11... | collective-permute-start | bytes 3145736 | tf_op jit(solution)/shard_map/ppermute | solution.py:20
  41.4 3.1 %shard_map.104 = (f32[1152,384]{1,0:T(8,128)S(1)}, f32[512,384]{1,0:T(8,128)S(1)}) custom-call(s32[2]{0:T(128)S(1)} %pad_add_fusion.ids, f32[2]{0:T(128)S(1)} %pad_maximum_fusion.scal, bf16[1152,384]{1,0:T(8,128)(2,1)S(1)} %get-tuple-element.41.f0, bf16[1152,128]{1,0:T(8,128)(2,1)S(1)} %get-tuple-element.42.f1, f32[384,384]{1,0:T(8,128)S(1)} %get-tuple-element.43.w0, ...), custom_call_target="tpu_custom_call" | custom-call | flops 27179089920 | tf_op jit(solution)/shard_map/pallas_call | solution.py:316
  44.5 1.4 %shard_map.105 = (bf16[16,192,128]{2,1,0:T(8,128)(2,1)S(1)}, f32[16,192,128]{2,1,0:T(8,128)S(1)}, f32[8,128]{1,0:T(8,128)S(1)}) custom-call(s32[2]{0:T(128)S(1)} %pad_add_fusion.ids, f32[2]{0:T(128)S(1)} %pad_maximum_fusion.scal, bf16[1152,512]{1,0:T(8,128)(2,1)S(1)} %get-tuple-element.35.turned, f32[512,384]{1,0:T(8,128)S(1)} %get-tuple-element.36.window, ...), custom_call_target="tpu_custom_call" | custom-call | tf_op jit(solution)/shard_map/pallas_call | solution.py:316
  46.1 1.2 %shard_map.108 = f32[136,1152]{1,0:T(8,128)} custom-call(bf16[1024,512]{1,0:T(8,128)(2,1)S(1)} %get-tuple-element.49.slopes_turned, bf16[512,1152]{1,0:T(8,128)(2,1)S(1)} %get-tuple-element.47.emb, f32[8,128]{1,0:T(8,128)S(1)} %get-tuple-element.57.loss, f32[8,128]{1,0:T(8,128)S(1)} %get-tuple-element.58.after), custom_call_target="tpu_custom_call" | custom-call | flops 27179089920 | tf_op jit(solution)/shard_map/pallas_call | solution.py:316
  47.2 0.5 collective-permute-start.11
  47.7 0.6 collective-permute-done.10.got
  48.3 1.1 %shard_map.106 = (bf16[16,192,128]{2,1,0:T(8,128)(2,1)}, f32[8,128]{1,0:T(8,128)S(1)}) custom-call(f32[16,192,128]{2,1,0:T(8,128)S(1)} %get-tuple-element.54.keep, bf16[16,192,128]{2,1,0:T(8,128)(2,1)S(1)} %collective-permute-done.10.got), custom_call_target="tpu_custom_call" | custom-call | tf_op jit(solution)/shard_map/pallas_call | solution.py:316
  49.4 9.5 %all-to-all-start = ((bf16[16,192,128]{2,1,0:T(8,128)(2,1)}), bf16[16,192,128]{2,1,0:T(8,128)(2,1)S(1)}, u32[]{:S(2)}, u32[]{:S(2)}) async-start(bf16[16,192,128]{2,1,0:T(8,128)(2,1)} %get-tuple-element.56), calls=%async_computation | async-start | bytes 1572864 | tf_op jit(solution)/shard_map/all_to_all | solution.py:377
  58.9 1.3 %copy-done.2 = bf16[512,1152]{1,0:T(8,128)(2,1)S(1)} copy-done((bf16[512,1152]{1,0:T(8,128)(2,1)S(1)}, bf16[512,1152]{1,0:T(8,128)(2,1)}, u32[]{:S(2)}) %copy-start.2) | copy-done | bytes 1179672
  60.2 1.3 %copy-done.4 = bf16[512,1152]{1,0:T(8,128)(2,1)S(1)} copy-done((bf16[512,1152]{1,0:T(8,128)(2,1)S(1)}, bf16[512,1152]{1,0:T(8,128)(2,1)}, u32[]{:S(2)}) %copy-start.4) | copy-done | bytes 1179672
  61.4 1.2 %copy-done.6 = bf16[512,1024]{1,0:T(8,128)(2,1)S(1)} copy-done((bf16[512,1024]{1,0:T(8,128)(2,1)S(1)}, bf16[512,1024]{1,0:T(8,128)(2,1)}, u32[]{:S(2)}) %copy-start.6) | copy-done | bytes 1048600
  62.7 1.2 %copy-done.8 = bf16[1024,512]{1,0:T(8,128)(2,1)S(1)} copy-done((bf16[1024,512]{1,0:T(8,128)(2,1)S(1)}, bf16[1024,512]{1,0:T(8,128)(2,1)}, u32[]{:S(2)}) %copy-start.8) | copy-done | bytes 1048600
  63.9 2.1 %shard_map.109 = bf16[272,1152]{1,0:T(8,128)(2,1)} custom-call(f32[2]{0:T(128)S(1)} %pad_maximum_fusion.scal, bf16[512,1024]{1,0:T(8,128)(2,1)S(1)} %copy-done.6, bf16[1024,512]{1,0:T(8,128)(2,1)S(1)} %copy-done.8, bf16[512,1152]{1,0:T(8,128)(2,1)S(1)} %copy-done.4, bf16[512,1152]{1,0:T(8,128)(2,1)S(1)} %get-tuple-element.39.own, ...), custom_call_target="tpu_custom_call" | custom-call | flops 27179089920 | tf_op jit(solution)/shard_map/pallas_call | solution.py:316
  66.0 1.7 %collective-permute-start.12 = (bf16[272,1152]{1,0:T(8,128)(2,1)}, bf16[272,1152]{1,0:T(8,128)(2,1)S(1)}, u32[]{:S(2)}, u32[]{:S(2)}) collective-permute-start(bf16[272,1152]{1,0:T(8,128)(2,1)} %shard_map.109), channel_id=1, source_target_pairs={{0,0},{1,128},{128,1},{129,129},{2,2},{3,130},{130,3},{131,131},{4... | collective-permute-start | bytes 1880072 | tf_op jit(solution)/shard_map/ppermute | solution.py:16
  67.7 12.1 %all-to-all-done.parts = bf16[16,192,128]{2,1,0:T(8,128)(2,1)S(1)} async-done(((bf16[16,192,128]{2,1,0:T(8,128)(2,1)}), bf16[16,192,128]{2,1,0:T(8,128)(2,1)S(1)}, u32[]{:S(2)}, u32[]{:S(2)}) %all-to-all-start) | async-done | bytes 786464 | tf_op jit(solution)/shard_map/all_to_all | solution.py:377
  79.8 0.9 shard_map.107
  80.7 4.0 %all-to-all-start.1 = ((bf16[8,192,128]{2,1,0:T(8,128)(2,1)}), bf16[8,192,128]{2,1,0:T(8,128)(2,1)S(1)}, u32[]{:S(2)}, u32[]{:S(2)}) async-start(bf16[8,192,128]{2,1,0:T(8,128)(2,1)} %shard_map.107), calls=%async_computation.1 | async-start | bytes 786432 | tf_op jit(solution)/shard_map/all_to_all | solution.py:379
  84.7 9.2 %all-to-all-done.1.spread = bf16[8,192,128]{2,1,0:T(8,128)(2,1)S(1)} async-done(((bf16[8,192,128]{2,1,0:T(8,128)(2,1)}), bf16[8,192,128]{2,1,0:T(8,128)(2,1)S(1)}, u32[]{:S(2)}, u32[]{:S(2)}) %all-to-all-start.1) | async-done | bytes 393248 | tf_op jit(solution)/shard_map/all_to_all | solution.py:379
  94.0 1.6 %shard_map.110 = (f32[36,1152]{1,0:T(8,128)}, f32[36,1152]{1,0:T(8,128)}, f32[1]{0:T(128)}, bf16[1,128,1152]{2,1,0:T(8,128)(2,1)}, bf16[1,128,1152]{2,1,0:T(8,128)(2,1)}) custom-call(s32[2]{0:T(128)S(1)} %pad_add_fusion.ids, bf16[8,192,128]{2,1,0:T(8,128)(2,1)S(1)} %all-to-all-done.1.spread, bf16[272,1152]{1,0:T(8,128)(2,1)S(1)} %collective-permute-done.12.outs), custom_call_target="tpu_custom_call" | custom-call | tf_op jit(solution)/shard_map/pallas_call | solution.py:316
  (28 shorter events, 0.5 us)
Async XLA Ops:
  0.6 3.2 %collective-permute-start = (bf16[128,1152]{1,0:T(8,128)(2,1)}, bf16[128,1152]{1,0:T(8,128)(2,1)S(1)}, u32[]{:S(2)}, u32[]{:S(2)}) collective-permute-start(bf16[128,1152]{1,0:T(8,128)(2,1)} %bitcast.4), channel_id=1, source_target_pairs={{0,0},{1,128},{128,1},{129,129},{2,2},{3,130},{130,3},{131,131},{4... | collective-permute-start | bytes 884744 | tf_op jit(solution)/shard_map/ppermute | solution.py:16
  2.3 8.3 %collective-permute-start.4 = (bf16[128,1152]{1,0:T(8,128)(2,1)}, bf16[128,1152]{1,0:T(8,128)(2,1)S(1)}, u32[]{:S(2)}, u32[]{:S(2)}) collective-permute-start(bf16[128,1152]{1,0:T(8,128)(2,1)} %bitcast.5), channel_id=1, source_target_pairs={{0,0},{1,128},{128,1},{129,129},{2,2},{3,130},{130,3},{131,131},{4... | collective-permute-start | bytes 884744 | tf_op jit(solution)/shard_map/ppermute | solution.py:16
  3.9 9.0 %collective-permute-start.3 = (bf16[128,1152]{1,0:T(8,128)(2,1)S(1)}, bf16[128,1152]{1,0:T(8,128)(2,1)S(1)}, u32[]{:S(2)}, u32[]{:S(2)}) collective-permute-start(bf16[128,1152]{1,0:T(8,128)(2,1)S(1)} %collective-permute-done.refs_0_), channel_id=1, source_target_pairs={{0,64},{32,96},{64,0},{96,32},{1,65},{33,97},{65,1},{97,33},{2,66}... | collective-permute-start | bytes 884744 | tf_op jit(solution)/shard_map/ppermute | solution.py:24
  7.1 9.1 %collective-permute-start.2 = (bf16[128,1152]{1,0:T(8,128)(2,1)S(1)}, bf16[128,1152]{1,0:T(8,128)(2,1)S(1)}, u32[]{:S(2)}, u32[]{:S(2)}) collective-permute-start(bf16[128,1152]{1,0:T(8,128)(2,1)S(1)} %collective-permute-done.refs_0_), channel_id=1, source_target_pairs={{0,96},{32,0},{64,32},{96,64},{1,97},{33,1},{65,33},{97,65},{2,98}... | collective-permute-start | bytes 884744 | tf_op jit(solution)/shard_map/ppermute | solution.py:24
  8.1 9.4 %collective-permute-start.1 = (bf16[128,1152]{1,0:T(8,128)(2,1)S(1)}, bf16[128,1152]{1,0:T(8,128)(2,1)S(1)}, u32[]{:S(2)}, u32[]{:S(2)}) collective-permute-start(bf16[128,1152]{1,0:T(8,128)(2,1)S(1)} %collective-permute-done.refs_0_), channel_id=1, source_target_pairs={{0,32},{32,64},{64,96},{96,0},{1,33},{33,65},{65,97},{97,1},{2,34}... | collective-permute-start | bytes 884744 | tf_op jit(solution)/shard_map/ppermute | solution.py:24
  10.5 22.8 %copy-start = (bf16[1152,1152]{1,0:T(8,128)(2,1)S(1)}, bf16[1152,1152]{1,0:T(8,128)(2,1)}, u32[]{:S(2)}) copy-start(bf16[1152,1152]{1,0:T(8,128)(2,1)} %weight.1) | copy-start | bytes 7962628
  10.5 22.8 %collective-permute-start.7 = (bf16[128,1152]{1,0:T(8,128)(2,1)S(1)}, bf16[128,1152]{1,0:T(8,128)(2,1)S(1)}, u32[]{:S(2)}, u32[]{:S(2)}) collective-permute-start(bf16[128,1152]{1,0:T(8,128)(2,1)S(1)} %collective-permute-done.4.refs_0_), channel_id=1, source_target_pairs={{0,96},{32,0},{64,32},{96,64},{1,97},{33,1},{65,33},{97,65},{2,98}... | collective-permute-start | bytes 884744 | tf_op jit(solution)/shard_map/ppermute | solution.py:24
  12.8 20.5 %collective-permute-start.6 = (bf16[128,1152]{1,0:T(8,128)(2,1)S(1)}, bf16[128,1152]{1,0:T(8,128)(2,1)S(1)}, u32[]{:S(2)}, u32[]{:S(2)}) collective-permute-start(bf16[128,1152]{1,0:T(8,128)(2,1)S(1)} %collective-permute-done.4.refs_0_), channel_id=1, source_target_pairs={{0,32},{32,64},{64,96},{96,0},{1,33},{33,65},{65,97},{97,1},{2,34}... | collective-permute-start | bytes 884744 | tf_op jit(solution)/shard_map/ppermute | solution.py:24
  12.8 22.8 %collective-permute-start.5 = (bf16[128,1152]{1,0:T(8,128)(2,1)S(1)}, bf16[128,1152]{1,0:T(8,128)(2,1)S(1)}, u32[]{:S(2)}, u32[]{:S(2)}) collective-permute-start(bf16[128,1152]{1,0:T(8,128)(2,1)S(1)} %collective-permute-done.4.refs_0_), channel_id=1, source_target_pairs={{0,64},{32,96},{64,0},{96,32},{1,65},{33,97},{65,1},{97,33},{2,66}... | collective-permute-start | bytes 884744 | tf_op jit(solution)/shard_map/ppermute | solution.py:24
  22.0 13.8 %collective-permute-start.8 = (bf16[512,1152]{1,0:T(8,128)(2,1)S(1)}, bf16[512,1152]{1,0:T(8,128)(2,1)S(1)}, u32[]{:S(2)}, u32[]{:S(2)}) collective-permute-start(bf16[512,1152]{1,0:T(8,128)(2,1)S(1)} %get-tuple-element.39.own), channel_id=1, source_target_pairs={{0,1},{1,0},{2,3},{3,2},{4,5},{5,4},{6,7},{7,6},{8,9},{9,8},{10,11... | collective-permute-start | bytes 3538952 | tf_op jit(solution)/shard_map/ppermute | solution.py:20
  35.8 5.6 %copy-start.1 = (bf16[512,1152]{1,0:T(8,128)(2,1)}, bf16[512,1152]{1,0:T(8,128)(2,1)S(1)}, u32[]{:S(2)}) copy-start(bf16[512,1152]{1,0:T(8,128)(2,1)S(1)} %collective-permute-done.8.other) | copy-start | bytes 3538948
  39.7 4.8 %copy-start.5 = (bf16[512,1024]{1,0:T(8,128)(2,1)}, bf16[512,1024]{1,0:T(8,128)(2,1)S(1)}, u32[]{:S(2)}) copy-start(bf16[512,1024]{1,0:T(8,128)(2,1)S(1)} %get-tuple-element.48.slopes) | copy-start | bytes 3145732
  39.7 6.4 %copy-start.3 = (bf16[512,1152]{1,0:T(8,128)(2,1)}, bf16[512,1152]{1,0:T(8,128)(2,1)S(1)}, u32[]{:S(2)}) copy-start(bf16[512,1152]{1,0:T(8,128)(2,1)S(1)} %get-tuple-element.47.emb) | copy-start | bytes 3538948
  39.7 6.4 %copy-start.7 = (bf16[1024,512]{1,0:T(8,128)(2,1)}, bf16[1024,512]{1,0:T(8,128)(2,1)S(1)}, u32[]{:S(2)}) copy-start(bf16[1024,512]{1,0:T(8,128)(2,1)S(1)} %get-tuple-element.49.slopes_turned) | copy-start | bytes 3145732
  39.7 4.8 %collective-permute-start.9 = (f32[512,512]{1,0:T(8,128)S(1)}, f32[512,512]{1,0:T(8,128)S(1)}, u32[]{:S(2)}, u32[]{:S(2)}) collective-permute-start(f32[512,512]{1,0:T(8,128)S(1)} %get-tuple-element.52), channel_id=1, source_target_pairs={{0,1},{1,0},{2,3},{3,2},{4,5},{5,4},{6,7},{7,6},{8,9},{9,8},{10,11... | collective-permute-start | bytes 3145736 | tf_op jit(solution)/shard_map/ppermute | solution.py:20
  45.9 2.4 %collective-permute-start.10 = (bf16[16,192,128]{2,1,0:T(8,128)(2,1)S(1)}, bf16[16,192,128]{2,1,0:T(8,128)(2,1)S(1)}, u32[]{:S(2)}, u32[]{:S(2)}) collective-permute-start(bf16[16,192,128]{2,1,0:T(8,128)(2,1)S(1)} %get-tuple-element.55), channel_id=1, source_target_pairs={{0,1},{1,0},{2,3},{3,2},{4,5},{5,4},{6,7},{7,6},{8,9},{9,8},{10,11... | collective-permute-start | bytes 2359304 | tf_op jit(solution)/shard_map/ppermute | solution.py:20
  47.2 11.6 %collective-permute-start.11 = (f32[136,1152]{1,0:T(8,128)}, f32[136,1152]{1,0:T(8,128)S(1)}, u32[]{:S(2)}, u32[]{:S(2)}) collective-permute-start(f32[136,1152]{1,0:T(8,128)} %shard_map.108), channel_id=1, source_target_pairs={{0,1},{1,0},{2,3},{3,2},{4,5},{5,4},{6,7},{7,6},{8,9},{9,8},{10,11... | collective-permute-start | bytes 1880072 | tf_op jit(solution)/shard_map/ppermute | solution.py:20
  49.4 30.4 %all-to-all-start = ((bf16[16,192,128]{2,1,0:T(8,128)(2,1)}), bf16[16,192,128]{2,1,0:T(8,128)(2,1)S(1)}, u32[]{:S(2)}, u32[]{:S(2)}) async-start(bf16[16,192,128]{2,1,0:T(8,128)(2,1)} %get-tuple-element.56), calls=%async_computation | async-start | bytes 1572864 | tf_op jit(solution)/shard_map/all_to_all | solution.py:377
  58.9 1.3 %copy-start.2 = (bf16[512,1152]{1,0:T(8,128)(2,1)S(1)}, bf16[512,1152]{1,0:T(8,128)(2,1)}, u32[]{:S(2)}) copy-start(bf16[512,1152]{1,0:T(8,128)(2,1)} %copy-done.1) | copy-start | bytes 3538948
  60.2 1.3 %copy-start.4 = (bf16[512,1152]{1,0:T(8,128)(2,1)S(1)}, bf16[512,1152]{1,0:T(8,128)(2,1)}, u32[]{:S(2)}) copy-start(bf16[512,1152]{1,0:T(8,128)(2,1)} %copy-done.3) | copy-start | bytes 3538948
  61.4 1.2 %copy-start.6 = (bf16[512,1024]{1,0:T(8,128)(2,1)S(1)}, bf16[512,1024]{1,0:T(8,128)(2,1)}, u32[]{:S(2)}) copy-start(bf16[512,1024]{1,0:T(8,128)(2,1)} %copy-done.5) | copy-start | bytes 3145732
  62.7 1.2 %copy-start.8 = (bf16[1024,512]{1,0:T(8,128)(2,1)S(1)}, bf16[1024,512]{1,0:T(8,128)(2,1)}, u32[]{:S(2)}) copy-start(bf16[1024,512]{1,0:T(8,128)(2,1)} %copy-done.7) | copy-start | bytes 3145732
  66.0 18.8 %collective-permute-start.12 = (bf16[272,1152]{1,0:T(8,128)(2,1)}, bf16[272,1152]{1,0:T(8,128)(2,1)S(1)}, u32[]{:S(2)}, u32[]{:S(2)}) collective-permute-start(bf16[272,1152]{1,0:T(8,128)(2,1)} %shard_map.109), channel_id=1, source_target_pairs={{0,0},{1,128},{128,1},{129,129},{2,2},{3,130},{130,3},{131,131},{4... | collective-permute-start | bytes 1880072 | tf_op jit(solution)/shard_map/ppermute | solution.py:16
  80.7 13.3 %all-to-all-start.1 = ((bf16[8,192,128]{2,1,0:T(8,128)(2,1)}), bf16[8,192,128]{2,1,0:T(8,128)(2,1)S(1)}, u32[]{:S(2)}, u32[]{:S(2)}) async-start(bf16[8,192,128]{2,1,0:T(8,128)(2,1)} %shard_map.107), calls=%async_computation.1 | async-start | bytes 786432 | tf_op jit(solution)/shard_map/all_to_all | solution.py:379

commit v4 on v3

--- a/solution.py
+++ b/solution.py
@@ -6,6 +6,7 @@
 from jax.sharding import Mesh, PartitionSpec as P
 
 epsilon = 1e-06
+LOG2_E = 1.4426950408889634
 AXES = ("xh", "y", "xl", "z", "c")
 XH, Y, XL, Z, C = 2, 4, 2, 8, 2
 WIDE, SLIM, PACK, TERMS = 256, 128, 192, 16
@@ -96,18 +97,19 @@
 
 
 def slope_kernel(
-    ids, scal, far, weight, early, own, other,
+    ids, scal, p2, p3, weight, early, own, other,
     emb, turned, window, inv, slopes, slopes_turned, radial, text_radial, give, loss,
     late, joined, unit,
 ):
     y = ids[0]
     scale, bias = scal[0], scal[1]
-    image_kernel(ids, far, weight, turned, late, window, inv, joined, unit)
+    image_kernel(ids, p2, p3, weight, turned, late, window, inv, joined, unit)
     rows = emb.shape[0]
     join((early, late), emb)
     embedded = emb[...]
     lost = jnp.zeros((8, WIDE), f32)
     along = [jnp.zeros((WIDE, WIDE), f32) for _ in range(0, rows, WIDE)]
+    scale2, bias2 = scale * LOG2_E, bias * LOG2_E
     for j in reversed(range(0, 2 * rows, WIDE)):
         mine = j < rows
         side, at = (own, j) if mine else (other, j - rows)
@@ -115,20 +117,20 @@
         down = jnp.zeros((8, WIDE), f32)
         for i in range(0, rows, WIDE):
             cosine = cosines[i : i + WIDE]
-            logits = scale * cosine + bias
+            power = scale2 * cosine + bias2
             diagonal = mine and i == at
             if diagonal:
-                same = lax.broadcasted_iota(jnp.int32, logits.shape, 0) == lax.broadcasted_iota(
-                    jnp.int32, logits.shape, 1
+                same = lax.broadcasted_iota(jnp.int32, power.shape, 0) == lax.broadcasted_iota(
+                    jnp.int32, power.shape, 1
                 )
-                logits = jnp.where(same, -logits, logits)
-            small = jnp.exp(-jnp.abs(logits))
-            whole = 1.0 + small
-            slope = jnp.where(logits >= 0, 1.0, small) * pl.reciprocal(whole, approx=True)
+                power = jnp.where(same, -power, power)
+            grown = jnp.exp2(power)
+            whole = 1.0 + grown
+            slope = grown * pl.reciprocal(whole, approx=True)
             if diagonal:
                 slope = jnp.where(same, -slope, slope)
+            lost = lost + fold(jnp.log(whole[: WIDE // 2] * whole[WIDE // 2 :]), jnp.add)
             slope = slope.astype(bf16)
-            lost = lost + fold(jnp.maximum(logits, 0.0), jnp.add) + jnp.log(fold(whole, jnp.multiply))
             slopes[i : i + WIDE, j : j + WIDE] = slope
             slopes_turned[j : j + WIDE, i : i + WIDE] = slope.T
             weighted = slope.astype(f32) * cosine
@@ -169,8 +171,8 @@
 
 
 def grad_kernel(
-    ids, scal, f0, f1, w0, w1, v0, v1, emb, slopes, slopes_turned, radial, own, other,
-    term, part,
+    ids, scal, f0, f1, w0, w1, v0, v1, emb, slopes, slopes_turned, radial, loss, own, other,
+    term, part, rest,
 ):
     y = ids[0]
     scale = scal[0]
@@ -182,12 +184,18 @@
         grad = back(grad, window[:, at : at + size], scale * radial[...], inv)
         term[:, at : at + size] = outer((f0, f1), grad)
 
-    columns(pl.ds(image_start(y), WIDE), 0, WIDE)
+    n = rest.shape[0] - 8
+    rest[:n, :] = dot(slopes_turned[rows : rows + n, :], emb[...])
+    rest[n:, :] = jnp.broadcast_to(loss[:, :1], (8, rest.shape[1]))
     part[:, :WIDE] = dot(slopes_turned[:rows, :], emb[:, pl.ds(text_start(y), WIDE)])
 
     @pl.when(y == 0)
     def _():
-        columns(slice(WIDE, WIDE + SLIM), WIDE, SLIM)
+        columns(slice(0, WIDE + SLIM), 0, WIDE + SLIM)
+
+    @pl.when(y != 0)
+    def _():
+        columns(pl.ds(image_start(y), WIDE), 0, WIDE)
 
     @pl.when(y == Y - 1)
     def _():
@@ -240,12 +248,13 @@
     return jnp.concatenate(parts, axis=0)
 
 
-def add_kernel(keep, got, mine, token):
-    token[...] = jnp.zeros(token.shape, f32)
+def add_kernel(keep, got, after, mine):
+    del after
     mine[...] = (keep[...] + got[...].astype(f32)).astype(bf16)
 
 
-def spread_kernel(parts, spread):
+def spread_kernel(parts, after, spread):
+    del after
     summed = jnp.sum(parts[...].astype(f32), axis=0).astype(bf16)
     for i in range(spread.shape[0]):
         spread[i] = summed
@@ -281,14 +290,6 @@
         pl.when(core == c)(lambda c=c: place(c))
 
 
-def rest_kernel(slopes_turned, emb, loss, after, give):
-    del after
-    n = give.shape[0] - 8
-    rows = emb.shape[0]
-    give[:n, :] = dot(slopes_turned[rows : rows + n, :], emb[...])
-    give[n:, :] = jnp.broadcast_to(loss[:, :1], (8, give.shape[1]))
-
-
 def out_kernel(scal, slopes, slopes_turned, emb, own, other, loss, got, after, out):
     del after
     scale = scal[0]
@@ -348,10 +349,10 @@
         text_kernel, projected(rows), scratch(rows) + streams, macs, len(text) + 1
     )(ids, *text, pltpu.with_memory_space_constraint(text_proj, pltpu.HBM))
     text_other = other_core(text_emb)
-    turned_a, early, window_a, inv_a = call(image_kernel, projected(3 * n), scratch(3 * n), macs)(
-        ids, *image[:3], image_proj
+    turned_a, early, window_a, inv_a = call(image_kernel, projected(2 * n), scratch(2 * n), macs)(
+        ids, *image[:2], image_proj
     )
-    turned, _, window, inv = projected(n)
+    turned, _, window, inv = projected(2 * n)
     emb, turned_b, window_b, inv_b, slopes, slopes_turned, radial, text_radial, give, loss = call(
         slope_kernel,
         [
@@ -359,13 +360,15 @@
             ((rows, C * rows), bf16), ((C * rows, rows), bf16), ((rows, SLIM), f32), ((rows, SLIM), f32),
             ((rows, WIDE + 2 * SLIM), f32), ((8, SLIM), f32),
         ],
-        [pltpu.VMEM((n, width), bf16)] + scratch(n),
+        [pltpu.VMEM((2 * n, width), bf16)] + scratch(2 * n),
         macs,
-    )(ids, scal, *image[3:], image_proj, early, text_emb, text_other)
+    )(ids, scal, *image[2:], image_proj, early, text_emb, text_other)
     got = other_core(give)
-    image_term, part = call(grad_kernel, [((depth, WIDE + SLIM), f32), ((rows, WIDE + SLIM), f32)], (), macs)(
+    image_term, part, rest = call(
+        grad_kernel, [((depth, WIDE + SLIM), f32), ((rows, WIDE + SLIM), f32), ((n + 8, width), f32)], (), macs
+    )(
         ids, scal, turned_a, turned_b, window_a, window_b, inv_a, inv_b, emb, slopes, slopes_turned,
-        radial, text_emb, text_other,
+        radial, loss, text_emb, text_other,
     )
     packed = (XL * Z, PACK, SLIM)
     give, keep, token = call(
@@ -373,15 +376,14 @@
         [(packed, bf16), (packed, f32), ((8, SLIM), f32)],
         [pltpu.VMEM((depth, WIDE + SLIM), f32)],
     )(ids, scal, text_turned, text_window, text_inv, text_radial, part, got, image_term)
-    mine, behind = call(add_kernel, [(packed, bf16), ((8, SLIM), f32)])(keep, other_core(give))
+    (outs,) = call(out_kernel, [((2 * n + TERMS, width), bf16)], (), macs)(
+        scal, slopes, slopes_turned, emb, text_emb, text_other, loss, other_core(rest), token
+    )
+    (mine,) = call(add_kernel, [(packed, bf16)])(keep, other_core(give), outs)
+    outs = trade(outs)
     arrived = lax.all_to_all(mine, ("xl", "z"), 0, 0)
-    (spread,) = call(spread_kernel, [((XH * Y, PACK, SLIM), bf16)])(arrived)
+    (spread,) = call(spread_kernel, [((XH * Y, PACK, SLIM), bf16)])(arrived, outs)
     spread = lax.all_to_all(spread, ("xh", "y"), 0, 0)
-    (give_rest,) = call(rest_kernel, [((n + 8, width), f32)], (), macs)(slopes_turned, emb, loss, token)
-    (outs,) = call(out_kernel, [((2 * n + TERMS, width), bf16)], (), macs)(
-        scal, slopes, slopes_turned, emb, text_emb, text_other, loss, other_core(give_rest), behind
-    )
-    outs = trade(outs)
     grad = (depth // (XL * Z * C), width), f32
     image_grad, text_grad, total, image_out, text_out = call(
         unpack_kernel, [grad, grad, ((1,), f32), ((1, n, width), bf16), ((1, n, width), bf16)]

time: 96.4 us -> 95.8 us (level)
  blocking collectives: 0 us -> 14.1 us
  starting transfers between devices: 42.1 us -> 36.6 us
  local copies, waits for them, and re-layouts: 5 us -> 0.01 us
  Pallas kernels: 22 us -> 18.2 us
    all_to_all x0 -> x1, blocking collectives: none -> 14.1 us  [on_device(): spread = lax.all_to_all(spread, ('xh', 'y'), 0, 0)]
    all_to_all x1 -> x0, waiting for transfers between devices: 9.25 us -> none  [on_device(): spread = lax.all_to_all(spread, ('xh', 'y'), 0, 0)]
    all_to_all x1, waiting for transfers between devices: 12.1 us -> 20.6 us  [on_device(): arrived = lax.all_to_all(mine, ('xl', 'z'), 0, 0)]
    unnamed x18 -> x2, local copies, waits for them, and re-layouts: 5 us -> 0.01 us
    all_to_all x1 -> x0, starting transfers between devices: 4.03 us -> none  [on_device(): spread = lax.all_to_all(spread, ('xh', 'y'), 0, 0)]
    pallas_call x10 -> x9, Pallas kernels: 22 us -> 18.2 us  [run(): pl.pallas_call(kernel, out_shape=[jax.ShapeDtypeStruct(s, d) for s, d in...]
    ppermute x3, starting transfers between devices: 4.95 us -> 3.92 us  [trade(): return lax.ppermute(x, ('xh', 'c'), [(0, 0), (1, 2), (2, 1), (3, 3)])]
  transfers between devices with their start and end apart: 15 -> 14, of which waited for: 6 -> 6; matrix products, arithmetic and copies ran while one was open for 0% -> 0% of each run, Pallas kernels for 16% -> 12%
where the time goes in v4:
time: 95.8 us; the launch traced here: 95.4 us
  starting transfers between devices  36.6 us (38%)
  waiting for transfers between devices  24.2 us (25%)
  Pallas kernels  18.2 us (19%)
  blocking collectives  14.1 us (15%)
  between operations  2.18 us (2%)
    all_to_all x1, waiting for transfers between devices, on_device(): arrived = lax.all_to_all(mine, ('xl', 'z'), 0, 0)  20.6 us
    pallas_call x9, Pallas kernels, run(): pl.pallas_call(kernel, out_shape=[jax.ShapeDtypeStruct(s, d) for s, d in...  18.2 us
    all_to_all x1, blocking collectives, on_device(): spread = lax.all_to_all(spread, ('xh', 'y'), 0, 0)  14.1 us
    ppermute x4, starting transfers between devices, other_core(): return lax.ppermute(x, 'c', [(0, 1), (1, 0)])  13.2 us
    ppermute x6, starting transfers between devices, from_y(): return lax.ppermute(x, 'y', [(i, (i + k) % Y) for i in range(Y)])  9.89 us
    all_to_all x1, starting transfers between devices, on_device(): arrived = lax.all_to_all(mine, ('xl', 'z'), 0, 0)  9.54 us
    ppermute x3, starting transfers between devices, trade(): return lax.ppermute(x, ('xh', 'c'), [(0, 0), (1, 2), (2, 1), (3, 3)])  3.92 us
    ppermute x6, waiting for transfers between devices, from_y(): return lax.ppermute(x, 'y', [(i, (i + k) % Y) for i in range(Y)])  2.23 us
  transfers between devices with their start and end apart: 14, of which 6 were waited for; matrix products, arithmetic and copies ran while one was open for 0% of the time, Pallas kernels for 12%

profile of v4, /device:TPU:32, one launch (start us, length us, event | category | flops | bytes accessed | tf_op | source)
XLA Modules:
  0.0 95.4 jit_solution(12551799972805917378)
XLA Ops:
  0.6 1.6 %collective-permute-start = (bf16[128,1152]{1,0:T(8,128)(2,1)}, bf16[128,1152]{1,0:T(8,128)(2,1)S(1)}, u32[]{:S(2)}, u32[]{:S(2)}) collective-permute-start(bf16[128,1152]{1,0:T(8,128)(2,1)} %bitcast.4), channel_id=1, source_target_pairs={{0,0},{1,128},{128,1},{129,129},{2,2},{3,130},{130,3},{131,131},{4... | collective-permute-start | bytes 884744 | tf_op jit(solution)/shard_map/ppermute | solution.py:17
  2.3 1.6 %collective-permute-start.4 = (bf16[128,1152]{1,0:T(8,128)(2,1)}, bf16[128,1152]{1,0:T(8,128)(2,1)S(1)}, u32[]{:S(2)}, u32[]{:S(2)}) collective-permute-start(bf16[128,1152]{1,0:T(8,128)(2,1)} %bitcast.5), channel_id=1, source_target_pairs={{0,0},{1,128},{128,1},{129,129},{2,2},{3,130},{130,3},{131,131},{4... | collective-permute-start | bytes 884744 | tf_op jit(solution)/shard_map/ppermute | solution.py:17
  3.9 3.2 %collective-permute-start.3 = (bf16[128,1152]{1,0:T(8,128)(2,1)S(1)}, bf16[128,1152]{1,0:T(8,128)(2,1)S(1)}, u32[]{:S(2)}, u32[]{:S(2)}) collective-permute-start(bf16[128,1152]{1,0:T(8,128)(2,1)S(1)} %collective-permute-done.refs_0_), channel_id=1, source_target_pairs={{0,64},{32,96},{64,0},{96,32},{1,65},{33,97},{65,1},{97,33},{2,66}... | collective-permute-start | bytes 884744 | tf_op jit(solution)/shard_map/ppermute | solution.py:25
  7.1 1.1 %collective-permute-start.2 = (bf16[128,1152]{1,0:T(8,128)(2,1)S(1)}, bf16[128,1152]{1,0:T(8,128)(2,1)S(1)}, u32[]{:S(2)}, u32[]{:S(2)}) collective-permute-start(bf16[128,1152]{1,0:T(8,128)(2,1)S(1)} %collective-permute-done.refs_0_), channel_id=1, source_target_pairs={{0,96},{32,0},{64,32},{96,64},{1,97},{33,1},{65,33},{97,65},{2,98}... | collective-permute-start | bytes 884744 | tf_op jit(solution)/shard_map/ppermute | solution.py:25
  8.1 1.0 %collective-permute-start.1 = (bf16[128,1152]{1,0:T(8,128)(2,1)S(1)}, bf16[128,1152]{1,0:T(8,128)(2,1)S(1)}, u32[]{:S(2)}, u32[]{:S(2)}) collective-permute-start(bf16[128,1152]{1,0:T(8,128)(2,1)S(1)} %collective-permute-done.refs_0_), channel_id=1, source_target_pairs={{0,32},{32,64},{64,96},{96,0},{1,33},{33,65},{65,97},{97,1},{2,34}... | collective-permute-start | bytes 884744 | tf_op jit(solution)/shard_map/ppermute | solution.py:25
  10.4 0.1 pad_add_fusion.ids
  10.5 0.1 pad_maximum_fusion.scal
  10.5 0.7 collective-permute-start.7
  11.2 3.0 %collective-permute-start.6 = (bf16[128,1152]{1,0:T(8,128)(2,1)S(1)}, bf16[128,1152]{1,0:T(8,128)(2,1)S(1)}, u32[]{:S(2)}, u32[]{:S(2)}) collective-permute-start(bf16[128,1152]{1,0:T(8,128)(2,1)S(1)} %collective-permute-done.4.refs_0_), channel_id=1, source_target_pairs={{0,64},{32,96},{64,0},{96,32},{1,65},{33,97},{65,1},{97,33},{2,66}... | collective-permute-start | bytes 884744 | tf_op jit(solution)/shard_map/ppermute | solution.py:25
  14.3 0.9 collective-permute-start.5
  15.2 1.0 %collective-permute-done.2.refs_2_ = bf16[128,1152]{1,0:T(8,128)(2,1)S(1)} collective-permute-done((bf16[128,1152]{1,0:T(8,128)(2,1)S(1)}, bf16[128,1152]{1,0:T(8,128)(2,1)S(1)}, u32[]{:S(2)}, u32[]{:S(2)}) %collective-permute-start.2) | collective-permute-done | bytes 294944 | tf_op jit(solution)/shard_map/ppermute | solution.py:25
  16.2 1.3 %collective-permute-done.1.refs_1_ = bf16[128,1152]{1,0:T(8,128)(2,1)S(1)} collective-permute-done((bf16[128,1152]{1,0:T(8,128)(2,1)S(1)}, bf16[128,1152]{1,0:T(8,128)(2,1)S(1)}, u32[]{:S(2)}, u32[]{:S(2)}) %collective-permute-start.1) | collective-permute-done | bytes 294944 | tf_op jit(solution)/shard_map/ppermute | solution.py:25
  17.4 4.5 %shard_map.101 = (bf16[1152,512]{1,0:T(8,128)(2,1)S(1)}, bf16[512,1152]{1,0:T(8,128)(2,1)S(1)}, f32[512,384]{1,0:T(8,128)S(1)}, f32[512,128]{1,0:T(8,128)S(1)}) custom-call(s32[2]{0:T(128)S(1)} %pad_add_fusion.ids, bf16[128,1152]{1,0:T(8,128)(2,1)S(1)} %collective-permute-done.refs_0_, bf16[128,1152]{1,0:T(8,128)(2,1)S(1)} %collective-permute-done.1.refs_1_, ...), custom_call_target="tpu_custom_call" | custom-call | flops 27179089920 | tf_op jit(solution)/shard_map/pallas_call | solution.py:317
  21.9 11.2 %collective-permute-start.8 = (bf16[512,1152]{1,0:T(8,128)(2,1)S(1)}, bf16[512,1152]{1,0:T(8,128)(2,1)S(1)}, u32[]{:S(2)}, u32[]{:S(2)}) collective-permute-start(bf16[512,1152]{1,0:T(8,128)(2,1)S(1)} %get-tuple-element.38.own), channel_id=1, source_target_pairs={{0,1},{1,0},{2,3},{3,2},{4,5},{5,4},{6,7},{7,6},{8,9},{9,8},{10,11... | collective-permute-start | bytes 3538952 | tf_op jit(solution)/shard_map/ppermute | solution.py:21
  33.2 1.8 %shard_map.102 = (bf16[1152,256]{1,0:T(8,128)(2,1)S(1)}, bf16[256,1152]{1,0:T(8,128)(2,1)S(1)}, f32[256,384]{1,0:T(8,128)S(1)}, f32[256,128]{1,0:T(8,128)S(1)}) custom-call(s32[2]{0:T(128)S(1)} %pad_add_fusion.ids, bf16[128,1152]{1,0:T(8,128)(2,1)S(1)} %collective-permute-done.4.refs_0_, bf16[128,1152]{1,0:T(8,128)(2,1)S(1)} %collective-permute-done.7.refs_1_, ...), custom_call_target="tpu_custom_call" | custom-call | flops 27179089920 | tf_op jit(solution)/shard_map/pallas_call | solution.py:317
  34.9 0.7 collective-permute-done.8.other
  35.6 4.1 %shard_map.103 = (bf16[512,1152]{1,0:T(8,128)(2,1)S(1)}, bf16[1152,256]{1,0:T(8,128)(2,1)S(1)}, f32[256,384]{1,0:T(8,128)S(1)}, f32[256,128]{1,0:T(8,128)S(1)}, ...) custom-call(s32[2]{0:T(128)S(1)} %pad_add_fusion.ids, ...), custom_call_target="tpu_custom_call" | custom-call | flops 27179089920 | tf_op jit(solution)/shard_map/pallas_call | solution.py:317
  39.7 1.3 %collective-permute-start.9 = (f32[512,512]{1,0:T(8,128)S(1)}, f32[512,512]{1,0:T(8,128)S(1)}, u32[]{:S(2)}, u32[]{:S(2)}) collective-permute-start(f32[512,512]{1,0:T(8,128)S(1)} %get-tuple-element.52), channel_id=1, source_target_pairs={{0,1},{1,0},{2,3},{3,2},{4,5},{5,4},{6,7},{7,6},{8,9},{9,8},{10,11... | collective-permute-start | bytes 3145736 | tf_op jit(solution)/shard_map/ppermute | solution.py:21
  41.0 2.5 %shard_map.104 = (f32[1152,384]{1,0:T(8,128)S(1)}, f32[512,384]{1,0:T(8,128)S(1)}, f32[136,1152]{1,0:T(8,128)S(1)}) custom-call(s32[2]{0:T(128)S(1)} %pad_add_fusion.ids, f32[2]{0:T(128)S(1)} %pad_maximum_fusion.scal, bf16[1152,256]{1,0:T(8,128)(2,1)S(1)} %get-tuple-element.40.f0, bf16[1152,256]{1,0:T(8,128)(2,1)S(1)} %get-tuple-element.41.f1, ...), custom_call_target="tpu_custom_call" | custom-call | flops 27179089920 | tf_op jit(solution)/shard_map/pallas_call | solution.py:317
  43.5 0.1 collective-permute-start.11
  43.6 1.4 %shard_map.105 = (bf16[16,192,128]{2,1,0:T(8,128)(2,1)S(1)}, f32[16,192,128]{2,1,0:T(8,128)S(1)}, f32[8,128]{1,0:T(8,128)S(1)}) custom-call(s32[2]{0:T(128)S(1)} %pad_add_fusion.ids, f32[2]{0:T(128)S(1)} %pad_maximum_fusion.scal, bf16[1152,512]{1,0:T(8,128)(2,1)S(1)} %get-tuple-element.34.turned, f32[512,384]{1,0:T(8,128)S(1)} %get-tuple-element.35.window, ...), custom_call_target="tpu_custom_call" | custom-call | tf_op jit(solution)/shard_map/pallas_call | solution.py:317
  45.0 0.6 collective-permute-start.10
  45.5 0.1 collective-permute-done.11.got
  45.6 1.2 %shard_map.106.after = bf16[272,1152]{1,0:T(8,128)(2,1)S(1)} custom-call(f32[2]{0:T(128)S(1)} %pad_maximum_fusion.scal, bf16[512,1024]{1,0:T(8,128)(2,1)S(1)} %get-tuple-element.47.slopes, bf16[1024,512]{1,0:T(8,128)(2,1)S(1)} %get-tuple-element.48.slopes_turned, bf16[512,1152]{1,0:T(8,128)(2,1)S(1)} %get-tuple-element.46.emb, ...), custom_call_target="tpu_custom_call" | custom-call | flops 27179089920 | tf_op jit(solution)/shard_map/pallas_call | solution.py:317
  46.9 0.6 collective-permute-done.10.got
  47.5 1.0 %shard_map.107 = bf16[16,192,128]{2,1,0:T(8,128)(2,1)} custom-call(f32[16,192,128]{2,1,0:T(8,128)S(1)} %get-tuple-element.54.keep, bf16[16,192,128]{2,1,0:T(8,128)(2,1)S(1)} %collective-permute-done.10.got, bf16[272,1152]{1,0:T(8,128)(2,1)S(1)} %shard_map.106.after), custom_call_target="tpu_custom_call" | custom-call | tf_op jit(solution)/shard_map/pallas_call | solution.py:317
  48.5 9.5 %all-to-all-start = ((bf16[16,192,128]{2,1,0:T(8,128)(2,1)}), bf16[16,192,128]{2,1,0:T(8,128)(2,1)S(1)}, u32[]{:S(2)}, u32[]{:S(2)}) async-start(bf16[16,192,128]{2,1,0:T(8,128)(2,1)} %shard_map.107), calls=%async_computation | async-start | bytes 1572864 | tf_op jit(solution)/shard_map/all_to_all | solution.py:384
  58.1 0.7 collective-permute-start.12
  58.8 20.6 %all-to-all-done.parts = bf16[16,192,128]{2,1,0:T(8,128)(2,1)S(1)} async-done(((bf16[16,192,128]{2,1,0:T(8,128)(2,1)}), bf16[16,192,128]{2,1,0:T(8,128)(2,1)S(1)}, u32[]{:S(2)}, u32[]{:S(2)}) %all-to-all-start) | async-done | bytes 786464 | tf_op jit(solution)/shard_map/all_to_all | solution.py:384
  79.4 0.1 shard_map.108
  79.5 14.1 %all_to_all.10.spread = bf16[8,192,128]{2,1,0:T(8,128)(2,1)S(1)} all-to-all(bf16[8,192,128]{2,1,0:T(8,128)(2,1)S(1)} %shard_map.108), channel_id=1, replica_groups=mesh['xh'=2,'y'=4,'xl'=2,'z'=8,'c'=2] {'xh','y'}, dimensions={0} | all-to-all | bytes 786432 | tf_op jit(solution)/shard_map/all_to_all | solution.py:386
  93.6 1.6 %shard_map.109 = (f32[36,1152]{1,0:T(8,128)}, f32[36,1152]{1,0:T(8,128)}, f32[1]{0:T(128)}, bf16[1,128,1152]{2,1,0:T(8,128)(2,1)}, bf16[1,128,1152]{2,1,0:T(8,128)(2,1)}) custom-call(s32[2]{0:T(128)S(1)} %pad_add_fusion.ids, bf16[8,192,128]{2,1,0:T(8,128)(2,1)S(1)} %all_to_all.10.spread, bf16[272,1152]{1,0:T(8,128)(2,1)S(1)} %collective-permute-done.12.after.outs), custom_call_target="tpu_custom_call" | custom-call | tf_op jit(solution)/shard_map/pallas_call | solution.py:317
  (10 shorter events, 0.0 us)
Async XLA Ops:
  0.6 3.2 %collective-permute-start = (bf16[128,1152]{1,0:T(8,128)(2,1)}, bf16[128,1152]{1,0:T(8,128)(2,1)S(1)}, u32[]{:S(2)}, u32[]{:S(2)}) collective-permute-start(bf16[128,1152]{1,0:T(8,128)(2,1)} %bitcast.4), channel_id=1, source_target_pairs={{0,0},{1,128},{128,1},{129,129},{2,2},{3,130},{130,3},{131,131},{4... | collective-permute-start | bytes 884744 | tf_op jit(solution)/shard_map/ppermute | solution.py:17
  2.3 8.3 %collective-permute-start.4 = (bf16[128,1152]{1,0:T(8,128)(2,1)}, bf16[128,1152]{1,0:T(8,128)(2,1)S(1)}, u32[]{:S(2)}, u32[]{:S(2)}) collective-permute-start(bf16[128,1152]{1,0:T(8,128)(2,1)} %bitcast.5), channel_id=1, source_target_pairs={{0,0},{1,128},{128,1},{129,129},{2,2},{3,130},{130,3},{131,131},{4... | collective-permute-start | bytes 884744 | tf_op jit(solution)/shard_map/ppermute | solution.py:17
  3.9 10.4 %collective-permute-start.3 = (bf16[128,1152]{1,0:T(8,128)(2,1)S(1)}, bf16[128,1152]{1,0:T(8,128)(2,1)S(1)}, u32[]{:S(2)}, u32[]{:S(2)}) collective-permute-start(bf16[128,1152]{1,0:T(8,128)(2,1)S(1)} %collective-permute-done.refs_0_), channel_id=1, source_target_pairs={{0,64},{32,96},{64,0},{96,32},{1,65},{33,97},{65,1},{97,33},{2,66}... | collective-permute-start | bytes 884744 | tf_op jit(solution)/shard_map/ppermute | solution.py:25
  7.1 9.1 %collective-permute-start.2 = (bf16[128,1152]{1,0:T(8,128)(2,1)S(1)}, bf16[128,1152]{1,0:T(8,128)(2,1)S(1)}, u32[]{:S(2)}, u32[]{:S(2)}) collective-permute-start(bf16[128,1152]{1,0:T(8,128)(2,1)S(1)} %collective-permute-done.refs_0_), channel_id=1, source_target_pairs={{0,96},{32,0},{64,32},{96,64},{1,97},{33,1},{65,33},{97,65},{2,98}... | collective-permute-start | bytes 884744 | tf_op jit(solution)/shard_map/ppermute | solution.py:25
  8.1 9.3 %collective-permute-start.1 = (bf16[128,1152]{1,0:T(8,128)(2,1)S(1)}, bf16[128,1152]{1,0:T(8,128)(2,1)S(1)}, u32[]{:S(2)}, u32[]{:S(2)}) collective-permute-start(bf16[128,1152]{1,0:T(8,128)(2,1)S(1)} %collective-permute-done.refs_0_), channel_id=1, source_target_pairs={{0,32},{32,64},{64,96},{96,0},{1,33},{33,65},{65,97},{97,1},{2,34}... | collective-permute-start | bytes 884744 | tf_op jit(solution)/shard_map/ppermute | solution.py:25
  10.5 22.6 %copy-start = (bf16[1152,1152]{1,0:T(8,128)(2,1)S(1)}, bf16[1152,1152]{1,0:T(8,128)(2,1)}, u32[]{:S(2)}) copy-start(bf16[1152,1152]{1,0:T(8,128)(2,1)} %weight.1) | copy-start | bytes 7962628
  10.5 22.6 %collective-permute-start.7 = (bf16[128,1152]{1,0:T(8,128)(2,1)S(1)}, bf16[128,1152]{1,0:T(8,128)(2,1)S(1)}, u32[]{:S(2)}, u32[]{:S(2)}) collective-permute-start(bf16[128,1152]{1,0:T(8,128)(2,1)S(1)} %collective-permute-done.4.refs_0_), channel_id=1, source_target_pairs={{0,32},{32,64},{64,96},{96,0},{1,33},{33,65},{65,97},{97,1},{2,34}... | collective-permute-start | bytes 884744 | tf_op jit(solution)/shard_map/ppermute | solution.py:25
  11.2 23.7 %collective-permute-start.6 = (bf16[128,1152]{1,0:T(8,128)(2,1)S(1)}, bf16[128,1152]{1,0:T(8,128)(2,1)S(1)}, u32[]{:S(2)}, u32[]{:S(2)}) collective-permute-start(bf16[128,1152]{1,0:T(8,128)(2,1)S(1)} %collective-permute-done.4.refs_0_), channel_id=1, source_target_pairs={{0,64},{32,96},{64,0},{96,32},{1,65},{33,97},{65,1},{97,33},{2,66}... | collective-permute-start | bytes 884744 | tf_op jit(solution)/shard_map/ppermute | solution.py:25
  14.3 20.6 %collective-permute-start.5 = (bf16[128,1152]{1,0:T(8,128)(2,1)S(1)}, bf16[128,1152]{1,0:T(8,128)(2,1)S(1)}, u32[]{:S(2)}, u32[]{:S(2)}) collective-permute-start(bf16[128,1152]{1,0:T(8,128)(2,1)S(1)} %collective-permute-done.4.refs_0_), channel_id=1, source_target_pairs={{0,96},{32,0},{64,32},{96,64},{1,97},{33,1},{65,33},{97,65},{2,98}... | collective-permute-start | bytes 884744 | tf_op jit(solution)/shard_map/ppermute | solution.py:25
  21.9 13.7 %collective-permute-start.8 = (bf16[512,1152]{1,0:T(8,128)(2,1)S(1)}, bf16[512,1152]{1,0:T(8,128)(2,1)S(1)}, u32[]{:S(2)}, u32[]{:S(2)}) collective-permute-start(bf16[512,1152]{1,0:T(8,128)(2,1)S(1)} %get-tuple-element.38.own), channel_id=1, source_target_pairs={{0,1},{1,0},{2,3},{3,2},{4,5},{5,4},{6,7},{7,6},{8,9},{9,8},{10,11... | collective-permute-start | bytes 3538952 | tf_op jit(solution)/shard_map/ppermute | solution.py:21
  39.7 3.9 %collective-permute-start.9 = (f32[512,512]{1,0:T(8,128)S(1)}, f32[512,512]{1,0:T(8,128)S(1)}, u32[]{:S(2)}, u32[]{:S(2)}) collective-permute-start(f32[512,512]{1,0:T(8,128)S(1)} %get-tuple-element.52), channel_id=1, source_target_pairs={{0,1},{1,0},{2,3},{3,2},{4,5},{5,4},{6,7},{7,6},{8,9},{9,8},{10,11... | collective-permute-start | bytes 3145736 | tf_op jit(solution)/shard_map/ppermute | solution.py:21
  43.5 2.1 %collective-permute-start.11 = (f32[136,1152]{1,0:T(8,128)S(1)}, f32[136,1152]{1,0:T(8,128)S(1)}, u32[]{:S(2)}, u32[]{:S(2)}) collective-permute-start(f32[136,1152]{1,0:T(8,128)S(1)} %get-tuple-element.56), channel_id=1, source_target_pairs={{0,1},{1,0},{2,3},{3,2},{4,5},{5,4},{6,7},{7,6},{8,9},{9,8},{10,11... | collective-permute-start | bytes 1880072 | tf_op jit(solution)/shard_map/ppermute | solution.py:21
  45.0 2.5 %collective-permute-start.10 = (bf16[16,192,128]{2,1,0:T(8,128)(2,1)S(1)}, bf16[16,192,128]{2,1,0:T(8,128)(2,1)S(1)}, u32[]{:S(2)}, u32[]{:S(2)}) collective-permute-start(bf16[16,192,128]{2,1,0:T(8,128)(2,1)S(1)} %get-tuple-element.55), channel_id=1, source_target_pairs={{0,1},{1,0},{2,3},{3,2},{4,5},{5,4},{6,7},{7,6},{8,9},{9,8},{10,11... | collective-permute-start | bytes 2359304 | tf_op jit(solution)/shard_map/ppermute | solution.py:21
  48.5 30.9 %all-to-all-start = ((bf16[16,192,128]{2,1,0:T(8,128)(2,1)}), bf16[16,192,128]{2,1,0:T(8,128)(2,1)S(1)}, u32[]{:S(2)}, u32[]{:S(2)}) async-start(bf16[16,192,128]{2,1,0:T(8,128)(2,1)} %shard_map.107), calls=%async_computation | async-start | bytes 1572864 | tf_op jit(solution)/shard_map/all_to_all | solution.py:384
  58.1 0.7 collective-permute-start.12

commit v5 on v4

--- a/solution.py
+++ b/solution.py
@@ -9,7 +9,7 @@
 LOG2_E = 1.4426950408889634
 AXES = ("xh", "y", "xl", "z", "c")
 XH, Y, XL, Z, C = 2, 4, 2, 8, 2
-WIDE, SLIM, PACK, TERMS = 256, 128, 192, 16
+WIDE, SLIM, PACK, TERMS = 256, 128, 184, 16
 f32, bf16 = jnp.float32, jnp.bfloat16
 
 
@@ -244,13 +244,21 @@
     split = [source[base + 32 : base + 40, col : col + SLIM] for source, col in tiles]
     owned = lax.broadcasted_iota(jnp.int32, (8, SLIM), 0) // 4 == core
     parts += [jnp.where(owned, split[i], pltpu.roll(split[i + 1], 4, 0)) for i in (0, 2)]
-    parts += [split[4], jnp.zeros((8, SLIM), f32)]
+    parts.append(split[4])
     return jnp.concatenate(parts, axis=0)
 
 
-def add_kernel(keep, got, after, mine):
+def add_kernel(keep, got, after, mine, held, sent):
     del after
-    mine[...] = (keep[...] + got[...].astype(f32)).astype(bf16)
+    step = held.shape[0] // sent.shape[0]
+    copies = []
+    for i in range(sent.shape[0]):
+        part = pl.ds(i * step, step)
+        held[part] = (keep[part] + got[part].astype(f32)).astype(bf16)
+        copies.append(pltpu.make_async_copy(held.at[part], mine.at[part], sent.at[i]))
+        copies[-1].start()
+    for copy in copies:
+        copy.wait()
 
 
 def spread_kernel(parts, after, spread):
@@ -307,7 +315,7 @@
     out[2 * n :, :] = terms.astype(bf16)
 
 
-def call(kernel, outs, scratch=(), macs=0, far=None):
+def call(kernel, outs, scratch=(), macs=0, far=None, result=pltpu.VMEM):
     def space(i, x):
         if i == far:
             return pltpu.HBM
@@ -318,7 +326,7 @@
             kernel,
             out_shape=[jax.ShapeDtypeStruct(s, d) for s, d in outs],
             in_specs=[pl.BlockSpec(memory_space=space(i, a)) for i, a in enumerate(args)],
-            out_specs=[pl.BlockSpec(memory_space=pltpu.SMEM if len(s) == 1 else pltpu.VMEM) for s, _ in outs],
+            out_specs=[pl.BlockSpec(memory_space=pltpu.SMEM if len(s) == 1 else result) for s, _ in outs],
             scratch_shapes=list(scratch),
             compiler_params=pltpu.CompilerParams(vmem_limit_bytes=16 * 2**20),
             cost_estimate=pl.CostEstimate(flops=2 * macs, bytes_accessed=0, transcendentals=0),
@@ -379,7 +387,9 @@
     (outs,) = call(out_kernel, [((2 * n + TERMS, width), bf16)], (), macs)(
         scal, slopes, slopes_turned, emb, text_emb, text_other, loss, other_core(rest), token
     )
-    (mine,) = call(add_kernel, [(packed, bf16)])(keep, other_core(give), outs)
+    (mine,) = call(
+        add_kernel, [(packed, bf16)], [pltpu.VMEM(packed, bf16), pltpu.SemaphoreType.DMA((4,))], 0, None, pl.ANY
+    )(keep, other_core(give), outs)
     outs = trade(outs)
     arrived = lax.all_to_all(mine, ("xl", "z"), 0, 0)
     (spread,) = call(spread_kernel, [((XH * Y, PACK, SLIM), bf16)])(arrived, outs)

time: 95.8 us -> 94.9 us (level)
  no operation moved by 1% of the time
where the time goes in v5:
time: 94.9 us; the launch traced here: 94.6 us
  starting transfers between devices  36.6 us (39%)
  waiting for transfers between devices  23.5 us (25%)
  Pallas kernels  18.1 us (19%)
  blocking collectives  14.1 us (15%)
  between operations  2.18 us (2%)
    all_to_all x1, waiting for transfers between devices, on_device(): arrived = lax.all_to_all(mine, ('xl', 'z'), 0, 0)  19.9 us
    pallas_call x9, Pallas kernels, run(): pl.pallas_call(kernel, out_shape=[jax.ShapeDtypeStruct(s, d) for s, d in...  18.1 us
    all_to_all x1, blocking collectives, on_device(): spread = lax.all_to_all(spread, ('xh', 'y'), 0, 0)  14.1 us
    ppermute x4, starting transfers between devices, other_core(): return lax.ppermute(x, 'c', [(0, 1), (1, 0)])  13.2 us
    ppermute x6, starting transfers between devices, from_y(): return lax.ppermute(x, 'y', [(i, (i + k) % Y) for i in range(Y)])  9.89 us
    all_to_all x1, starting transfers between devices, on_device(): arrived = lax.all_to_all(mine, ('xl', 'z'), 0, 0)  9.55 us
    ppermute x3, starting transfers between devices, trade(): return lax.ppermute(x, ('xh', 'c'), [(0, 0), (1, 2), (2, 1), (3, 3)])  3.92 us
    ppermute x6, waiting for transfers between devices, from_y(): return lax.ppermute(x, 'y', [(i, (i + k) % Y) for i in range(Y)])  2.23 us
  transfers between devices with their start and end apart: 14, of which 6 were waited for; matrix products, arithmetic and copies ran while one was open for 0% of the time, Pallas kernels for 12%

profile of v5, /device:TPU:32, one launch (start us, length us, event | category | flops | bytes accessed | tf_op | source)
XLA Modules:
  0.0 94.6 jit_solution(9771491803190961467)
XLA Ops:
  0.6 1.6 %collective-permute-start = (bf16[128,1152]{1,0:T(8,128)(2,1)}, bf16[128,1152]{1,0:T(8,128)(2,1)S(1)}, u32[]{:S(2)}, u32[]{:S(2)}) collective-permute-start(bf16[128,1152]{1,0:T(8,128)(2,1)} %bitcast.4), channel_id=1, source_target_pairs={{0,0},{1,128},{128,1},{129,129},{2,2},{3,130},{130,3},{131,131},{4... | collective-permute-start | bytes 884744 | tf_op jit(solution)/shard_map/ppermute | solution.py:17
  2.3 1.6 %collective-permute-start.4 = (bf16[128,1152]{1,0:T(8,128)(2,1)}, bf16[128,1152]{1,0:T(8,128)(2,1)S(1)}, u32[]{:S(2)}, u32[]{:S(2)}) collective-permute-start(bf16[128,1152]{1,0:T(8,128)(2,1)} %bitcast.5), channel_id=1, source_target_pairs={{0,0},{1,128},{128,1},{129,129},{2,2},{3,130},{130,3},{131,131},{4... | collective-permute-start | bytes 884744 | tf_op jit(solution)/shard_map/ppermute | solution.py:17
  3.9 3.2 %collective-permute-start.3 = (bf16[128,1152]{1,0:T(8,128)(2,1)S(1)}, bf16[128,1152]{1,0:T(8,128)(2,1)S(1)}, u32[]{:S(2)}, u32[]{:S(2)}) collective-permute-start(bf16[128,1152]{1,0:T(8,128)(2,1)S(1)} %collective-permute-done.refs_0_), channel_id=1, source_target_pairs={{0,64},{32,96},{64,0},{96,32},{1,65},{33,97},{65,1},{97,33},{2,66}... | collective-permute-start | bytes 884744 | tf_op jit(solution)/shard_map/ppermute | solution.py:25
  7.1 1.1 %collective-permute-start.2 = (bf16[128,1152]{1,0:T(8,128)(2,1)S(1)}, bf16[128,1152]{1,0:T(8,128)(2,1)S(1)}, u32[]{:S(2)}, u32[]{:S(2)}) collective-permute-start(bf16[128,1152]{1,0:T(8,128)(2,1)S(1)} %collective-permute-done.refs_0_), channel_id=1, source_target_pairs={{0,96},{32,0},{64,32},{96,64},{1,97},{33,1},{65,33},{97,65},{2,98}... | collective-permute-start | bytes 884744 | tf_op jit(solution)/shard_map/ppermute | solution.py:25
  8.1 1.0 %collective-permute-start.1 = (bf16[128,1152]{1,0:T(8,128)(2,1)S(1)}, bf16[128,1152]{1,0:T(8,128)(2,1)S(1)}, u32[]{:S(2)}, u32[]{:S(2)}) collective-permute-start(bf16[128,1152]{1,0:T(8,128)(2,1)S(1)} %collective-permute-done.refs_0_), channel_id=1, source_target_pairs={{0,32},{32,64},{64,96},{96,0},{1,33},{33,65},{65,97},{97,1},{2,34}... | collective-permute-start | bytes 884744 | tf_op jit(solution)/shard_map/ppermute | solution.py:25
  10.4 0.1 pad_add_fusion.ids
  10.5 0.1 pad_maximum_fusion.scal
  10.5 0.7 collective-permute-start.7
  11.2 3.0 %collective-permute-start.6 = (bf16[128,1152]{1,0:T(8,128)(2,1)S(1)}, bf16[128,1152]{1,0:T(8,128)(2,1)S(1)}, u32[]{:S(2)}, u32[]{:S(2)}) collective-permute-start(bf16[128,1152]{1,0:T(8,128)(2,1)S(1)} %collective-permute-done.4.refs_0_), channel_id=1, source_target_pairs={{0,64},{32,96},{64,0},{96,32},{1,65},{33,97},{65,1},{97,33},{2,66}... | collective-permute-start | bytes 884744 | tf_op jit(solution)/shard_map/ppermute | solution.py:25
  14.3 0.9 collective-permute-start.5
  15.2 1.0 %collective-permute-done.2.refs_2_ = bf16[128,1152]{1,0:T(8,128)(2,1)S(1)} collective-permute-done((bf16[128,1152]{1,0:T(8,128)(2,1)S(1)}, bf16[128,1152]{1,0:T(8,128)(2,1)S(1)}, u32[]{:S(2)}, u32[]{:S(2)}) %collective-permute-start.2) | collective-permute-done | bytes 294944 | tf_op jit(solution)/shard_map/ppermute | solution.py:25
  16.2 1.3 %collective-permute-done.1.refs_1_ = bf16[128,1152]{1,0:T(8,128)(2,1)S(1)} collective-permute-done((bf16[128,1152]{1,0:T(8,128)(2,1)S(1)}, bf16[128,1152]{1,0:T(8,128)(2,1)S(1)}, u32[]{:S(2)}, u32[]{:S(2)}) %collective-permute-start.1) | collective-permute-done | bytes 294944 | tf_op jit(solution)/shard_map/ppermute | solution.py:25
  17.4 4.5 %shard_map.101 = (bf16[1152,512]{1,0:T(8,128)(2,1)S(1)}, bf16[512,1152]{1,0:T(8,128)(2,1)S(1)}, f32[512,384]{1,0:T(8,128)S(1)}, f32[512,128]{1,0:T(8,128)S(1)}) custom-call(s32[2]{0:T(128)S(1)} %pad_add_fusion.ids, bf16[128,1152]{1,0:T(8,128)(2,1)S(1)} %collective-permute-done.refs_0_, bf16[128,1152]{1,0:T(8,128)(2,1)S(1)} %collective-permute-done.1.refs_1_, ...), custom_call_target="tpu_custom_call" | custom-call | flops 27179089920 | tf_op jit(solution)/shard_map/pallas_call | solution.py:325
  21.9 11.2 %collective-permute-start.8 = (bf16[512,1152]{1,0:T(8,128)(2,1)S(1)}, bf16[512,1152]{1,0:T(8,128)(2,1)S(1)}, u32[]{:S(2)}, u32[]{:S(2)}) collective-permute-start(bf16[512,1152]{1,0:T(8,128)(2,1)S(1)} %get-tuple-element.38.own), channel_id=1, source_target_pairs={{0,1},{1,0},{2,3},{3,2},{4,5},{5,4},{6,7},{7,6},{8,9},{9,8},{10,11... | collective-permute-start | bytes 3538952 | tf_op jit(solution)/shard_map/ppermute | solution.py:21
  33.2 1.8 %shard_map.102 = (bf16[1152,256]{1,0:T(8,128)(2,1)S(1)}, bf16[256,1152]{1,0:T(8,128)(2,1)S(1)}, f32[256,384]{1,0:T(8,128)S(1)}, f32[256,128]{1,0:T(8,128)S(1)}) custom-call(s32[2]{0:T(128)S(1)} %pad_add_fusion.ids, bf16[128,1152]{1,0:T(8,128)(2,1)S(1)} %collective-permute-done.4.refs_0_, bf16[128,1152]{1,0:T(8,128)(2,1)S(1)} %collective-permute-done.7.refs_1_, ...), custom_call_target="tpu_custom_call" | custom-call | flops 27179089920 | tf_op jit(solution)/shard_map/pallas_call | solution.py:325
  34.9 0.7 collective-permute-done.8.other
  35.6 4.1 %shard_map.103 = (bf16[512,1152]{1,0:T(8,128)(2,1)S(1)}, bf16[1152,256]{1,0:T(8,128)(2,1)S(1)}, f32[256,384]{1,0:T(8,128)S(1)}, f32[256,128]{1,0:T(8,128)S(1)}, ...) custom-call(s32[2]{0:T(128)S(1)} %pad_add_fusion.ids, ...), custom_call_target="tpu_custom_call" | custom-call | flops 27179089920 | tf_op jit(solution)/shard_map/pallas_call | solution.py:325
  39.7 1.3 %collective-permute-start.9 = (f32[512,512]{1,0:T(8,128)S(1)}, f32[512,512]{1,0:T(8,128)S(1)}, u32[]{:S(2)}, u32[]{:S(2)}) collective-permute-start(f32[512,512]{1,0:T(8,128)S(1)} %get-tuple-element.52), channel_id=1, source_target_pairs={{0,1},{1,0},{2,3},{3,2},{4,5},{5,4},{6,7},{7,6},{8,9},{9,8},{10,11... | collective-permute-start | bytes 3145736 | tf_op jit(solution)/shard_map/ppermute | solution.py:21
  41.0 2.5 %shard_map.104 = (f32[1152,384]{1,0:T(8,128)S(1)}, f32[512,384]{1,0:T(8,128)S(1)}, f32[136,1152]{1,0:T(8,128)S(1)}) custom-call(s32[2]{0:T(128)S(1)} %pad_add_fusion.ids, f32[2]{0:T(128)S(1)} %pad_maximum_fusion.scal, bf16[1152,256]{1,0:T(8,128)(2,1)S(1)} %get-tuple-element.40.f0, bf16[1152,256]{1,0:T(8,128)(2,1)S(1)} %get-tuple-element.41.f1, ...), custom_call_target="tpu_custom_call" | custom-call | flops 27179089920 | tf_op jit(solution)/shard_map/pallas_call | solution.py:325
  43.5 0.1 collective-permute-start.11
  43.6 1.4 %shard_map.105 = (bf16[16,184,128]{2,1,0:T(8,128)(2,1)S(1)}, f32[16,184,128]{2,1,0:T(8,128)S(1)}, f32[8,128]{1,0:T(8,128)S(1)}) custom-call(s32[2]{0:T(128)S(1)} %pad_add_fusion.ids, f32[2]{0:T(128)S(1)} %pad_maximum_fusion.scal, bf16[1152,512]{1,0:T(8,128)(2,1)S(1)} %get-tuple-element.34.turned, f32[512,384]{1,0:T(8,128)S(1)} %get-tuple-element.35.window, ...), custom_call_target="tpu_custom_call" | custom-call | tf_op jit(solution)/shard_map/pallas_call | solution.py:325
  45.0 0.6 collective-permute-start.10
  45.6 0.1 collective-permute-done.11.got
  45.6 1.2 %shard_map.106.after = bf16[272,1152]{1,0:T(8,128)(2,1)S(1)} custom-call(f32[2]{0:T(128)S(1)} %pad_maximum_fusion.scal, bf16[512,1024]{1,0:T(8,128)(2,1)S(1)} %get-tuple-element.47.slopes, bf16[1024,512]{1,0:T(8,128)(2,1)S(1)} %get-tuple-element.48.slopes_turned, bf16[512,1152]{1,0:T(8,128)(2,1)S(1)} %get-tuple-element.46.emb, ...), custom_call_target="tpu_custom_call" | custom-call | flops 27179089920 | tf_op jit(solution)/shard_map/pallas_call | solution.py:325
  46.9 0.6 collective-permute-done.10.got
  47.4 1.0 %shard_map.107 = bf16[16,184,128]{2,1,0:T(8,128)(2,1)} custom-call(f32[16,184,128]{2,1,0:T(8,128)S(1)} %get-tuple-element.54.keep, bf16[16,184,128]{2,1,0:T(8,128)(2,1)S(1)} %collective-permute-done.10.got, bf16[272,1152]{1,0:T(8,128)(2,1)S(1)} %shard_map.106.after), custom_call_target="tpu_custom_call" | custom-call | tf_op jit(solution)/shard_map/pallas_call | solution.py:325
  48.4 9.6 %all-to-all-start = ((bf16[16,184,128]{2,1,0:T(8,128)(2,1)}), bf16[16,184,128]{2,1,0:T(8,128)(2,1)S(1)}, u32[]{:S(2)}, u32[]{:S(2)}) async-start(bf16[16,184,128]{2,1,0:T(8,128)(2,1)} %shard_map.107), calls=%async_computation | async-start | bytes 1507328 | tf_op jit(solution)/shard_map/all_to_all | solution.py:394
  57.9 0.7 collective-permute-start.12
  58.7 19.9 %all-to-all-done.parts = bf16[16,184,128]{2,1,0:T(8,128)(2,1)S(1)} async-done(((bf16[16,184,128]{2,1,0:T(8,128)(2,1)}), bf16[16,184,128]{2,1,0:T(8,128)(2,1)S(1)}, u32[]{:S(2)}, u32[]{:S(2)}) %all-to-all-start) | async-done | bytes 753696 | tf_op jit(solution)/shard_map/all_to_all | solution.py:394
  78.6 0.1 shard_map.108
  78.7 14.1 %all_to_all.10.spread = bf16[8,184,128]{2,1,0:T(8,128)(2,1)S(1)} all-to-all(bf16[8,184,128]{2,1,0:T(8,128)(2,1)S(1)} %shard_map.108), channel_id=1, replica_groups=mesh['xh'=2,'y'=4,'xl'=2,'z'=8,'c'=2] {'xh','y'}, dimensions={0} | all-to-all | bytes 753664 | tf_op jit(solution)/shard_map/all_to_all | solution.py:396
  92.7 1.6 %shard_map.109 = (f32[36,1152]{1,0:T(8,128)}, f32[36,1152]{1,0:T(8,128)}, f32[1]{0:T(128)}, bf16[1,128,1152]{2,1,0:T(8,128)(2,1)}, bf16[1,128,1152]{2,1,0:T(8,128)(2,1)}) custom-call(s32[2]{0:T(128)S(1)} %pad_add_fusion.ids, bf16[8,184,128]{2,1,0:T(8,128)(2,1)S(1)} %all_to_all.10.spread, bf16[272,1152]{1,0:T(8,128)(2,1)S(1)} %collective-permute-done.12.after.outs), custom_call_target="tpu_custom_call" | custom-call | tf_op jit(solution)/shard_map/pallas_call | solution.py:325
  (10 shorter events, 0.0 us)
Async XLA Ops:
  0.6 3.2 %collective-permute-start = (bf16[128,1152]{1,0:T(8,128)(2,1)}, bf16[128,1152]{1,0:T(8,128)(2,1)S(1)}, u32[]{:S(2)}, u32[]{:S(2)}) collective-permute-start(bf16[128,1152]{1,0:T(8,128)(2,1)} %bitcast.4), channel_id=1, source_target_pairs={{0,0},{1,128},{128,1},{129,129},{2,2},{3,130},{130,3},{131,131},{4... | collective-permute-start | bytes 884744 | tf_op jit(solution)/shard_map/ppermute | solution.py:17
  2.3 8.3 %collective-permute-start.4 = (bf16[128,1152]{1,0:T(8,128)(2,1)}, bf16[128,1152]{1,0:T(8,128)(2,1)S(1)}, u32[]{:S(2)}, u32[]{:S(2)}) collective-permute-start(bf16[128,1152]{1,0:T(8,128)(2,1)} %bitcast.5), channel_id=1, source_target_pairs={{0,0},{1,128},{128,1},{129,129},{2,2},{3,130},{130,3},{131,131},{4... | collective-permute-start | bytes 884744 | tf_op jit(solution)/shard_map/ppermute | solution.py:17
  3.9 10.4 %collective-permute-start.3 = (bf16[128,1152]{1,0:T(8,128)(2,1)S(1)}, bf16[128,1152]{1,0:T(8,128)(2,1)S(1)}, u32[]{:S(2)}, u32[]{:S(2)}) collective-permute-start(bf16[128,1152]{1,0:T(8,128)(2,1)S(1)} %collective-permute-done.refs_0_), channel_id=1, source_target_pairs={{0,64},{32,96},{64,0},{96,32},{1,65},{33,97},{65,1},{97,33},{2,66}... | collective-permute-start | bytes 884744 | tf_op jit(solution)/shard_map/ppermute | solution.py:25
  7.1 9.1 %collective-permute-start.2 = (bf16[128,1152]{1,0:T(8,128)(2,1)S(1)}, bf16[128,1152]{1,0:T(8,128)(2,1)S(1)}, u32[]{:S(2)}, u32[]{:S(2)}) collective-permute-start(bf16[128,1152]{1,0:T(8,128)(2,1)S(1)} %collective-permute-done.refs_0_), channel_id=1, source_target_pairs={{0,96},{32,0},{64,32},{96,64},{1,97},{33,1},{65,33},{97,65},{2,98}... | collective-permute-start | bytes 884744 | tf_op jit(solution)/shard_map/ppermute | solution.py:25
  8.1 9.3 %collective-permute-start.1 = (bf16[128,1152]{1,0:T(8,128)(2,1)S(1)}, bf16[128,1152]{1,0:T(8,128)(2,1)S(1)}, u32[]{:S(2)}, u32[]{:S(2)}) collective-permute-start(bf16[128,1152]{1,0:T(8,128)(2,1)S(1)} %collective-permute-done.refs_0_), channel_id=1, source_target_pairs={{0,32},{32,64},{64,96},{96,0},{1,33},{33,65},{65,97},{97,1},{2,34}... | collective-permute-start | bytes 884744 | tf_op jit(solution)/shard_map/ppermute | solution.py:25
  10.5 22.6 %copy-start = (bf16[1152,1152]{1,0:T(8,128)(2,1)S(1)}, bf16[1152,1152]{1,0:T(8,128)(2,1)}, u32[]{:S(2)}) copy-start(bf16[1152,1152]{1,0:T(8,128)(2,1)} %weight.1) | copy-start | bytes 7962628
  10.5 22.6 %collective-permute-start.7 = (bf16[128,1152]{1,0:T(8,128)(2,1)S(1)}, bf16[128,1152]{1,0:T(8,128)(2,1)S(1)}, u32[]{:S(2)}, u32[]{:S(2)}) collective-permute-start(bf16[128,1152]{1,0:T(8,128)(2,1)S(1)} %collective-permute-done.4.refs_0_), channel_id=1, source_target_pairs={{0,32},{32,64},{64,96},{96,0},{1,33},{33,65},{65,97},{97,1},{2,34}... | collective-permute-start | bytes 884744 | tf_op jit(solution)/shard_map/ppermute | solution.py:25
  11.2 23.7 %collective-permute-start.6 = (bf16[128,1152]{1,0:T(8,128)(2,1)S(1)}, bf16[128,1152]{1,0:T(8,128)(2,1)S(1)}, u32[]{:S(2)}, u32[]{:S(2)}) collective-permute-start(bf16[128,1152]{1,0:T(8,128)(2,1)S(1)} %collective-permute-done.4.refs_0_), channel_id=1, source_target_pairs={{0,64},{32,96},{64,0},{96,32},{1,65},{33,97},{65,1},{97,33},{2,66}... | collective-permute-start | bytes 884744 | tf_op jit(solution)/shard_map/ppermute | solution.py:25
  14.3 20.6 %collective-permute-start.5 = (bf16[128,1152]{1,0:T(8,128)(2,1)S(1)}, bf16[128,1152]{1,0:T(8,128)(2,1)S(1)}, u32[]{:S(2)}, u32[]{:S(2)}) collective-permute-start(bf16[128,1152]{1,0:T(8,128)(2,1)S(1)} %collective-permute-done.4.refs_0_), channel_id=1, source_target_pairs={{0,96},{32,0},{64,32},{96,64},{1,97},{33,1},{65,33},{97,65},{2,98}... | collective-permute-start | bytes 884744 | tf_op jit(solution)/shard_map/ppermute | solution.py:25
  21.9 13.7 %collective-permute-start.8 = (bf16[512,1152]{1,0:T(8,128)(2,1)S(1)}, bf16[512,1152]{1,0:T(8,128)(2,1)S(1)}, u32[]{:S(2)}, u32[]{:S(2)}) collective-permute-start(bf16[512,1152]{1,0:T(8,128)(2,1)S(1)} %get-tuple-element.38.own), channel_id=1, source_target_pairs={{0,1},{1,0},{2,3},{3,2},{4,5},{5,4},{6,7},{7,6},{8,9},{9,8},{10,11... | collective-permute-start | bytes 3538952 | tf_op jit(solution)/shard_map/ppermute | solution.py:21
  39.7 3.9 %collective-permute-start.9 = (f32[512,512]{1,0:T(8,128)S(1)}, f32[512,512]{1,0:T(8,128)S(1)}, u32[]{:S(2)}, u32[]{:S(2)}) collective-permute-start(f32[512,512]{1,0:T(8,128)S(1)} %get-tuple-element.52), channel_id=1, source_target_pairs={{0,1},{1,0},{2,3},{3,2},{4,5},{5,4},{6,7},{7,6},{8,9},{9,8},{10,11... | collective-permute-start | bytes 3145736 | tf_op jit(solution)/shard_map/ppermute | solution.py:21
  43.5 2.1 %collective-permute-start.11 = (f32[136,1152]{1,0:T(8,128)S(1)}, f32[136,1152]{1,0:T(8,128)S(1)}, u32[]{:S(2)}, u32[]{:S(2)}) collective-permute-start(f32[136,1152]{1,0:T(8,128)S(1)} %get-tuple-element.56), channel_id=1, source_target_pairs={{0,1},{1,0},{2,3},{3,2},{4,5},{5,4},{6,7},{7,6},{8,9},{9,8},{10,11... | collective-permute-start | bytes 1880072 | tf_op jit(solution)/shard_map/ppermute | solution.py:21
  45.0 2.4 %collective-permute-start.10 = (bf16[16,184,128]{2,1,0:T(8,128)(2,1)S(1)}, bf16[16,184,128]{2,1,0:T(8,128)(2,1)S(1)}, u32[]{:S(2)}, u32[]{:S(2)}) collective-permute-start(bf16[16,184,128]{2,1,0:T(8,128)(2,1)S(1)} %get-tuple-element.55), channel_id=1, source_target_pairs={{0,1},{1,0},{2,3},{3,2},{4,5},{5,4},{6,7},{7,6},{8,9},{9,8},{10,11... | collective-permute-start | bytes 2261000 | tf_op jit(solution)/shard_map/ppermute | solution.py:21
  48.4 30.2 %all-to-all-start = ((bf16[16,184,128]{2,1,0:T(8,128)(2,1)}), bf16[16,184,128]{2,1,0:T(8,128)(2,1)S(1)}, u32[]{:S(2)}, u32[]{:S(2)}) async-start(bf16[16,184,128]{2,1,0:T(8,128)(2,1)} %shard_map.107), calls=%async_computation | async-start | bytes 1507328 | tf_op jit(solution)/shard_map/all_to_all | solution.py:394
  57.9 0.7 collective-permute-start.12

commit v6 on v5

--- a/solution.py
+++ b/solution.py
@@ -187,7 +187,6 @@
     n = rest.shape[0] - 8
     rest[:n, :] = dot(slopes_turned[rows : rows + n, :], emb[...])
     rest[n:, :] = jnp.broadcast_to(loss[:, :1], (8, rest.shape[1]))
-    part[:, :WIDE] = dot(slopes_turned[:rows, :], emb[:, pl.ds(text_start(y), WIDE)])
 
     @pl.when(y == 0)
     def _():
@@ -199,10 +198,11 @@
 
     @pl.when(y == Y - 1)
     def _():
-        part[:, WIDE:] = dot(slopes_turned[:rows, :], emb[:, emb.shape[1] - SLIM :])
+        part[...] = dot(slopes_turned[:rows, :], emb[:, emb.shape[1] - WIDE - SLIM :])
 
     @pl.when(y != Y - 1)
     def _():
+        part[:, :WIDE] = dot(slopes_turned[:rows, :], emb[:, pl.ds(text_start(y), WIDE)])
         part[:, WIDE:] = jnp.zeros((rows, SLIM), f32)
 
 
@@ -215,11 +215,14 @@
     grad = scale * (part[...] + got[:, : WIDE + SLIM])
     radial = scale * (text_radial[...] + got[:, WIDE + SLIM :])
     grad = back(grad, window[...], radial, inv[...])
-    term[:, :WIDE] = dot(turned[...], grad[:, :WIDE])
 
     @pl.when(y == Y - 1)
     def _():
-        term[:, WIDE:] = dot(turned[...], grad[:, WIDE:])
+        term[...] = dot(turned[...], grad)
+
+    @pl.when(y != Y - 1)
+    def _():
+        term[:, :WIDE] = dot(turned[...], grad[:, :WIDE])
 
     @pl.when(y == 0)
     def _():

time: 94.9 us -> 95 us (level)
  transfers between devices with their start and end apart: 14 -> 14, of which waited for: 6 -> 5; matrix products, arithmetic and copies ran while one was open for 0% -> 0% of each run, Pallas kernels for 12% -> 13%
where the time goes in v6:
time: 95 us; the launch traced here: 94.6 us
  starting transfers between devices  36.4 us (38%)
  waiting for transfers between devices  23.5 us (25%)
  Pallas kernels  18.7 us (20%)
  blocking collectives  13.8 us (15%)
  between operations  2.18 us (2%)
    all_to_all x1, waiting for transfers between devices, on_device(): arrived = lax.all_to_all(mine, ('xl', 'z'), 0, 0)  19.9 us
    pallas_call x9, Pallas kernels, run(): pl.pallas_call(kernel, out_shape=[jax.ShapeDtypeStruct(s, d) for s, d in...  18.7 us
    all_to_all x1, blocking collectives, on_device(): spread = lax.all_to_all(spread, ('xh', 'y'), 0, 0)  13.8 us
    ppermute x4, starting transfers between devices, other_core(): return lax.ppermute(x, 'c', [(0, 1), (1, 0)])  13 us
    ppermute x6, starting transfers between devices, from_y(): return lax.ppermute(x, 'y', [(i, (i + k) % Y) for i in range(Y)])  9.89 us
    all_to_all x1, starting transfers between devices, on_device(): arrived = lax.all_to_all(mine, ('xl', 'z'), 0, 0)  9.55 us
    ppermute x3, starting transfers between devices, trade(): return lax.ppermute(x, ('xh', 'c'), [(0, 0), (1, 2), (2, 1), (3, 3)])  3.92 us
    ppermute x6, waiting for transfers between devices, from_y(): return lax.ppermute(x, 'y', [(i, (i + k) % Y) for i in range(Y)])  2.23 us
  transfers between devices with their start and end apart: 14, of which 5 were waited for; matrix products, arithmetic and copies ran while one was open for 0% of the time, Pallas kernels for 13%

profile of v6, /device:TPU:32, one launch (start us, length us, event | category | flops | bytes accessed | tf_op | source)
XLA Modules:
  0.0 94.6 jit_solution(16524243407763766010)
XLA Ops:
  0.6 1.6 %collective-permute-start = (bf16[128,1152]{1,0:T(8,128)(2,1)}, bf16[128,1152]{1,0:T(8,128)(2,1)S(1)}, u32[]{:S(2)}, u32[]{:S(2)}) collective-permute-start(bf16[128,1152]{1,0:T(8,128)(2,1)} %bitcast.4), channel_id=1, source_target_pairs={{0,0},{1,128},{128,1},{129,129},{2,2},{3,130},{130,3},{131,131},{4... | collective-permute-start | bytes 884744 | tf_op jit(solution)/shard_map/ppermute | solution.py:17
  2.3 1.6 %collective-permute-start.4 = (bf16[128,1152]{1,0:T(8,128)(2,1)}, bf16[128,1152]{1,0:T(8,128)(2,1)S(1)}, u32[]{:S(2)}, u32[]{:S(2)}) collective-permute-start(bf16[128,1152]{1,0:T(8,128)(2,1)} %bitcast.5), channel_id=1, source_target_pairs={{0,0},{1,128},{128,1},{129,129},{2,2},{3,130},{130,3},{131,131},{4... | collective-permute-start | bytes 884744 | tf_op jit(solution)/shard_map/ppermute | solution.py:17
  3.9 0.0 collective-permute-done.refs_0_
  3.9 3.2 %collective-permute-start.3 = (bf16[128,1152]{1,0:T(8,128)(2,1)S(1)}, bf16[128,1152]{1,0:T(8,128)(2,1)S(1)}, u32[]{:S(2)}, u32[]{:S(2)}) collective-permute-start(bf16[128,1152]{1,0:T(8,128)(2,1)S(1)} %collective-permute-done.refs_0_), channel_id=1, source_target_pairs={{0,64},{32,96},{64,0},{96,32},{1,65},{33,97},{65,1},{97,33},{2,66}... | collective-permute-start | bytes 884744 | tf_op jit(solution)/shard_map/ppermute | solution.py:25
  7.1 1.1 %collective-permute-start.2 = (bf16[128,1152]{1,0:T(8,128)(2,1)S(1)}, bf16[128,1152]{1,0:T(8,128)(2,1)S(1)}, u32[]{:S(2)}, u32[]{:S(2)}) collective-permute-start(bf16[128,1152]{1,0:T(8,128)(2,1)S(1)} %collective-permute-done.refs_0_), channel_id=1, source_target_pairs={{0,96},{32,0},{64,32},{96,64},{1,97},{33,1},{65,33},{97,65},{2,98}... | collective-permute-start | bytes 884744 | tf_op jit(solution)/shard_map/ppermute | solution.py:25
  8.1 1.0 %collective-permute-start.1 = (bf16[128,1152]{1,0:T(8,128)(2,1)S(1)}, bf16[128,1152]{1,0:T(8,128)(2,1)S(1)}, u32[]{:S(2)}, u32[]{:S(2)}) collective-permute-start(bf16[128,1152]{1,0:T(8,128)(2,1)S(1)} %collective-permute-done.refs_0_), channel_id=1, source_target_pairs={{0,32},{32,64},{64,96},{96,0},{1,33},{33,65},{65,97},{97,1},{2,34}... | collective-permute-start | bytes 884744 | tf_op jit(solution)/shard_map/ppermute | solution.py:25
  10.4 0.1 pad_add_fusion.ids
  10.5 0.1 pad_maximum_fusion.scal
  10.5 0.7 collective-permute-start.7
  11.2 3.0 %collective-permute-start.6 = (bf16[128,1152]{1,0:T(8,128)(2,1)S(1)}, bf16[128,1152]{1,0:T(8,128)(2,1)S(1)}, u32[]{:S(2)}, u32[]{:S(2)}) collective-permute-start(bf16[128,1152]{1,0:T(8,128)(2,1)S(1)} %collective-permute-done.4.refs_0_), channel_id=1, source_target_pairs={{0,64},{32,96},{64,0},{96,32},{1,65},{33,97},{65,1},{97,33},{2,66}... | collective-permute-start | bytes 884744 | tf_op jit(solution)/shard_map/ppermute | solution.py:25
  14.3 0.9 collective-permute-start.5
  15.2 1.0 %collective-permute-done.2.refs_2_ = bf16[128,1152]{1,0:T(8,128)(2,1)S(1)} collective-permute-done((bf16[128,1152]{1,0:T(8,128)(2,1)S(1)}, bf16[128,1152]{1,0:T(8,128)(2,1)S(1)}, u32[]{:S(2)}, u32[]{:S(2)}) %collective-permute-start.2) | collective-permute-done | bytes 294944 | tf_op jit(solution)/shard_map/ppermute | solution.py:25
  16.2 1.3 %collective-permute-done.1.refs_1_ = bf16[128,1152]{1,0:T(8,128)(2,1)S(1)} collective-permute-done((bf16[128,1152]{1,0:T(8,128)(2,1)S(1)}, bf16[128,1152]{1,0:T(8,128)(2,1)S(1)}, u32[]{:S(2)}, u32[]{:S(2)}) %collective-permute-start.1) | collective-permute-done | bytes 294944 | tf_op jit(solution)/shard_map/ppermute | solution.py:25
  17.4 4.5 %shard_map.101 = (bf16[1152,512]{1,0:T(8,128)(2,1)S(1)}, bf16[512,1152]{1,0:T(8,128)(2,1)S(1)}, f32[512,384]{1,0:T(8,128)S(1)}, f32[512,128]{1,0:T(8,128)S(1)}) custom-call(s32[2]{0:T(128)S(1)} %pad_add_fusion.ids, bf16[128,1152]{1,0:T(8,128)(2,1)S(1)} %collective-permute-done.refs_0_, bf16[128,1152]{1,0:T(8,128)(2,1)S(1)} %collective-permute-done.1.refs_1_, ...), custom_call_target="tpu_custom_call" | custom-call | flops 27179089920 | tf_op jit(solution)/shard_map/pallas_call | solution.py:328
  21.9 11.2 %collective-permute-start.8 = (bf16[512,1152]{1,0:T(8,128)(2,1)S(1)}, bf16[512,1152]{1,0:T(8,128)(2,1)S(1)}, u32[]{:S(2)}, u32[]{:S(2)}) collective-permute-start(bf16[512,1152]{1,0:T(8,128)(2,1)S(1)} %get-tuple-element.38.own), channel_id=1, source_target_pairs={{0,1},{1,0},{2,3},{3,2},{4,5},{5,4},{6,7},{7,6},{8,9},{9,8},{10,11... | collective-permute-start | bytes 3538952 | tf_op jit(solution)/shard_map/ppermute | solution.py:21
  33.2 1.8 %shard_map.102 = (bf16[1152,256]{1,0:T(8,128)(2,1)S(1)}, bf16[256,1152]{1,0:T(8,128)(2,1)S(1)}, f32[256,384]{1,0:T(8,128)S(1)}, f32[256,128]{1,0:T(8,128)S(1)}) custom-call(s32[2]{0:T(128)S(1)} %pad_add_fusion.ids, bf16[128,1152]{1,0:T(8,128)(2,1)S(1)} %collective-permute-done.4.refs_0_, bf16[128,1152]{1,0:T(8,128)(2,1)S(1)} %collective-permute-done.7.refs_1_, ...), custom_call_target="tpu_custom_call" | custom-call | flops 27179089920 | tf_op jit(solution)/shard_map/pallas_call | solution.py:328
  34.9 0.7 collective-permute-done.8.other
  35.6 4.1 %shard_map.103 = (bf16[512,1152]{1,0:T(8,128)(2,1)S(1)}, bf16[1152,256]{1,0:T(8,128)(2,1)S(1)}, f32[256,384]{1,0:T(8,128)S(1)}, f32[256,128]{1,0:T(8,128)S(1)}, ...) custom-call(s32[2]{0:T(128)S(1)} %pad_add_fusion.ids, ...), custom_call_target="tpu_custom_call" | custom-call | flops 27179089920 | tf_op jit(solution)/shard_map/pallas_call | solution.py:328
  39.7 1.1 %collective-permute-start.9 = (f32[512,512]{1,0:T(8,128)S(1)}, f32[512,512]{1,0:T(8,128)S(1)}, u32[]{:S(2)}, u32[]{:S(2)}) collective-permute-start(f32[512,512]{1,0:T(8,128)S(1)} %get-tuple-element.52), channel_id=1, source_target_pairs={{0,1},{1,0},{2,3},{3,2},{4,5},{5,4},{6,7},{7,6},{8,9},{9,8},{10,11... | collective-permute-start | bytes 3145736 | tf_op jit(solution)/shard_map/ppermute | solution.py:21
  40.8 2.8 %shard_map.104 = (f32[1152,384]{1,0:T(8,128)S(1)}, f32[512,384]{1,0:T(8,128)S(1)}, f32[136,1152]{1,0:T(8,128)S(1)}) custom-call(s32[2]{0:T(128)S(1)} %pad_add_fusion.ids, f32[2]{0:T(128)S(1)} %pad_maximum_fusion.scal, bf16[1152,256]{1,0:T(8,128)(2,1)S(1)} %get-tuple-element.40.f0, bf16[1152,256]{1,0:T(8,128)(2,1)S(1)} %get-tuple-element.41.f1, ...), custom_call_target="tpu_custom_call" | custom-call | flops 27179089920 | tf_op jit(solution)/shard_map/pallas_call | solution.py:328
  43.6 0.1 collective-permute-start.11
  43.8 1.6 %shard_map.105 = (bf16[16,184,128]{2,1,0:T(8,128)(2,1)S(1)}, f32[16,184,128]{2,1,0:T(8,128)S(1)}, f32[8,128]{1,0:T(8,128)S(1)}) custom-call(s32[2]{0:T(128)S(1)} %pad_add_fusion.ids, f32[2]{0:T(128)S(1)} %pad_maximum_fusion.scal, bf16[1152,512]{1,0:T(8,128)(2,1)S(1)} %get-tuple-element.34.turned, f32[512,384]{1,0:T(8,128)S(1)} %get-tuple-element.35.window, ...), custom_call_target="tpu_custom_call" | custom-call | tf_op jit(solution)/shard_map/pallas_call | solution.py:328
  45.3 0.6 collective-permute-start.10
  45.9 1.2 %shard_map.106.after = bf16[272,1152]{1,0:T(8,128)(2,1)S(1)} custom-call(f32[2]{0:T(128)S(1)} %pad_maximum_fusion.scal, bf16[512,1024]{1,0:T(8,128)(2,1)S(1)} %get-tuple-element.47.slopes, bf16[1024,512]{1,0:T(8,128)(2,1)S(1)} %get-tuple-element.48.slopes_turned, bf16[512,1152]{1,0:T(8,128)(2,1)S(1)} %get-tuple-element.46.emb, ...), custom_call_target="tpu_custom_call" | custom-call | flops 27179089920 | tf_op jit(solution)/shard_map/pallas_call | solution.py:328
  47.2 0.6 collective-permute-done.10.got
  47.8 1.0 %shard_map.107 = bf16[16,184,128]{2,1,0:T(8,128)(2,1)} custom-call(f32[16,184,128]{2,1,0:T(8,128)S(1)} %get-tuple-element.54.keep, bf16[16,184,128]{2,1,0:T(8,128)(2,1)S(1)} %collective-permute-done.10.got, bf16[272,1152]{1,0:T(8,128)(2,1)S(1)} %shard_map.106.after), custom_call_target="tpu_custom_call" | custom-call | tf_op jit(solution)/shard_map/pallas_call | solution.py:328
  48.8 9.5 %all-to-all-start = ((bf16[16,184,128]{2,1,0:T(8,128)(2,1)}), bf16[16,184,128]{2,1,0:T(8,128)(2,1)S(1)}, u32[]{:S(2)}, u32[]{:S(2)}) async-start(bf16[16,184,128]{2,1,0:T(8,128)(2,1)} %shard_map.107), calls=%async_computation | async-start | bytes 1507328 | tf_op jit(solution)/shard_map/all_to_all | solution.py:397
  58.3 0.7 collective-permute-start.12
  59.0 19.9 %all-to-all-done.parts = bf16[16,184,128]{2,1,0:T(8,128)(2,1)S(1)} async-done(((bf16[16,184,128]{2,1,0:T(8,128)(2,1)}), bf16[16,184,128]{2,1,0:T(8,128)(2,1)S(1)}, u32[]{:S(2)}, u32[]{:S(2)}) %all-to-all-start) | async-done | bytes 753696 | tf_op jit(solution)/shard_map/all_to_all | solution.py:397
  78.9 0.1 shard_map.108
  79.0 13.8 %all_to_all.10.spread = bf16[8,184,128]{2,1,0:T(8,128)(2,1)S(1)} all-to-all(bf16[8,184,128]{2,1,0:T(8,128)(2,1)S(1)} %shard_map.108), channel_id=1, replica_groups=mesh['xh'=2,'y'=4,'xl'=2,'z'=8,'c'=2] {'xh','y'}, dimensions={0} | all-to-all | bytes 753664 | tf_op jit(solution)/shard_map/all_to_all | solution.py:399
  92.8 1.6 %shard_map.109 = (f32[36,1152]{1,0:T(8,128)}, f32[36,1152]{1,0:T(8,128)}, f32[1]{0:T(128)}, bf16[1,128,1152]{2,1,0:T(8,128)(2,1)}, bf16[1,128,1152]{2,1,0:T(8,128)(2,1)}) custom-call(s32[2]{0:T(128)S(1)} %pad_add_fusion.ids, bf16[8,184,128]{2,1,0:T(8,128)(2,1)S(1)} %all_to_all.10.spread, bf16[272,1152]{1,0:T(8,128)(2,1)S(1)} %collective-permute-done.12.after.outs), custom_call_target="tpu_custom_call" | custom-call | tf_op jit(solution)/shard_map/pallas_call | solution.py:328
  (10 shorter events, 0.0 us)
Async XLA Ops:
  0.6 3.2 %collective-permute-start = (bf16[128,1152]{1,0:T(8,128)(2,1)}, bf16[128,1152]{1,0:T(8,128)(2,1)S(1)}, u32[]{:S(2)}, u32[]{:S(2)}) collective-permute-start(bf16[128,1152]{1,0:T(8,128)(2,1)} %bitcast.4), channel_id=1, source_target_pairs={{0,0},{1,128},{128,1},{129,129},{2,2},{3,130},{130,3},{131,131},{4... | collective-permute-start | bytes 884744 | tf_op jit(solution)/shard_map/ppermute | solution.py:17
  2.3 8.3 %collective-permute-start.4 = (bf16[128,1152]{1,0:T(8,128)(2,1)}, bf16[128,1152]{1,0:T(8,128)(2,1)S(1)}, u32[]{:S(2)}, u32[]{:S(2)}) collective-permute-start(bf16[128,1152]{1,0:T(8,128)(2,1)} %bitcast.5), channel_id=1, source_target_pairs={{0,0},{1,128},{128,1},{129,129},{2,2},{3,130},{130,3},{131,131},{4... | collective-permute-start | bytes 884744 | tf_op jit(solution)/shard_map/ppermute | solution.py:17
  3.9 10.4 %collective-permute-start.3 = (bf16[128,1152]{1,0:T(8,128)(2,1)S(1)}, bf16[128,1152]{1,0:T(8,128)(2,1)S(1)}, u32[]{:S(2)}, u32[]{:S(2)}) collective-permute-start(bf16[128,1152]{1,0:T(8,128)(2,1)S(1)} %collective-permute-done.refs_0_), channel_id=1, source_target_pairs={{0,64},{32,96},{64,0},{96,32},{1,65},{33,97},{65,1},{97,33},{2,66}... | collective-permute-start | bytes 884744 | tf_op jit(solution)/shard_map/ppermute | solution.py:25
  7.1 9.1 %collective-permute-start.2 = (bf16[128,1152]{1,0:T(8,128)(2,1)S(1)}, bf16[128,1152]{1,0:T(8,128)(2,1)S(1)}, u32[]{:S(2)}, u32[]{:S(2)}) collective-permute-start(bf16[128,1152]{1,0:T(8,128)(2,1)S(1)} %collective-permute-done.refs_0_), channel_id=1, source_target_pairs={{0,96},{32,0},{64,32},{96,64},{1,97},{33,1},{65,33},{97,65},{2,98}... | collective-permute-start | bytes 884744 | tf_op jit(solution)/shard_map/ppermute | solution.py:25
  8.1 9.3 %collective-permute-start.1 = (bf16[128,1152]{1,0:T(8,128)(2,1)S(1)}, bf16[128,1152]{1,0:T(8,128)(2,1)S(1)}, u32[]{:S(2)}, u32[]{:S(2)}) collective-permute-start(bf16[128,1152]{1,0:T(8,128)(2,1)S(1)} %collective-permute-done.refs_0_), channel_id=1, source_target_pairs={{0,32},{32,64},{64,96},{96,0},{1,33},{33,65},{65,97},{97,1},{2,34}... | collective-permute-start | bytes 884744 | tf_op jit(solution)/shard_map/ppermute | solution.py:25
  10.5 22.6 %copy-start = (bf16[1152,1152]{1,0:T(8,128)(2,1)S(1)}, bf16[1152,1152]{1,0:T(8,128)(2,1)}, u32[]{:S(2)}) copy-start(bf16[1152,1152]{1,0:T(8,128)(2,1)} %weight.1) | copy-start | bytes 7962628
  10.5 22.6 %collective-permute-start.7 = (bf16[128,1152]{1,0:T(8,128)(2,1)S(1)}, bf16[128,1152]{1,0:T(8,128)(2,1)S(1)}, u32[]{:S(2)}, u32[]{:S(2)}) collective-permute-start(bf16[128,1152]{1,0:T(8,128)(2,1)S(1)} %collective-permute-done.4.refs_0_), channel_id=1, source_target_pairs={{0,32},{32,64},{64,96},{96,0},{1,33},{33,65},{65,97},{97,1},{2,34}... | collective-permute-start | bytes 884744 | tf_op jit(solution)/shard_map/ppermute | solution.py:25
  11.2 23.7 %collective-permute-start.6 = (bf16[128,1152]{1,0:T(8,128)(2,1)S(1)}, bf16[128,1152]{1,0:T(8,128)(2,1)S(1)}, u32[]{:S(2)}, u32[]{:S(2)}) collective-permute-start(bf16[128,1152]{1,0:T(8,128)(2,1)S(1)} %collective-permute-done.4.refs_0_), channel_id=1, source_target_pairs={{0,64},{32,96},{64,0},{96,32},{1,65},{33,97},{65,1},{97,33},{2,66}... | collective-permute-start | bytes 884744 | tf_op jit(solution)/shard_map/ppermute | solution.py:25
  14.3 20.6 %collective-permute-start.5 = (bf16[128,1152]{1,0:T(8,128)(2,1)S(1)}, bf16[128,1152]{1,0:T(8,128)(2,1)S(1)}, u32[]{:S(2)}, u32[]{:S(2)}) collective-permute-start(bf16[128,1152]{1,0:T(8,128)(2,1)S(1)} %collective-permute-done.4.refs_0_), channel_id=1, source_target_pairs={{0,96},{32,0},{64,32},{96,64},{1,97},{33,1},{65,33},{97,65},{2,98}... | collective-permute-start | bytes 884744 | tf_op jit(solution)/shard_map/ppermute | solution.py:25
  21.9 13.7 %collective-permute-start.8 = (bf16[512,1152]{1,0:T(8,128)(2,1)S(1)}, bf16[512,1152]{1,0:T(8,128)(2,1)S(1)}, u32[]{:S(2)}, u32[]{:S(2)}) collective-permute-start(bf16[512,1152]{1,0:T(8,128)(2,1)S(1)} %get-tuple-element.38.own), channel_id=1, source_target_pairs={{0,1},{1,0},{2,3},{3,2},{4,5},{5,4},{6,7},{7,6},{8,9},{9,8},{10,11... | collective-permute-start | bytes 3538952 | tf_op jit(solution)/shard_map/ppermute | solution.py:21
  39.7 4.0 %collective-permute-start.9 = (f32[512,512]{1,0:T(8,128)S(1)}, f32[512,512]{1,0:T(8,128)S(1)}, u32[]{:S(2)}, u32[]{:S(2)}) collective-permute-start(f32[512,512]{1,0:T(8,128)S(1)} %get-tuple-element.52), channel_id=1, source_target_pairs={{0,1},{1,0},{2,3},{3,2},{4,5},{5,4},{6,7},{7,6},{8,9},{9,8},{10,11... | collective-permute-start | bytes 3145736 | tf_op jit(solution)/shard_map/ppermute | solution.py:21
  43.6 2.3 %collective-permute-start.11 = (f32[136,1152]{1,0:T(8,128)S(1)}, f32[136,1152]{1,0:T(8,128)S(1)}, u32[]{:S(2)}, u32[]{:S(2)}) collective-permute-start(f32[136,1152]{1,0:T(8,128)S(1)} %get-tuple-element.56), channel_id=1, source_target_pairs={{0,1},{1,0},{2,3},{3,2},{4,5},{5,4},{6,7},{7,6},{8,9},{9,8},{10,11... | collective-permute-start | bytes 1880072 | tf_op jit(solution)/shard_map/ppermute | solution.py:21
  45.3 2.4 %collective-permute-start.10 = (bf16[16,184,128]{2,1,0:T(8,128)(2,1)S(1)}, bf16[16,184,128]{2,1,0:T(8,128)(2,1)S(1)}, u32[]{:S(2)}, u32[]{:S(2)}) collective-permute-start(bf16[16,184,128]{2,1,0:T(8,128)(2,1)S(1)} %get-tuple-element.55), channel_id=1, source_target_pairs={{0,1},{1,0},{2,3},{3,2},{4,5},{5,4},{6,7},{7,6},{8,9},{9,8},{10,11... | collective-permute-start | bytes 2261000 | tf_op jit(solution)/shard_map/ppermute | solution.py:21
  48.8 30.2 %all-to-all-start = ((bf16[16,184,128]{2,1,0:T(8,128)(2,1)}), bf16[16,184,128]{2,1,0:T(8,128)(2,1)S(1)}, u32[]{:S(2)}, u32[]{:S(2)}) async-start(bf16[16,184,128]{2,1,0:T(8,128)(2,1)} %shard_map.107), calls=%async_computation | async-start | bytes 1507328 | tf_op jit(solution)/shard_map/all_to_all | solution.py:397
  58.3 0.7 collective-permute-start.12
